TPU v7x, 32 devices: a whole 2x2x4 slice. The times are simulated.
32 devices in a mesh: rep: 16 (over z, y, x), sp: 2 (over core).
Axes of the slice: x: 2, y: 2, z: 4, core: 2. Of those that a mesh axis runs over, the one named last changes fastest.
Arguments:
- level_four: bfloat16 [16, 96, 96, 256], P('rep', 'sp'), may hold values from -25 to 25
- level_six: bfloat16 [16, 24, 24, 256], P('rep', 'sp'), may hold values from -25 to 25
- conv_weight: bfloat16 [9, 256, 256], replicated, may hold values from -0.125 to 0.125
- bn_gain: float32 [2, 256], replicated, may hold values from 0.1 to 1.9
- bn_shift: float32 [2, 256], replicated, may hold values from -3 to 3
- cotan_four: bfloat16 [16, 96, 96, 256], P('rep', 'sp'), may hold values from -6 to 6
- cotan_six: bfloat16 [16, 24, 24, 256], P('rep', 'sp'), may hold values from -6 to 6
Outputs:
- grad_four: bfloat16 [16, 96, 96, 256], P('rep', 'sp')
- grad_six: bfloat16 [16, 24, 24, 256], P('rep', 'sp')
- grad_weight: float32 [9, 256, 256], P(None, 'sp')
- grad_gain: float32 [2, 256], replicated
- grad_shift: float32 [2, 256], replicated
All inputs are finite; a program needn't handle non-finite values.
Results may differ from a plain program's by a relative error of at most 0.0052.
Values may be sent and summed in bfloat16 or wider, within the bound.
No kernel may reach another device: no remote copies, remote signals or barrier semaphores. Data moves between devices by JAX's collectives and lax.ppermute only.
A program may use at most 128 MiB of HBM per device.

v0:
```python
import functools

import jax
import jax.numpy as jnp
from jax import lax
from jax.experimental import pallas as pl
from jax.experimental.pallas import tpu as pltpu
from jax.sharding import PartitionSpec as P

GROUP = 16
RADIX = 4
EPSILON = 1e-05
F32 = jnp.float32
BF16 = jnp.bfloat16
VMEM_LIMIT = 20 * 1024 * 1024
EDGE_LIMIT = 60 * 1024 * 1024


def chunk_of(rows, most):
    return max(size for size in range(1, most + 1) if rows % size == 0)


def pitch_of(cols):
    return -(-cols // 16) * 16


def chunks_of(rows, most):
    size = chunk_of(rows, most)
    return [(start, start + size) for start in range(0, rows, size)]


def widen(cells, pitch):
    cells = cells.astype(F32)
    extra = pitch - cells.shape[0]
    if extra:
        cells = jnp.concatenate([cells, jnp.zeros((extra, cells.shape[1]), F32)], 0)
    return cells


def put_three(three, row, cells, cols, turned):
    pitch, chan = cells.shape
    col = lax.broadcasted_iota(jnp.int32, cells.shape, 0)
    left = jnp.where(col == 0, 0.0, pltpu.roll(cells, 1, 0))
    right = jnp.where(col >= cols - 1, 0.0, pltpu.roll(cells, pitch - 1, 0))
    parts = (right, cells, left) if turned else (left, cells, right)
    for place, part in enumerate(parts):
        three[row, :, place * chan : (place + 1) * chan] = part.astype(BF16)


def beside(three, starts, size):
    pitch, width = three.shape[1:]
    return jnp.concatenate([three[start : start + size].reshape(size * pitch, width) for start in starts], 1)


def edges_valid(sp_count):
    index = lax.axis_index("sp")
    return jnp.where(index > 0, 1.0, 0.0), jnp.where(index < sp_count - 1, 1.0, 0.0)


def level_coefs(moments, gain, shift, count):
    mean = moments[0:1] / count
    spread = moments[1:2] / count - mean * mean
    return mean, lax.rsqrt(spread + EPSILON), gain, shift


def slope_of(conv, cotan, coefs):
    mean, rstd, gain, shift = coefs
    centred = conv.astype(F32) - mean
    half = centred * (0.5 * rstd * gain) + 0.5 * shift
    turn = jnp.tanh(half)
    return centred, cotan.astype(F32) * ((1.0 + turn) * (1.0 + half * (1.0 - turn)))


def masked(cells, cols):
    if cells.shape[0] == cols:
        return cells
    col = lax.broadcasted_iota(jnp.int32, cells.shape, 0)
    return jnp.where(col < cols, cells, 0.0)


def staged(fills, dots):
    fills[0]()
    for index, dot in enumerate(dots):
        if index + 1 < len(fills):
            fills[index + 1]()
        dot()


def forward_level(x_ref, top, bottom, valid, w_ref, conv_ref, three, sums, most):
    rows, cols, chan = x_ref.shape
    pitch = three.shape[1]

    def fill_row(row):
        if row < 2:
            cells = top(row) * valid[0]
        elif row < rows + 2:
            cells = widen(x_ref[row - 2], pitch)
        else:
            cells = bottom(row - rows - 2) * valid[1]
        put_three(three, row, cells, cols, False)

    def dot(start, end, index):
        lhs = beside(three, (start, start + 1, start + 2), end - start)
        conv = jnp.dot(lhs, w_ref[...].reshape(9 * chan, chan), preferred_element_type=F32).astype(BF16)
        conv = conv.reshape(end - start, pitch, chan)
        conv_ref[start:end] = conv
        first, last = max(start, 1), min(end, rows + 1)
        conv = conv[first - start : last - start].astype(F32)
        if pitch != cols:
            conv = conv[:, :cols]
        conv = conv.reshape(-1, 8, chan)
        sums[0].append(jnp.sum(conv, 0))
        sums[1].append(jnp.sum(conv * conv, 0))

    chunks = [[start + 1, end + 1] for start, end in chunks_of(rows, most)]
    chunks[0][0] = 0
    chunks[-1][1] = rows + 2
    fills, dots, done = [], [], 0
    for index, (start, end) in enumerate(chunks):
        fills.append(lambda todo=range(done, end + 2): [fill_row(row) for row in todo])
        done = end + 2
        dots.append(functools.partial(dot, start, end, index))
    return fills, dots


def folded(parts):
    total = parts[0]
    for part in parts[1:]:
        total = total + part
    return jnp.sum(total, 0, keepdims=True)


def forward_kernel(
    sp_count, four_ref, six_ref, above_ref, below_ref, w_ref,
    conv_four_ref, conv_six_ref, moments_ref, three_four, three_six,
):
    cols_four = four_ref.shape[1]
    valid = edges_valid(sp_count)
    base, pitch_six = 3 * cols_four, three_six.shape[1]

    def reader(ref, start, pitch):
        return lambda edge: ref[start + edge * pitch : start + (edge + 1) * pitch].astype(F32)

    sums_four, sums_six = ([], []), ([], [])
    fills_six, dots_six = forward_level(
        six_ref, reader(above_ref, base, pitch_six), reader(below_ref, base, pitch_six), valid, w_ref,
        conv_six_ref, three_six, sums_six, 12,
    )
    fills_four, dots_four = forward_level(
        four_ref, reader(above_ref, 0, cols_four), reader(below_ref, 0, cols_four), valid, w_ref,
        conv_four_ref, three_four, sums_four, 8,
    )
    staged(fills_six + fills_four, dots_six + dots_four)
    sums = [folded(parts) for parts in sums_four + sums_six]
    moments_ref[...] = jnp.concatenate(sums, 0)


def slope_level(conv_ref, cotan_ref, above, below, coefs, slope_ref):
    rows, cols, chan = cotan_ref.shape
    pitch = conv_ref.shape[1]

    def put(row, cotan):
        centred, slope = slope_of(conv_ref[row], widen(cotan, pitch), coefs)
        slope_ref[row] = slope
        return centred, slope

    def step(row, sums):
        centred, slope = put(row + 1, cotan_ref[row])
        first = jnp.sum(slope.reshape(-1, 8, chan), 0)
        second = jnp.sum((slope * centred).reshape(-1, 8, chan), 0)
        return sums[0] + first, sums[1] + second

    put(0, above)
    put(rows + 1, below)
    zero = jnp.zeros((8, chan), F32)
    first, second = lax.fori_loop(0, rows, step, (zero, zero), unroll=3)
    first = 0.5 * jnp.sum(first, 0, keepdims=True)
    return first, 0.5 * coefs[1] * jnp.sum(second, 0, keepdims=True)


def slope_kernel(
    counts, conv_four_ref, conv_six_ref, cotan_four_ref, cotan_six_ref, above_ref, below_ref, moments_ref, gain_ref,
    shift_ref, slope_four_ref, slope_six_ref, slopes_ref,
):
    sums = ()
    cols_four = cotan_four_ref.shape[1]
    starts = (2 * cols_four, 3 * cols_four + 2 * conv_six_ref.shape[1])
    for level, (conv_ref, cotan_ref, slope_ref) in enumerate(
        ((conv_four_ref, cotan_four_ref, slope_four_ref), (conv_six_ref, cotan_six_ref, slope_six_ref))
    ):
        pair = moments_ref[2 * level : 2 * level + 2]
        here = slice(level, level + 1)
        edge = slice(starts[level], starts[level] + conv_ref.shape[1])
        coefs = level_coefs(pair, gain_ref[here], shift_ref[here], counts[level])
        sums += slope_level(conv_ref, cotan_ref, above_ref[edge], below_ref[edge], coefs, slope_ref)
    slopes_ref[...] = jnp.concatenate(sums, 0)


def backward_level(x_ref, conv_ref, slope_ref, valid, coefs, slopes, count, three, put, most):
    rows, cols, chan = x_ref.shape
    pitch = three.shape[1]
    mean, rstd, gain, shift = coefs
    lead = gain * rstd
    offset, factor = lead * (slopes[0:1] / count), lead * rstd * (slopes[1:2] / count)

    def fill_row(row):
        centred = conv_ref[row].astype(F32) - mean
        dconv = masked((0.5 * lead) * slope_ref[row] - (offset + centred * factor), cols)
        if row == 0:
            dconv = dconv * valid[0]
        elif row == rows + 1:
            dconv = dconv * valid[1]
        put_three(three, row, dconv, cols, True)

    def dot(start, end):
        size = end - start
        cells = x_ref[start:end]
        if pitch != cols:
            cells = cells.astype(F32)
            cells = jnp.concatenate([cells, jnp.zeros((size, pitch - cols, chan), F32)], 1).astype(BF16)
        lhs = cells.reshape(size * pitch, chan)
        rhs = beside(three, (start + 2, start + 1, start), size)
        put(lax.dot_general(lhs, rhs, (((0,), (0,)), ((), ())), preferred_element_type=F32))

    fills, dots, done = [], [], 0
    for start, end in chunks_of(rows, most):
        fills.append(lambda todo=range(done, end + 2): [fill_row(row) for row in todo])
        done = end + 2
        dots.append(functools.partial(dot, start, end))
    return fills, dots


def backward_kernel(
    counts, sp_count, four_ref, six_ref, conv_four_ref, conv_six_ref, slope_four_ref, slope_six_ref,
    moments_ref, slopes_ref, gain_ref, shift_ref, three_four, three_six, own_ref, sent_ref, total,
):
    valid = edges_valid(sp_count)
    begun = []

    def put(term):
        total[...] = total[...] + term if begun else term
        begun.append(True)

    fills, dots = [], []
    for level, x_ref, conv_ref, slope_ref, three, most in (
        (1, six_ref, conv_six_ref, slope_six_ref, three_six, 12),
        (0, four_ref, conv_four_ref, slope_four_ref, three_four, 8),
    ):
        here = slice(level, level + 1)
        pair = slice(2 * level, 2 * level + 2)
        coefs = level_coefs(moments_ref[pair], gain_ref[here], shift_ref[here], counts[level])
        level_fills, level_dots = backward_level(
            x_ref, conv_ref, slope_ref, valid, coefs, slopes_ref[pair], counts[level], three, put, most
        )
        fills += level_fills
        dots += level_dots
    staged(fills, dots)
    share, chan = own_ref.shape[1:]
    for step in range(sp_count):
        begin = pl.multiple_of((lax.axis_index("sp") ^ step) * share, share)
        for tap in range(9):
            part = total[pl.ds(begin, share), tap * chan : (tap + 1) * chan]
            if step == 0:
                own_ref[tap] = part
            else:
                sent_ref[step - 1, tap] = part.astype(BF16)


def input_level(three, w_ref, grad_ref, most):
    rows, cols, chan = grad_ref.shape
    pitch = three.shape[1]
    rhs = jnp.concatenate([w_ref[tap] for tap in range(9)], 1)
    for start, end in chunks_of(rows, most):
        size = end - start
        lhs = beside(three, (start + 2, start + 1, start), size)
        grad = lax.dot_general(lhs, rhs, (((1,), (1,)), ((), ())), preferred_element_type=F32)
        grad_ref[start:end] = grad.reshape(size, pitch, chan)[:, :cols].astype(BF16)


def input_kernel(three_four, three_six, w_ref, grad_four_ref, grad_six_ref):
    input_level(three_six, w_ref, grad_six_ref, 12)
    input_level(three_four, w_ref, grad_four_ref, 16)


def swap(array, axis, stride):
    count = lax.axis_size(axis)
    return lax.ppermute(array, axis, [(i, i ^ stride) for i in range(count)])


def edge_kernel(starts, four_ref, six_ref, cotan_four_ref, cotan_six_ref, *rest):
    outs, six_rows, sems = rest[:-2], rest[-2], rest[-1]
    rows_four, cols_four = four_ref.shape[:2]
    rows_six = six_ref.shape[0]
    pitch = pitch_of(six_ref.shape[1])
    copies = []
    for number, (start, out_ref) in enumerate(zip(starts, outs)):
        last = (1 - jnp.minimum(lax.axis_index("sp"), 1)) if start is None else start
        for part, (ref, row) in enumerate(
            (
                (four_ref, last * (rows_four - 2)),
                (four_ref, last * (rows_four - 2) + 1),
                (cotan_four_ref, last * (rows_four - 1)),
                (six_ref, last * (rows_six - 2)),
                (six_ref, last * (rows_six - 2) + 1),
                (cotan_six_ref, last * (rows_six - 1)),
            )
        ):
            if part < 3:
                target = out_ref.at[part * cols_four : (part + 1) * cols_four]
            else:
                target = six_rows.at[number, part - 3]
            copies.append(pltpu.make_async_copy(ref.at[row], target, sems.at[number, part]))
    for copy in copies:
        copy.start()
    for copy in copies:
        copy.wait()
    for number, out_ref in enumerate(outs):
        for part in range(3):
            begin = 3 * cols_four + part * pitch
            out_ref[begin : begin + pitch] = widen(six_rows[number, part], pitch).astype(BF16)


def edges(four, six, cotan_four, cotan_six):
    count = lax.axis_size("sp")
    starts = (None,) if count == 2 else (0, 1)
    length = 3 * four.shape[1] + 3 * pitch_of(six.shape[1])
    vmem = pl.BlockSpec(memory_space=pltpu.VMEM)
    hbm = pl.BlockSpec(memory_space=pltpu.HBM)
    outs = pl.pallas_call(
        functools.partial(edge_kernel, starts),
        out_shape=tuple(jax.ShapeDtypeStruct((length, four.shape[2]), BF16) for _ in starts),
        in_specs=[hbm] * 4,
        out_specs=tuple(vmem for _ in starts),
        scratch_shapes=[
            pltpu.VMEM((len(starts), 3) + six.shape[1:], BF16),
            pltpu.SemaphoreType.DMA((len(starts), 6)),
        ],
        compiler_params=pltpu.CompilerParams(vmem_limit_bytes=EDGE_LIMIT),
        name="edges",
    )(four, six, cotan_four, cotan_six)
    if count == 2:
        met = swap(outs[0], "sp", 1)
        return met, met
    above = lax.ppermute(outs[1], "sp", [(i, (i + 1) % count) for i in range(count)])
    below = lax.ppermute(outs[0], "sp", [((i + 1) % count, i) for i in range(count)])
    return above, below


def group_sum(sums):
    stride = 1
    while stride < lax.axis_size("sp"):
        sums = sums + swap(sums, "sp", stride)
        stride = 2 * stride
    stride = 1
    while stride < GROUP:
        met = [swap(sums, "rep", k * stride) for k in range(1, RADIX)]
        sums = (sums + met[0]) + (met[1] + met[2])
        stride = RADIX * stride
    return sums


def every_group(sums):
    stride = GROUP
    while stride < lax.axis_size("rep"):
        sums = sums + swap(sums, "rep", stride)
        stride = 2 * stride
    return sums


def digit_order(parts, digit):
    odd = digit % 2 == 1
    high = digit >= 2
    even = [jnp.where(odd, parts[k ^ 1], parts[k]) for k in range(4)]
    return jnp.stack([jnp.where(high, even[k ^ 2], even[k]) for k in range(4)])


def scatter_start(own, sent):
    met = [swap(sent[step], "sp", step + 1) for step in range(sent.shape[0])]
    chan = own.shape[2]
    parts = [part.reshape(RADIX, -1, chan) for part in [own] + met]
    digit = lax.axis_index("rep") % RADIX

    def piece(k):
        total = lax.dynamic_index_in_dim(parts[0], digit ^ k, 0, False)
        for part in parts[1:]:
            total = total + lax.dynamic_index_in_dim(part, digit ^ k, 0, False).astype(F32)
        return total

    return piece(0), [piece(k).astype(BF16) for k in range(1, RADIX)]


def added(own, met):
    return (own + met[0].astype(F32)) + (met[1].astype(F32) + met[2].astype(F32))


def weight_finish(total):
    chan = total.shape[1]
    digit = lax.axis_index("rep") // RADIX % RADIX
    pieces = total.reshape(RADIX, -1, chan)
    met = [
        swap(lax.dynamic_index_in_dim(pieces, digit ^ k, 0, False).astype(BF16), "rep", k * RADIX)
        for k in range(1, RADIX)
    ]
    total = added(lax.dynamic_index_in_dim(pieces, digit, 0, False), met).astype(BF16)
    stride = GROUP
    while stride < lax.axis_size("rep"):
        met = [swap(total, "rep", k * stride) for k in range(1, RADIX)]
        total = added(total.astype(F32), met).astype(BF16)
        stride = RADIX * stride
    for stride in (RADIX, 1):
        digit = lax.axis_index("rep") // stride % RADIX
        met = [total] + [swap(total, "rep", k * stride) for k in range(1, RADIX)]
        total = digit_order(met, digit).reshape(-1, chan)
    return total.astype(F32)


def local(level_four, level_six, conv_weight, bn_gain, bn_shift, cotan_four, cotan_six):
    sp_count = lax.axis_size("sp")
    images = level_four.shape[0]
    four, six, cot_four, cot_six = (a[0] for a in (level_four, level_six, cotan_four, cotan_six))
    rows_four, cols_four, chan = four.shape
    rows_six, cols_six = six.shape[:2]
    pitch_four, pitch_six = pitch_of(cols_four), pitch_of(cols_six)
    counts = (
        float(images * GROUP * rows_four * sp_count * cols_four),
        float(images * GROUP * rows_six * sp_count * cols_six),
    )
    above, below = edges(four, six, cot_four, cot_six)
    vmem = pl.BlockSpec(memory_space=pltpu.VMEM)
    params = pltpu.CompilerParams(vmem_limit_bytes=VMEM_LIMIT)
    framed_four = jax.ShapeDtypeStruct((rows_four + 2, pitch_four, chan), BF16)
    framed_six = jax.ShapeDtypeStruct((rows_six + 2, pitch_six, chan), BF16)
    four_sums = jax.ShapeDtypeStruct((4, chan), F32)
    flops = 2 * 9 * chan * chan * (rows_four * cols_four + rows_six * cols_six)

    def cost(share, size):
        return pl.CostEstimate(flops=int(flops * share), bytes_accessed=size, transcendentals=0)

    conv_four, conv_six, moments = pl.pallas_call(
        functools.partial(forward_kernel, sp_count),
        out_shape=(framed_four, framed_six, four_sums),
        in_specs=[vmem] * 5,
        out_specs=(vmem, vmem, vmem),
        scratch_shapes=[
            pltpu.VMEM((rows_four + 4, pitch_four, 3 * chan), BF16),
            pltpu.VMEM((rows_six + 4, pitch_six, 3 * chan), BF16),
        ],
        compiler_params=params,
        cost_estimate=cost(1, 4 * four.size),
        name="forward",
    )(four, six, above, below, conv_weight)
    moments = group_sum(moments)

    slope_four, slope_six, slopes = pl.pallas_call(
        functools.partial(slope_kernel, counts),
        out_shape=(
            jax.ShapeDtypeStruct(framed_four.shape, F32),
            jax.ShapeDtypeStruct(framed_six.shape, F32),
            four_sums,
        ),
        in_specs=[vmem] * 9,
        out_specs=(vmem,) * 3,
        compiler_params=params,
        cost_estimate=cost(0.01, 4 * four.size),
        name="slopes",
    )(conv_four, conv_six, cot_four, cot_six, above, below, moments, bn_gain, bn_shift)
    slopes = group_sum(slopes)

    share = chan // sp_count
    wide_four, wide_six = (
        jax.ShapeDtypeStruct(framed.shape[:2] + (3 * chan,), BF16) for framed in (framed_four, framed_six)
    )
    three_four, three_six, own, sent = pl.pallas_call(
        functools.partial(backward_kernel, counts, sp_count),
        out_shape=(
            wide_four,
            wide_six,
            jax.ShapeDtypeStruct((9, share, chan), F32),
            jax.ShapeDtypeStruct((sp_count - 1, 9, share, chan), BF16),
        ),
        in_specs=[vmem] * 10,
        out_specs=(vmem,) * 4,
        scratch_shapes=[pltpu.VMEM((chan, 9 * chan), F32)],
        compiler_params=params,
        cost_estimate=cost(1.2, 8 * four.size),
        name="backward",
    )(four, six, conv_four, conv_six, slope_four, slope_six, moments, slopes, bn_gain, bn_shift)

    piece, pieces = scatter_start(own, sent)
    pieces, three_four = lax.optimization_barrier((pieces, three_four))
    met = [swap(pieces[k - 1], "rep", k) for k in range(1, RADIX)]
    grad_four, grad_six = pl.pallas_call(
        input_kernel,
        out_shape=(
            jax.ShapeDtypeStruct(four.shape, BF16),
            jax.ShapeDtypeStruct(six.shape, BF16),
        ),
        in_specs=[vmem] * 3,
        out_specs=(vmem, vmem),
        compiler_params=params,
        cost_estimate=cost(1, 4 * four.size),
        name="inputs",
    )(three_four, three_six, conv_weight)
    met, grad_six = lax.optimization_barrier((met, grad_six))
    grad_weight = weight_finish(added(piece, met)).reshape(own.shape)
    totals = every_group(slopes)
    grad_gain = jnp.stack([totals[1], totals[3]])
    grad_shift = jnp.stack([totals[0], totals[2]])
    return (grad_four[None], grad_six[None], grad_weight, grad_gain, grad_shift)


def solution(mesh):
    placed = (
        P("rep", "sp", None, None),
        P("rep", "sp", None, None),
        P(),
        P(),
        P(),
        P("rep", "sp", None, None),
        P("rep", "sp", None, None),
    )
    return jax.shard_map(
        local,
        mesh=mesh,
        in_specs=placed,
        out_specs=(
            P("rep", "sp", None, None),
            P("rep", "sp", None, None),
            P(None, "sp", None),
            P(),
            P(),
        ),
        check_vma=False,
    )
```

profile of v0, /device:TPU:0, one launch (start us, length us, event | category | flops | bytes accessed | tf_op | source)
XLA Modules:
  0.0 99.2 jit_solution(8686584100366868514)
XLA Ops:
  0.7 1.7 %edges.1 = bf16[384,256]{1,0:T(8,128)(2,1)} custom-call(bf16[48,96,256]{2,1,0:T(8,128)(2,1)} %bitcast.57, bf16[12,24,256]{2,1,0:T(8,128)(2,1)} %bitcast.64, bf16[48,96,256]{2,1,0:T(8,128)(2,1)} %bitcast.55, bf16[12,24,256]{2,1,0:T(8,128)(2,1)} %bitcast.62), custom_call_target="tpu_custom_call" | custom-call | tf_op jit(solution)/shard_map/edges/pallas_call | solution.py:329
  2.4 0.0 copy-start.2
  2.4 0.0 copy-start.4
  2.5 0.5 collective-permute-start
  3.0 1.3 %collective-permute-done.above_ref.below_ref = bf16[384,256]{1,0:T(8,128)(2,1)S(1)} collective-permute-done((bf16[384,256]{1,0:T(8,128)(2,1)}, bf16[384,256]{1,0:T(8,128)(2,1)S(1)}, u32[]{:S(2)}, u32[]{:S(2)}) %collective-permute-start) | collective-permute-done | bytes 196640 | tf_op jit(solution)/shard_map/ppermute | solution.py:287
  4.3 6.4 %forward.1 = (bf16[50,96,256]{2,1,0:T(8,128)(2,1)S(1)}, bf16[14,32,256]{2,1,0:T(8,128)(2,1)S(1)}, f32[4,256]{1,0:T(4,128)S(1)}) custom-call(bf16[48,96,256]{2,1,0:T(8,128)(2,1)S(1)} %bitcast.58, bf16[12,24,256]{2,1,0:T(8,128)(2,1)S(1)} %bitcast.65, bf16[384,256]{1,0:T(8,128)(2,1)S(1)} %collective-permute-done.above_ref.below_ref, ...), custom_call_target="tpu_custom_call" | custom-call | flops 5775556608 | bytes 4718592 | tf_op jit(solution)/shard_map/forward/pallas_call | solution.py:439
  10.7 0.4 collective-permute-start.1
  11.1 0.8 collective-permute-done.1
  12.0 2.9 %collective-permute-start.3 = (f32[4,256]{1,0:T(4,128)S(1)}, f32[4,256]{1,0:T(4,128)S(1)}, u32[]{:S(2)}, u32[]{:S(2)}) collective-permute-start(f32[4,256]{1,0:T(4,128)S(1)} %add.126), channel_id=1, source_target_pairs={{0,4},{2,6},{4,0},{6,2},{8,12},{10,14},{12,8},{14,10},{16,20},{18,... | collective-permute-start | bytes 12296 | tf_op jit(solution)/shard_map/ppermute | solution.py:287
  14.8 1.4 %collective-permute-start.4 = (f32[4,256]{1,0:T(4,128)S(1)}, f32[4,256]{1,0:T(4,128)S(1)}, u32[]{:S(2)}, u32[]{:S(2)}) collective-permute-start(f32[4,256]{1,0:T(4,128)S(1)} %add.126), channel_id=1, source_target_pairs={{0,6},{2,4},{4,2},{6,0},{8,14},{10,12},{12,10},{14,8},{16,22},{18,... | collective-permute-start | bytes 12296 | tf_op jit(solution)/shard_map/ppermute | solution.py:287
  16.3 0.1 collective-permute-start.2
  16.3 0.1 collective-permute-done.3
  16.4 2.9 %collective-permute-done.4 = f32[4,256]{1,0:T(4,128)S(1)} collective-permute-done((f32[4,256]{1,0:T(4,128)S(1)}, f32[4,256]{1,0:T(4,128)S(1)}, u32[]{:S(2)}, u32[]{:S(2)}) %collective-permute-start.4) | collective-permute-done | bytes 4128 | tf_op jit(solution)/shard_map/ppermute | solution.py:287
  19.3 0.5 collective-permute-done.2
  19.9 2.6 %collective-permute-start.6 = (f32[4,256]{1,0:T(4,128)S(1)}, f32[4,256]{1,0:T(4,128)S(1)}, u32[]{:S(2)}, u32[]{:S(2)}) collective-permute-start(f32[4,256]{1,0:T(4,128)S(1)} %add_add_fusion.3), channel_id=1, source_target_pairs={{0,16},{2,18},{4,20},{6,22},{8,24},{10,26},{12,28},{14,30},{16,0},... | collective-permute-start | bytes 12296 | tf_op jit(solution)/shard_map/ppermute | solution.py:287
  22.5 1.3 %collective-permute-start.7 = (f32[4,256]{1,0:T(4,128)S(1)}, f32[4,256]{1,0:T(4,128)S(1)}, u32[]{:S(2)}, u32[]{:S(2)}) collective-permute-start(f32[4,256]{1,0:T(4,128)S(1)} %add_add_fusion.3), channel_id=1, source_target_pairs={{0,24},{2,26},{4,28},{6,30},{8,16},{10,18},{12,20},{14,22},{16,8},... | collective-permute-start | bytes 12296 | tf_op jit(solution)/shard_map/ppermute | solution.py:287
  23.8 0.2 collective-permute-start.5
  24.1 0.4 collective-permute-done.6
  24.4 3.5 %collective-permute-done.7 = f32[4,256]{1,0:T(4,128)S(1)} collective-permute-done((f32[4,256]{1,0:T(4,128)S(1)}, f32[4,256]{1,0:T(4,128)S(1)}, u32[]{:S(2)}, u32[]{:S(2)}) %collective-permute-start.7) | collective-permute-done | bytes 4128 | tf_op jit(solution)/shard_map/ppermute | solution.py:287
  27.9 3.0 %slopes.1 = (f32[50,96,256]{2,1,0:T(8,128)S(1)}, f32[14,32,256]{2,1,0:T(8,128)S(1)}, f32[4,256]{1,0:T(4,128)S(1)}) custom-call(bf16[50,96,256]{2,1,0:T(8,128)(2,1)S(1)} %get-tuple-element.25.conv_four_ref, bf16[14,32,256]{2,1,0:T(8,128)(2,1)S(1)} %get-tuple-element.26.conv_six_ref, bf16[48,96,256]{2,1,0:T(8,128)(2,1)S(1)} %bitcast.56, ...), custom_call_target="tpu_custom_call" | custom-call | flops 57755568 | bytes 4718592 | tf_op jit(solution)/shard_map/slopes/pallas_call | solution.py:454
  30.9 0.1 collective-permute-start.8
  31.0 1.2 %collective-permute-done.8 = f32[4,256]{1,0:T(4,128)S(1)} collective-permute-done((f32[4,256]{1,0:T(4,128)S(1)}, f32[4,256]{1,0:T(4,128)S(1)}, u32[]{:S(2)}, u32[]{:S(2)}) %collective-permute-start.8) | collective-permute-done | bytes 4128 | tf_op jit(solution)/shard_map/ppermute | solution.py:287
  32.2 1.5 %collective-permute-start.10 = (f32[4,256]{1,0:T(4,128)S(1)}, f32[4,256]{1,0:T(4,128)S(1)}, u32[]{:S(2)}, u32[]{:S(2)}) collective-permute-start(f32[4,256]{1,0:T(4,128)S(1)} %add.133), channel_id=1, source_target_pairs={{0,4},{2,6},{4,0},{6,2},{8,12},{10,14},{12,8},{14,10},{16,20},{18,... | collective-permute-start | bytes 12296 | tf_op jit(solution)/shard_map/ppermute | solution.py:287
  33.7 1.0 collective-permute-start.11
  34.7 1.0 %collective-permute-start.9 = (f32[4,256]{1,0:T(4,128)S(1)}, f32[4,256]{1,0:T(4,128)S(1)}, u32[]{:S(2)}, u32[]{:S(2)}) collective-permute-start(f32[4,256]{1,0:T(4,128)S(1)} %add.133), channel_id=1, source_target_pairs={{0,2},{2,0},{4,6},{6,4},{8,10},{10,8},{12,14},{14,12},{16,18},{18,... | collective-permute-start | bytes 12296 | tf_op jit(solution)/shard_map/ppermute | solution.py:287
  35.7 0.1 collective-permute-done.10
  35.8 2.4 %collective-permute-done.11 = f32[4,256]{1,0:T(4,128)S(1)} collective-permute-done((f32[4,256]{1,0:T(4,128)S(1)}, f32[4,256]{1,0:T(4,128)S(1)}, u32[]{:S(2)}, u32[]{:S(2)}) %collective-permute-start.11) | collective-permute-done | bytes 4128 | tf_op jit(solution)/shard_map/ppermute | solution.py:287
  38.2 0.1 collective-permute-done.9
  38.3 1.2 %collective-permute-start.13 = (f32[4,256]{1,0:T(4,128)S(1)}, f32[4,256]{1,0:T(4,128)S(1)}, u32[]{:S(2)}, u32[]{:S(2)}) collective-permute-start(f32[4,256]{1,0:T(4,128)S(1)} %add_add_fusion.1), channel_id=1, source_target_pairs={{0,16},{2,18},{4,20},{6,22},{8,24},{10,26},{12,28},{14,30},{16,0},... | collective-permute-start | bytes 12296 | tf_op jit(solution)/shard_map/ppermute | solution.py:287
  39.5 0.9 collective-permute-start.14
  40.4 1.3 %collective-permute-start.12 = (f32[4,256]{1,0:T(4,128)S(1)}, f32[4,256]{1,0:T(4,128)S(1)}, u32[]{:S(2)}, u32[]{:S(2)}) collective-permute-start(f32[4,256]{1,0:T(4,128)S(1)} %add_add_fusion.1), channel_id=1, source_target_pairs={{0,8},{2,10},{4,12},{6,14},{8,0},{10,2},{12,4},{14,6},{16,24},{18,... | collective-permute-start | bytes 12296 | tf_op jit(solution)/shard_map/ppermute | solution.py:287
  41.8 1.0 %collective-permute-done.13 = f32[4,256]{1,0:T(4,128)S(1)} collective-permute-done((f32[4,256]{1,0:T(4,128)S(1)}, f32[4,256]{1,0:T(4,128)S(1)}, u32[]{:S(2)}, u32[]{:S(2)}) %collective-permute-start.13) | collective-permute-done | bytes 4128 | tf_op jit(solution)/shard_map/ppermute | solution.py:287
  42.8 2.1 %collective-permute-done.14 = f32[4,256]{1,0:T(4,128)S(1)} collective-permute-done((f32[4,256]{1,0:T(4,128)S(1)}, f32[4,256]{1,0:T(4,128)S(1)}, u32[]{:S(2)}, u32[]{:S(2)}) %collective-permute-start.14) | collective-permute-done | bytes 4128 | tf_op jit(solution)/shard_map/ppermute | solution.py:287
  44.9 8.1 %backward.1 = (bf16[50,96,768]{2,1,0:T(8,128)(2,1)S(1)}, bf16[14,32,768]{2,1,0:T(8,128)(2,1)S(1)}, f32[9,128,256]{2,1,0:T(8,128)S(1)}, bf16[1,9,128,256]{3,2,1,0:T(8,128)(2,1)}) custom-call(bf16[48,96,256]{2,1,0:T(8,128)(2,1)S(1)} %bitcast.59, bf16[12,24,256]{2,1,0:T(8,128)(2,1)S(1)} %bitcast.66, bf16[50,96,256]{2,1,0:T(8,128)(2,1)S(1)} %get-tuple-element.25.conv_four_ref, ...), custom_call_target="tpu_custom_call" | custom-call | flops 6930668032 | bytes 9437184 | tf_op jit(solution)/shard_map/backward/pallas_call | solution.py:473
  53.0 2.9 %copy-done.8 = bf16[50,96,768]{2,1,0:T(8,128)(2,1)} copy-done((bf16[50,96,768]{2,1,0:T(8,128)(2,1)}, bf16[50,96,768]{2,1,0:T(8,128)(2,1)S(1)}, u32[]{:S(2)}) %copy-start.8) | copy-done | bytes 7372824
  55.9 0.8 copy-done.10
  56.8 2.2 %collective-permute-done.15 = bf16[9,128,256]{2,1,0:T(8,128)(2,1)S(1)} collective-permute-done((bf16[9,128,256]{2,1,0:T(8,128)(2,1)}, bf16[9,128,256]{2,1,0:T(8,128)(2,1)S(1)}, u32[]{:S(2)}, u32[]{:S(2)}) %collective-permute-start.15) | collective-permute-done | bytes 589856 | tf_op jit(solution)/shard_map/ppermute | solution.py:287
  59.0 0.1 fusion.3
  59.1 1.1 %collective-permute-start.16 = (bf16[288,256]{1,0:T(8,128)(2,1)S(1)}, bf16[288,256]{1,0:T(8,128)(2,1)S(1)}, u32[]{:S(2)}, u32[]{:S(2)}) collective-permute-start(bf16[288,256]{1,0:T(8,128)(2,1)S(1)} %get-tuple-element.37), channel_id=1, source_target_pairs={{0,2},{2,0},{4,6},{6,4},{8,10},{10,8},{12,14},{14,12},{16,18},{18,... | collective-permute-start | bytes 442376 | tf_op jit(solution)/shard_map/ppermute | solution.py:287
  60.2 1.5 %collective-permute-start.17 = (bf16[288,256]{1,0:T(8,128)(2,1)S(1)}, bf16[288,256]{1,0:T(8,128)(2,1)S(1)}, u32[]{:S(2)}, u32[]{:S(2)}) collective-permute-start(bf16[288,256]{1,0:T(8,128)(2,1)S(1)} %get-tuple-element.38), channel_id=1, source_target_pairs={{0,4},{2,6},{4,0},{6,2},{8,12},{10,14},{12,8},{14,10},{16,20},{18,... | collective-permute-start | bytes 442376 | tf_op jit(solution)/shard_map/ppermute | solution.py:287
  61.7 1.0 collective-permute-start.18
  62.6 1.3 %copy-done.7 = bf16[9,256,256]{2,1,0:T(8,128)(2,1)S(1)} copy-done((bf16[9,256,256]{2,1,0:T(8,128)(2,1)S(1)}, bf16[9,256,256]{2,1,0:T(8,128)(2,1)}, u32[]{:S(2)}) %copy-start.7) | copy-done | bytes 1179672
  63.9 3.1 %copy-done.9 = bf16[50,96,768]{2,1,0:T(8,128)(2,1)S(1)} copy-done((bf16[50,96,768]{2,1,0:T(8,128)(2,1)S(1)}, bf16[50,96,768]{2,1,0:T(8,128)(2,1)}, u32[]{:S(2)}) %copy-start.9) | copy-done | bytes 7372824
  67.0 1.1 %copy-done.11 = bf16[14,32,768]{2,1,0:T(8,128)(2,1)S(1)} copy-done((bf16[14,32,768]{2,1,0:T(8,128)(2,1)S(1)}, bf16[14,32,768]{2,1,0:T(8,128)(2,1)}, u32[]{:S(2)}) %copy-start.11) | copy-done | bytes 688152
  68.1 7.6 %inputs.1 = (bf16[48,96,256]{2,1,0:T(8,128)(2,1)}, bf16[12,24,256]{2,1,0:T(8,128)(2,1)}) custom-call(bf16[50,96,768]{2,1,0:T(8,128)(2,1)S(1)} %copy-done.9, bf16[14,32,768]{2,1,0:T(8,128)(2,1)S(1)} %copy-done.11, bf16[9,256,256]{2,1,0:T(8,128)(2,1)S(1)} %copy-done.7), custom_call_target="tpu_custom_call" | custom-call | flops 5775556608 | bytes 4718592 | tf_op jit(solution)/shard_map/inputs/pallas_call | solution.py:492
  75.7 0.1 fusion
  75.8 2.1 %collective-permute-start.21 = (bf16[72,256]{1,0:T(8,128)(2,1)S(1)}, bf16[72,256]{1,0:T(8,128)(2,1)S(1)}, u32[]{:S(2)}, u32[]{:S(2)}) collective-permute-start(bf16[72,256]{1,0:T(8,128)(2,1)S(1)} %get-tuple-element.53), channel_id=1, source_target_pairs={{0,24},{2,26},{4,28},{6,30},{8,16},{10,18},{12,20},{14,22},{16,8},... | collective-permute-start | bytes 110600 | tf_op jit(solution)/shard_map/ppermute | solution.py:287
  77.9 2.4 %collective-permute-start.19 = (bf16[72,256]{1,0:T(8,128)(2,1)S(1)}, bf16[72,256]{1,0:T(8,128)(2,1)S(1)}, u32[]{:S(2)}, u32[]{:S(2)}) collective-permute-start(bf16[72,256]{1,0:T(8,128)(2,1)S(1)} %get-tuple-element.52), channel_id=1, source_target_pairs={{0,8},{2,10},{4,12},{6,14},{8,0},{10,2},{12,4},{14,6},{16,24},{18,... | collective-permute-start | bytes 110600 | tf_op jit(solution)/shard_map/ppermute | solution.py:287
  80.3 1.5 %collective-permute-done.21 = bf16[72,256]{1,0:T(8,128)(2,1)S(1)} collective-permute-done((bf16[72,256]{1,0:T(8,128)(2,1)S(1)}, bf16[72,256]{1,0:T(8,128)(2,1)S(1)}, u32[]{:S(2)}, u32[]{:S(2)}) %collective-permute-start.21) | collective-permute-done | bytes 36896 | tf_op jit(solution)/shard_map/ppermute | solution.py:287
  81.8 1.1 %collective-permute-done.20 = bf16[72,256]{1,0:T(8,128)(2,1)S(1)} collective-permute-done((bf16[72,256]{1,0:T(8,128)(2,1)S(1)}, bf16[72,256]{1,0:T(8,128)(2,1)S(1)}, u32[]{:S(2)}, u32[]{:S(2)}) %collective-permute-start.20) | collective-permute-done | bytes 36896 | tf_op jit(solution)/shard_map/ppermute | solution.py:287
  82.9 2.1 %collective-permute-start.22 = (bf16[72,256]{1,0:T(8,128)(2,1)S(1)}, bf16[72,256]{1,0:T(8,128)(2,1)S(1)}, u32[]{:S(2)}, u32[]{:S(2)}) collective-permute-start(bf16[72,256]{1,0:T(8,128)(2,1)S(1)} %fusion.5), channel_id=1, source_target_pairs={{0,24},{2,26},{4,28},{6,30},{8,16},{10,18},{12,20},{14,22},{16,8},... | collective-permute-start | bytes 110600 | tf_op jit(solution)/shard_map/ppermute | solution.py:287
  84.9 0.9 collective-permute-start.23
  85.8 1.5 %collective-permute-start.24 = (bf16[72,256]{1,0:T(8,128)(2,1)S(1)}, bf16[72,256]{1,0:T(8,128)(2,1)S(1)}, u32[]{:S(2)}, u32[]{:S(2)}) collective-permute-start(bf16[72,256]{1,0:T(8,128)(2,1)S(1)} %fusion.5), channel_id=1, source_target_pairs={{0,8},{2,10},{4,12},{6,14},{8,0},{10,2},{12,4},{14,6},{16,24},{18,... | collective-permute-start | bytes 110600 | tf_op jit(solution)/shard_map/ppermute | solution.py:287
  87.3 1.4 %collective-permute-done.22 = bf16[72,256]{1,0:T(8,128)(2,1)S(1)} collective-permute-done((bf16[72,256]{1,0:T(8,128)(2,1)S(1)}, bf16[72,256]{1,0:T(8,128)(2,1)S(1)}, u32[]{:S(2)}, u32[]{:S(2)}) %collective-permute-start.22) | collective-permute-done | bytes 36896 | tf_op jit(solution)/shard_map/ppermute | solution.py:287
  88.7 1.5 %collective-permute-done.23 = bf16[72,256]{1,0:T(8,128)(2,1)S(1)} collective-permute-done((bf16[72,256]{1,0:T(8,128)(2,1)S(1)}, bf16[72,256]{1,0:T(8,128)(2,1)S(1)}, u32[]{:S(2)}, u32[]{:S(2)}) %collective-permute-start.23) | collective-permute-done | bytes 36896 | tf_op jit(solution)/shard_map/ppermute | solution.py:287
  90.2 2.0 %collective-permute-start.25 = (bf16[288,256]{1,0:T(8,128)(2,1)S(1)}, bf16[288,256]{1,0:T(8,128)(2,1)S(1)}, u32[]{:S(2)}, u32[]{:S(2)}) collective-permute-start(bf16[288,256]{1,0:T(8,128)(2,1)S(1)} %bitcast.72), channel_id=1, source_target_pairs={{0,6},{2,4},{4,2},{6,0},{8,14},{10,12},{12,10},{14,8},{16,22},{18,... | collective-permute-start | bytes 442376 | tf_op jit(solution)/shard_map/ppermute | solution.py:287
  92.2 0.5 collective-permute-start.26
  92.7 1.0 %collective-permute-start.27 = (bf16[288,256]{1,0:T(8,128)(2,1)S(1)}, bf16[288,256]{1,0:T(8,128)(2,1)S(1)}, u32[]{:S(2)}, u32[]{:S(2)}) collective-permute-start(bf16[288,256]{1,0:T(8,128)(2,1)S(1)} %bitcast.74), channel_id=1, source_target_pairs={{0,2},{2,0},{4,6},{6,4},{8,10},{10,8},{12,14},{14,12},{16,18},{18,... | collective-permute-start | bytes 442376 | tf_op jit(solution)/shard_map/ppermute | solution.py:287
  93.8 0.6 pad_maximum_fusion.2
  94.4 2.0 %collective-permute-done.25 = bf16[288,256]{1,0:T(8,128)(2,1)S(1)} collective-permute-done((bf16[288,256]{1,0:T(8,128)(2,1)S(1)}, bf16[288,256]{1,0:T(8,128)(2,1)S(1)}, u32[]{:S(2)}, u32[]{:S(2)}) %collective-permute-start.25) | collective-permute-done | bytes 147488 | tf_op jit(solution)/shard_map/ppermute | solution.py:287
  96.4 1.5 %collective-permute-done.26 = bf16[288,256]{1,0:T(8,128)(2,1)S(1)} collective-permute-done((bf16[288,256]{1,0:T(8,128)(2,1)S(1)}, bf16[288,256]{1,0:T(8,128)(2,1)S(1)}, u32[]{:S(2)}, u32[]{:S(2)}) %collective-permute-start.26) | collective-permute-done | bytes 147488 | tf_op jit(solution)/shard_map/ppermute | solution.py:287
  97.9 0.1 select_bitcast_fusion.3
  98.0 0.1 pad_maximum_fusion
  98.1 1.1 %convert.1 = f32[9,128,256]{2,1,0:T(8,128)} convert(bf16[9,128,256]{2,1,0:T(8,128)(2,1)S(1)} %bitcast.67) | non-fusion elementwise | flops 294912 | bytes 1769472 | tf_op jit(solution)/shard_map/convert_element_type | solution.py:414
  (38 shorter events, 0.2 us)
Async XLA Ops:
  0.6 3.6 %copy-start.1 = (bf16[1,48,96,256]{3,2,1,0:T(8,128)(2,1)S(1)}, bf16[1,48,96,256]{3,2,1,0:T(8,128)(2,1)}, u32[]{:S(2)}) copy-start(bf16[1,48,96,256]{3,2,1,0:T(8,128)(2,1)} %param.7) | copy-start | bytes 7077892
  0.6 3.6 %copy-start.3 = (bf16[1,12,24,256]{3,2,1,0:T(8,128)(2,1)S(1)}, bf16[1,12,24,256]{3,2,1,0:T(8,128)(2,1)}, u32[]{:S(2)}) copy-start(bf16[1,12,24,256]{3,2,1,0:T(8,128)(2,1)} %param.8) | copy-start | bytes 442372
  0.7 3.6 %copy-start.6 = (bf16[9,256,256]{2,1,0:T(8,128)(2,1)S(1)}, bf16[9,256,256]{2,1,0:T(8,128)(2,1)}, u32[]{:S(2)}) copy-start(bf16[9,256,256]{2,1,0:T(8,128)(2,1)} %w_ref.3) | copy-start | bytes 3538948
  2.4 25.5 %copy-start = (bf16[1,48,96,256]{3,2,1,0:T(8,128)(2,1)S(1)}, bf16[1,48,96,256]{3,2,1,0:T(8,128)(2,1)}, u32[]{:S(2)}) copy-start(bf16[1,48,96,256]{3,2,1,0:T(8,128)(2,1)} %param.12) | copy-start | bytes 7077892
  2.4 25.5 %copy-start.2 = (bf16[1,12,24,256]{3,2,1,0:T(8,128)(2,1)S(1)}, bf16[1,12,24,256]{3,2,1,0:T(8,128)(2,1)}, u32[]{:S(2)}) copy-start(bf16[1,12,24,256]{3,2,1,0:T(8,128)(2,1)} %param.13) | copy-start | bytes 442372
  2.4 25.5 %copy-start.4 = (f32[2,256]{1,0:T(2,128)S(1)}, f32[2,256]{1,0:T(2,128)}, u32[]{:S(2)}) copy-start(f32[2,256]{1,0:T(2,128)} %gain_ref.3) | copy-start | bytes 6148
  2.4 25.5 %copy-start.5 = (f32[2,256]{1,0:T(2,128)S(1)}, f32[2,256]{1,0:T(2,128)}, u32[]{:S(2)}) copy-start(f32[2,256]{1,0:T(2,128)} %shift_ref.3) | copy-start | bytes 6148
  2.5 1.8 %collective-permute-start = (bf16[384,256]{1,0:T(8,128)(2,1)}, bf16[384,256]{1,0:T(8,128)(2,1)S(1)}, u32[]{:S(2)}, u32[]{:S(2)}) collective-permute-start(bf16[384,256]{1,0:T(8,128)(2,1)} %edges.1), channel_id=1, source_target_pairs={{0,1},{1,0},{2,3},{3,2},{4,5},{5,4},{6,7},{7,6},{8,9},{9,8},{10,11... | collective-permute-start | bytes 589832 | tf_op jit(solution)/shard_map/ppermute | solution.py:287
  10.7 1.3 %collective-permute-start.1 = (f32[4,256]{1,0:T(4,128)S(1)}, f32[4,256]{1,0:T(4,128)S(1)}, u32[]{:S(2)}, u32[]{:S(2)}) collective-permute-start(f32[4,256]{1,0:T(4,128)S(1)} %get-tuple-element.27), channel_id=1, source_target_pairs={{0,1},{1,0},{2,3},{3,2},{4,5},{5,4},{6,7},{7,6},{8,9},{9,8},{10,11... | collective-permute-start | bytes 12296 | tf_op jit(solution)/shard_map/ppermute | solution.py:287
  12.0 4.4 %collective-permute-start.3 = (f32[4,256]{1,0:T(4,128)S(1)}, f32[4,256]{1,0:T(4,128)S(1)}, u32[]{:S(2)}, u32[]{:S(2)}) collective-permute-start(f32[4,256]{1,0:T(4,128)S(1)} %add.126), channel_id=1, source_target_pairs={{0,4},{2,6},{4,0},{6,2},{8,12},{10,14},{12,8},{14,10},{16,20},{18,... | collective-permute-start | bytes 12296 | tf_op jit(solution)/shard_map/ppermute | solution.py:287
  14.8 4.5 %collective-permute-start.4 = (f32[4,256]{1,0:T(4,128)S(1)}, f32[4,256]{1,0:T(4,128)S(1)}, u32[]{:S(2)}, u32[]{:S(2)}) collective-permute-start(f32[4,256]{1,0:T(4,128)S(1)} %add.126), channel_id=1, source_target_pairs={{0,6},{2,4},{4,2},{6,0},{8,14},{10,12},{12,10},{14,8},{16,22},{18,... | collective-permute-start | bytes 12296 | tf_op jit(solution)/shard_map/ppermute | solution.py:287
  16.3 3.6 %collective-permute-start.2 = (f32[4,256]{1,0:T(4,128)S(1)}, f32[4,256]{1,0:T(4,128)S(1)}, u32[]{:S(2)}, u32[]{:S(2)}) collective-permute-start(f32[4,256]{1,0:T(4,128)S(1)} %add.126), channel_id=1, source_target_pairs={{0,2},{2,0},{4,6},{6,4},{8,10},{10,8},{12,14},{14,12},{16,18},{18,... | collective-permute-start | bytes 12296 | tf_op jit(solution)/shard_map/ppermute | solution.py:287
  19.9 4.5 %collective-permute-start.6 = (f32[4,256]{1,0:T(4,128)S(1)}, f32[4,256]{1,0:T(4,128)S(1)}, u32[]{:S(2)}, u32[]{:S(2)}) collective-permute-start(f32[4,256]{1,0:T(4,128)S(1)} %add_add_fusion.3), channel_id=1, source_target_pairs={{0,16},{2,18},{4,20},{6,22},{8,24},{10,26},{12,28},{14,30},{16,0},... | collective-permute-start | bytes 12296 | tf_op jit(solution)/shard_map/ppermute | solution.py:287
  22.5 5.4 %collective-permute-start.7 = (f32[4,256]{1,0:T(4,128)S(1)}, f32[4,256]{1,0:T(4,128)S(1)}, u32[]{:S(2)}, u32[]{:S(2)}) collective-permute-start(f32[4,256]{1,0:T(4,128)S(1)} %add_add_fusion.3), channel_id=1, source_target_pairs={{0,24},{2,26},{4,28},{6,30},{8,16},{10,18},{12,20},{14,22},{16,8},... | collective-permute-start | bytes 12296 | tf_op jit(solution)/shard_map/ppermute | solution.py:287
  23.8 4.1 %collective-permute-start.5 = (f32[4,256]{1,0:T(4,128)S(1)}, f32[4,256]{1,0:T(4,128)S(1)}, u32[]{:S(2)}, u32[]{:S(2)}) collective-permute-start(f32[4,256]{1,0:T(4,128)S(1)} %add_add_fusion.3), channel_id=1, source_target_pairs={{0,8},{2,10},{4,12},{6,14},{8,0},{10,2},{12,4},{14,6},{16,24},{18,... | collective-permute-start | bytes 12296 | tf_op jit(solution)/shard_map/ppermute | solution.py:287
  30.9 1.2 %collective-permute-start.8 = (f32[4,256]{1,0:T(4,128)S(1)}, f32[4,256]{1,0:T(4,128)S(1)}, u32[]{:S(2)}, u32[]{:S(2)}) collective-permute-start(f32[4,256]{1,0:T(4,128)S(1)} %get-tuple-element.30), channel_id=1, source_target_pairs={{0,1},{1,0},{2,3},{3,2},{4,5},{5,4},{6,7},{7,6},{8,9},{9,8},{10,11... | collective-permute-start | bytes 12296 | tf_op jit(solution)/shard_map/ppermute | solution.py:287
  32.2 3.6 %collective-permute-start.10 = (f32[4,256]{1,0:T(4,128)S(1)}, f32[4,256]{1,0:T(4,128)S(1)}, u32[]{:S(2)}, u32[]{:S(2)}) collective-permute-start(f32[4,256]{1,0:T(4,128)S(1)} %add.133), channel_id=1, source_target_pairs={{0,4},{2,6},{4,0},{6,2},{8,12},{10,14},{12,8},{14,10},{16,20},{18,... | collective-permute-start | bytes 12296 | tf_op jit(solution)/shard_map/ppermute | solution.py:287
  33.7 4.5 %collective-permute-start.11 = (f32[4,256]{1,0:T(4,128)S(1)}, f32[4,256]{1,0:T(4,128)S(1)}, u32[]{:S(2)}, u32[]{:S(2)}) collective-permute-start(f32[4,256]{1,0:T(4,128)S(1)} %add.133), channel_id=1, source_target_pairs={{0,6},{2,4},{4,2},{6,0},{8,14},{10,12},{12,10},{14,8},{16,22},{18,... | collective-permute-start | bytes 12296 | tf_op jit(solution)/shard_map/ppermute | solution.py:287
  34.7 3.6 %collective-permute-start.9 = (f32[4,256]{1,0:T(4,128)S(1)}, f32[4,256]{1,0:T(4,128)S(1)}, u32[]{:S(2)}, u32[]{:S(2)}) collective-permute-start(f32[4,256]{1,0:T(4,128)S(1)} %add.133), channel_id=1, source_target_pairs={{0,2},{2,0},{4,6},{6,4},{8,10},{10,8},{12,14},{14,12},{16,18},{18,... | collective-permute-start | bytes 12296 | tf_op jit(solution)/shard_map/ppermute | solution.py:287
  38.3 4.5 %collective-permute-start.13 = (f32[4,256]{1,0:T(4,128)S(1)}, f32[4,256]{1,0:T(4,128)S(1)}, u32[]{:S(2)}, u32[]{:S(2)}) collective-permute-start(f32[4,256]{1,0:T(4,128)S(1)} %add_add_fusion.1), channel_id=1, source_target_pairs={{0,16},{2,18},{4,20},{6,22},{8,24},{10,26},{12,28},{14,30},{16,0},... | collective-permute-start | bytes 12296 | tf_op jit(solution)/shard_map/ppermute | solution.py:287
  39.5 5.4 %collective-permute-start.14 = (f32[4,256]{1,0:T(4,128)S(1)}, f32[4,256]{1,0:T(4,128)S(1)}, u32[]{:S(2)}, u32[]{:S(2)}) collective-permute-start(f32[4,256]{1,0:T(4,128)S(1)} %add_add_fusion.1), channel_id=1, source_target_pairs={{0,24},{2,26},{4,28},{6,30},{8,16},{10,18},{12,20},{14,22},{16,8},... | collective-permute-start | bytes 12296 | tf_op jit(solution)/shard_map/ppermute | solution.py:287
  40.4 4.5 %collective-permute-start.12 = (f32[4,256]{1,0:T(4,128)S(1)}, f32[4,256]{1,0:T(4,128)S(1)}, u32[]{:S(2)}, u32[]{:S(2)}) collective-permute-start(f32[4,256]{1,0:T(4,128)S(1)} %add_add_fusion.1), channel_id=1, source_target_pairs={{0,8},{2,10},{4,12},{6,14},{8,0},{10,2},{12,4},{14,6},{16,24},{18,... | collective-permute-start | bytes 12296 | tf_op jit(solution)/shard_map/ppermute | solution.py:287
  53.0 2.9 %copy-start.8 = (bf16[50,96,768]{2,1,0:T(8,128)(2,1)}, bf16[50,96,768]{2,1,0:T(8,128)(2,1)S(1)}, u32[]{:S(2)}) copy-start(bf16[50,96,768]{2,1,0:T(8,128)(2,1)S(1)} %get-tuple-element.34.three_four) | copy-start | bytes 22118404
  55.9 0.8 copy-start.10
  56.8 2.2 %collective-permute-start.15 = (bf16[9,128,256]{2,1,0:T(8,128)(2,1)}, bf16[9,128,256]{2,1,0:T(8,128)(2,1)S(1)}, u32[]{:S(2)}, u32[]{:S(2)}) collective-permute-start(bf16[9,128,256]{2,1,0:T(8,128)(2,1)} %bitcast.5), channel_id=1, source_target_pairs={{0,1},{1,0},{2,3},{3,2},{4,5},{5,4},{6,7},{7,6},{8,9},{9,8},{10,11... | collective-permute-start | bytes 1769480 | tf_op jit(solution)/shard_map/ppermute | solution.py:287
  59.1 16.6 %collective-permute-start.16 = (bf16[288,256]{1,0:T(8,128)(2,1)S(1)}, bf16[288,256]{1,0:T(8,128)(2,1)S(1)}, u32[]{:S(2)}, u32[]{:S(2)}) collective-permute-start(bf16[288,256]{1,0:T(8,128)(2,1)S(1)} %get-tuple-element.37), channel_id=1, source_target_pairs={{0,2},{2,0},{4,6},{6,4},{8,10},{10,8},{12,14},{14,12},{16,18},{18,... | collective-permute-start | bytes 442376 | tf_op jit(solution)/shard_map/ppermute | solution.py:287
  60.2 15.5 %collective-permute-start.17 = (bf16[288,256]{1,0:T(8,128)(2,1)S(1)}, bf16[288,256]{1,0:T(8,128)(2,1)S(1)}, u32[]{:S(2)}, u32[]{:S(2)}) collective-permute-start(bf16[288,256]{1,0:T(8,128)(2,1)S(1)} %get-tuple-element.38), channel_id=1, source_target_pairs={{0,4},{2,6},{4,0},{6,2},{8,12},{10,14},{12,8},{14,10},{16,20},{18,... | collective-permute-start | bytes 442376 | tf_op jit(solution)/shard_map/ppermute | solution.py:287
  61.7 14.0 %collective-permute-start.18 = (bf16[288,256]{1,0:T(8,128)(2,1)S(1)}, bf16[288,256]{1,0:T(8,128)(2,1)S(1)}, u32[]{:S(2)}, u32[]{:S(2)}) collective-permute-start(bf16[288,256]{1,0:T(8,128)(2,1)S(1)} %get-tuple-element.39), channel_id=1, source_target_pairs={{0,6},{2,4},{4,2},{6,0},{8,14},{10,12},{12,10},{14,8},{16,22},{18,... | collective-permute-start | bytes 442376 | tf_op jit(solution)/shard_map/ppermute | solution.py:287
  62.6 1.3 %copy-start.7 = (bf16[9,256,256]{2,1,0:T(8,128)(2,1)S(1)}, bf16[9,256,256]{2,1,0:T(8,128)(2,1)}, u32[]{:S(2)}) copy-start(bf16[9,256,256]{2,1,0:T(8,128)(2,1)} %w_ref.3) | copy-start | bytes 3538948
  63.9 3.1 %copy-start.9 = (bf16[50,96,768]{2,1,0:T(8,128)(2,1)S(1)}, bf16[50,96,768]{2,1,0:T(8,128)(2,1)}, u32[]{:S(2)}) copy-start(bf16[50,96,768]{2,1,0:T(8,128)(2,1)} %copy-done.8) | copy-start | bytes 22118404
  67.0 1.1 %copy-start.11 = (bf16[14,32,768]{2,1,0:T(8,128)(2,1)S(1)}, bf16[14,32,768]{2,1,0:T(8,128)(2,1)}, u32[]{:S(2)}) copy-start(bf16[14,32,768]{2,1,0:T(8,128)(2,1)} %copy-done.10) | copy-start | bytes 2064388
  75.8 6.0 %collective-permute-start.21 = (bf16[72,256]{1,0:T(8,128)(2,1)S(1)}, bf16[72,256]{1,0:T(8,128)(2,1)S(1)}, u32[]{:S(2)}, u32[]{:S(2)}) collective-permute-start(bf16[72,256]{1,0:T(8,128)(2,1)S(1)} %get-tuple-element.53), channel_id=1, source_target_pairs={{0,24},{2,26},{4,28},{6,30},{8,16},{10,18},{12,20},{14,22},{16,8},... | collective-permute-start | bytes 110600 | tf_op jit(solution)/shard_map/ppermute | solution.py:287
  77.9 4.9 %collective-permute-start.20 = (bf16[72,256]{1,0:T(8,128)(2,1)S(1)}, bf16[72,256]{1,0:T(8,128)(2,1)S(1)}, u32[]{:S(2)}, u32[]{:S(2)}) collective-permute-start(bf16[72,256]{1,0:T(8,128)(2,1)S(1)} %get-tuple-element.54), channel_id=1, source_target_pairs={{0,16},{2,18},{4,20},{6,22},{8,24},{10,26},{12,28},{14,30},{16,0},... | collective-permute-start | bytes 110600 | tf_op jit(solution)/shard_map/ppermute | solution.py:287
  77.9 4.9 %collective-permute-start.19 = (bf16[72,256]{1,0:T(8,128)(2,1)S(1)}, bf16[72,256]{1,0:T(8,128)(2,1)S(1)}, u32[]{:S(2)}, u32[]{:S(2)}) collective-permute-start(bf16[72,256]{1,0:T(8,128)(2,1)S(1)} %get-tuple-element.52), channel_id=1, source_target_pairs={{0,8},{2,10},{4,12},{6,14},{8,0},{10,2},{12,4},{14,6},{16,24},{18,... | collective-permute-start | bytes 110600 | tf_op jit(solution)/shard_map/ppermute | solution.py:287
  82.9 5.8 %collective-permute-start.22 = (bf16[72,256]{1,0:T(8,128)(2,1)S(1)}, bf16[72,256]{1,0:T(8,128)(2,1)S(1)}, u32[]{:S(2)}, u32[]{:S(2)}) collective-permute-start(bf16[72,256]{1,0:T(8,128)(2,1)S(1)} %fusion.5), channel_id=1, source_target_pairs={{0,24},{2,26},{4,28},{6,30},{8,16},{10,18},{12,20},{14,22},{16,8},... | collective-permute-start | bytes 110600 | tf_op jit(solution)/shard_map/ppermute | solution.py:287
  84.9 5.2 %collective-permute-start.23 = (bf16[72,256]{1,0:T(8,128)(2,1)S(1)}, bf16[72,256]{1,0:T(8,128)(2,1)S(1)}, u32[]{:S(2)}, u32[]{:S(2)}) collective-permute-start(bf16[72,256]{1,0:T(8,128)(2,1)S(1)} %fusion.5), channel_id=1, source_target_pairs={{0,16},{2,18},{4,20},{6,22},{8,24},{10,26},{12,28},{14,30},{16,0},... | collective-permute-start | bytes 110600 | tf_op jit(solution)/shard_map/ppermute | solution.py:287
  85.8 4.4 %collective-permute-start.24 = (bf16[72,256]{1,0:T(8,128)(2,1)S(1)}, bf16[72,256]{1,0:T(8,128)(2,1)S(1)}, u32[]{:S(2)}, u32[]{:S(2)}) collective-permute-start(bf16[72,256]{1,0:T(8,128)(2,1)S(1)} %fusion.5), channel_id=1, source_target_pairs={{0,8},{2,10},{4,12},{6,14},{8,0},{10,2},{12,4},{14,6},{16,24},{18,... | collective-permute-start | bytes 110600 | tf_op jit(solution)/shard_map/ppermute | solution.py:287
  90.2 6.2 %collective-permute-start.25 = (bf16[288,256]{1,0:T(8,128)(2,1)S(1)}, bf16[288,256]{1,0:T(8,128)(2,1)S(1)}, u32[]{:S(2)}, u32[]{:S(2)}) collective-permute-start(bf16[288,256]{1,0:T(8,128)(2,1)S(1)} %bitcast.72), channel_id=1, source_target_pairs={{0,6},{2,4},{4,2},{6,0},{8,14},{10,12},{12,10},{14,8},{16,22},{18,... | collective-permute-start | bytes 442376 | tf_op jit(solution)/shard_map/ppermute | solution.py:287
  92.2 5.7 %collective-permute-start.26 = (bf16[288,256]{1,0:T(8,128)(2,1)S(1)}, bf16[288,256]{1,0:T(8,128)(2,1)S(1)}, u32[]{:S(2)}, u32[]{:S(2)}) collective-permute-start(bf16[288,256]{1,0:T(8,128)(2,1)S(1)} %bitcast.73), channel_id=1, source_target_pairs={{0,4},{2,6},{4,0},{6,2},{8,12},{10,14},{12,8},{14,10},{16,20},{18,... | collective-permute-start | bytes 442376 | tf_op jit(solution)/shard_map/ppermute | solution.py:287
  92.7 5.2 %collective-permute-start.27 = (bf16[288,256]{1,0:T(8,128)(2,1)S(1)}, bf16[288,256]{1,0:T(8,128)(2,1)S(1)}, u32[]{:S(2)}, u32[]{:S(2)}) collective-permute-start(bf16[288,256]{1,0:T(8,128)(2,1)S(1)} %bitcast.74), channel_id=1, source_target_pairs={{0,2},{2,0},{4,6},{6,4},{8,10},{10,8},{12,14},{14,12},{16,18},{18,... | collective-permute-start | bytes 442376 | tf_op jit(solution)/shard_map/ppermute | solution.py:287
where the time goes:
time: 99.4 us; the launch traced here: 99.2 us
  starting transfers between devices  32.5 us (33%)
  waiting for transfers between devices  27.5 us (28%)
  Pallas kernels  26.9 us (27%)
  local copies, waits for them, and re-layouts  9.28 us (9%)
  other arithmetic  2.13 us (2%)
    ppermute x28, starting transfers between devices, swap(): return lax.ppermute(array, axis, [(i, i ^ stride) for i in range(count)])  32.5 us
    ppermute x28, waiting for transfers between devices, swap(): return lax.ppermute(array, axis, [(i, i ^ stride) for i in range(count)])  27.5 us
    unnamed x24, local copies, waits for them, and re-layouts  9.25 us
    pallas_call x1, Pallas kernels, local(): pl.pallas_call(functools.partial(backward_kernel, counts, sp_count), out_...  8.1 us
    pallas_call x1, Pallas kernels, local(): pl.pallas_call(input_kernel, out_shape=(jax.ShapeDtypeStruct(four.shape,...  7.58 us
    pallas_call x1, Pallas kernels, local(): pl.pallas_call(functools.partial(forward_kernel, sp_count), out_shape=(fr...  6.43 us
    pallas_call x1, Pallas kernels, local(): pl.pallas_call(functools.partial(slope_kernel, counts), out_shape=(jax.Sh...  3.01 us
  transfers between devices with their start and end apart: 28, of which 20 were waited for; matrix products, arithmetic and copies ran while one was open for 1% of the time, Pallas kernels for 8%

commit v1 on v0

--- a/solution.py
+++ b/solution.py
@@ -13,7 +13,7 @@
 F32 = jnp.float32
 BF16 = jnp.bfloat16
 VMEM_LIMIT = 20 * 1024 * 1024
-EDGE_LIMIT = 60 * 1024 * 1024
+EDGE_LIMIT = 62 * 1024 * 1024
 
 
 def chunk_of(rows, most):
@@ -39,9 +39,11 @@
 
 def put_three(three, row, cells, cols, turned):
     pitch, chan = cells.shape
-    col = lax.broadcasted_iota(jnp.int32, cells.shape, 0)
-    left = jnp.where(col == 0, 0.0, pltpu.roll(cells, 1, 0))
-    right = jnp.where(col >= cols - 1, 0.0, pltpu.roll(cells, pitch - 1, 0))
+    left, right = pltpu.roll(cells, 1, 0), pltpu.roll(cells, pitch - 1, 0)
+    if pitch == cols:
+        col = lax.broadcasted_iota(jnp.int32, (8, chan), 0)
+        left = jnp.concatenate([jnp.where(col == 0, 0.0, left[:8]), left[8:]], 0)
+        right = jnp.concatenate([right[:-8], jnp.where(col == 7, 0.0, right[-8:])], 0)
     parts = (right, cells, left) if turned else (left, cells, right)
     for place, part in enumerate(parts):
         three[row, :, place * chan : (place + 1) * chan] = part.astype(BF16)
@@ -173,7 +175,7 @@
     put(0, above)
     put(rows + 1, below)
     zero = jnp.zeros((8, chan), F32)
-    first, second = lax.fori_loop(0, rows, step, (zero, zero), unroll=3)
+    first, second = lax.fori_loop(0, rows, step, (zero, zero), unroll=chunk_of(rows, 8))
     first = 0.5 * jnp.sum(first, 0, keepdims=True)
     return first, 0.5 * coefs[1] * jnp.sum(second, 0, keepdims=True)
 
@@ -367,23 +369,34 @@
     return sums
 
 
-def digit_order(parts, digit):
-    odd = digit % 2 == 1
-    high = digit >= 2
-    even = [jnp.where(odd, parts[k ^ 1], parts[k]) for k in range(4)]
-    return jnp.stack([jnp.where(high, even[k ^ 2], even[k]) for k in range(4)])
-
-
-def scatter_start(own, sent):
+def places():
+    found = []
+    for shift in (0, 2):
+        digit = (lax.axis_index("rep") >> shift) & (RADIX - 1)
+        found.append(([digit ^ k for k in range(RADIX)], (digit & 1) == 1, digit >= 2))
+    return found
+
+
+def digit_order(parts, place):
+    unused, odd, high = place
+    even = [jnp.where(odd, parts[k ^ 1], parts[k]) for k in range(RADIX)]
+    return jnp.stack([jnp.where(high, even[k ^ 2], even[k]) for k in range(RADIX)])
+
+
+def piece_of(pieces, index):
+    sizes = (1,) + pieces.shape[1:]
+    return lax.dynamic_slice(pieces, (index, 0, 0), sizes, allow_negative_indices=False)[0]
+
+
+def scatter_start(own, sent, place):
     met = [swap(sent[step], "sp", step + 1) for step in range(sent.shape[0])]
     chan = own.shape[2]
     parts = [part.reshape(RADIX, -1, chan) for part in [own] + met]
-    digit = lax.axis_index("rep") % RADIX
 
     def piece(k):
-        total = lax.dynamic_index_in_dim(parts[0], digit ^ k, 0, False)
+        total = piece_of(parts[0], place[0][k])
         for part in parts[1:]:
-            total = total + lax.dynamic_index_in_dim(part, digit ^ k, 0, False).astype(F32)
+            total = total + piece_of(part, place[0][k]).astype(F32)
         return total
 
     return piece(0), [piece(k).astype(BF16) for k in range(1, RADIX)]
@@ -393,24 +406,23 @@
     return (own + met[0].astype(F32)) + (met[1].astype(F32) + met[2].astype(F32))
 
 
-def weight_finish(total):
+def weight_finish(total, found):
     chan = total.shape[1]
-    digit = lax.axis_index("rep") // RADIX % RADIX
+    indices = found[1][0]
     pieces = total.reshape(RADIX, -1, chan)
     met = [
-        swap(lax.dynamic_index_in_dim(pieces, digit ^ k, 0, False).astype(BF16), "rep", k * RADIX)
+        swap(piece_of(pieces, indices[k]).astype(BF16), "rep", k * RADIX)
         for k in range(1, RADIX)
     ]
-    total = added(lax.dynamic_index_in_dim(pieces, digit, 0, False), met).astype(BF16)
+    total = added(piece_of(pieces, indices[0]), met).astype(BF16)
     stride = GROUP
     while stride < lax.axis_size("rep"):
         met = [swap(total, "rep", k * stride) for k in range(1, RADIX)]
         total = added(total.astype(F32), met).astype(BF16)
         stride = RADIX * stride
-    for stride in (RADIX, 1):
-        digit = lax.axis_index("rep") // stride % RADIX
+    for stride, place in ((RADIX, found[1]), (1, found[0])):
         met = [total] + [swap(total, "rep", k * stride) for k in range(1, RADIX)]
-        total = digit_order(met, digit).reshape(-1, chan)
+        total = digit_order(met, place).reshape(-1, chan)
     return total.astype(F32)
 
 
@@ -425,6 +437,7 @@
         float(images * GROUP * rows_four * sp_count * cols_four),
         float(images * GROUP * rows_six * sp_count * cols_six),
     )
+    found, four = lax.optimization_barrier((places(), four))
     above, below = edges(four, six, cot_four, cot_six)
     vmem = pl.BlockSpec(memory_space=pltpu.VMEM)
     params = pltpu.CompilerParams(vmem_limit_bytes=VMEM_LIMIT)
@@ -486,7 +499,7 @@
         name="backward",
     )(four, six, conv_four, conv_six, slope_four, slope_six, moments, slopes, bn_gain, bn_shift)
 
-    piece, pieces = scatter_start(own, sent)
+    piece, pieces = scatter_start(own, sent, found[0])
     pieces, three_four = lax.optimization_barrier((pieces, three_four))
     met = [swap(pieces[k - 1], "rep", k) for k in range(1, RADIX)]
     grad_four, grad_six = pl.pallas_call(
@@ -502,7 +515,7 @@
         name="inputs",
     )(three_four, three_six, conv_weight)
     met, grad_six = lax.optimization_barrier((met, grad_six))
-    grad_weight = weight_finish(added(piece, met)).reshape(own.shape)
+    grad_weight = weight_finish(added(piece, met), found).reshape(own.shape)
     totals = every_group(slopes)
     grad_gain = jnp.stack([totals[1], totals[3]])
     grad_shift = jnp.stack([totals[0], totals[2]])

time: 99.4 us -> 91.5 us (0.921)
  local copies, waits for them, and re-layouts: 9.28 us -> 1.72 us
    unnamed x24 -> x14, local copies, waits for them, and re-layouts: 9.25 us -> 1.69 us
  transfers between devices with their start and end apart: 28 -> 28, of which waited for: 20 -> 20; matrix products, arithmetic and copies ran while one was open for 1% -> 1% of each run, Pallas kernels for 8% -> 9%
where the time goes in v1:
time: 91.5 us; the launch traced here: 91.3 us
  starting transfers between devices  32.6 us (36%)
  waiting for transfers between devices  27.3 us (30%)
  Pallas kernels  26.6 us (29%)
  other arithmetic  2.17 us (2%)
  local copies, waits for them, and re-layouts  1.72 us (2%)
    ppermute x28, starting transfers between devices, swap(): return lax.ppermute(array, axis, [(i, i ^ stride) for i in range(count)])  32.6 us
    ppermute x28, waiting for transfers between devices, swap(): return lax.ppermute(array, axis, [(i, i ^ stride) for i in range(count)])  27.3 us
    pallas_call x1, Pallas kernels, local(): pl.pallas_call(input_kernel, out_shape=(jax.ShapeDtypeStruct(four.shape,...  8 us
    pallas_call x1, Pallas kernels, local(): pl.pallas_call(functools.partial(backward_kernel, counts, sp_count), out_...  7.54 us
    pallas_call x1, Pallas kernels, local(): pl.pallas_call(functools.partial(forward_kernel, sp_count), out_shape=(fr...  6.48 us
    pallas_call x1, Pallas kernels, local(): pl.pallas_call(functools.partial(slope_kernel, counts), out_shape=(jax.Sh...  2.91 us
  transfers between devices with their start and end apart: 28, of which 20 were waited for; matrix products, arithmetic and copies ran while one was open for 1% of the time, Pallas kernels for 9%

profile of v1, /device:TPU:0, one launch (start us, length us, event | category | flops | bytes accessed | tf_op | source)
XLA Modules:
  0.0 91.3 jit_solution(15893337755539181311)
XLA Ops:
  0.7 1.7 %edges.1 = bf16[384,256]{1,0:T(8,128)(2,1)} custom-call(bf16[48,96,256]{2,1,0:T(8,128)(2,1)} %bitcast.57, bf16[12,24,256]{2,1,0:T(8,128)(2,1)} %bitcast.64, bf16[48,96,256]{2,1,0:T(8,128)(2,1)} %bitcast.55, bf16[12,24,256]{2,1,0:T(8,128)(2,1)} %bitcast.62), custom_call_target="tpu_custom_call" | custom-call | tf_op jit(solution)/shard_map/edges/pallas_call | solution.py:331
  2.4 0.0 copy-start
  2.4 0.5 collective-permute-start
  2.9 1.3 %collective-permute-done.above_ref.below_ref = bf16[384,256]{1,0:T(8,128)(2,1)S(1)} collective-permute-done((bf16[384,256]{1,0:T(8,128)(2,1)}, bf16[384,256]{1,0:T(8,128)(2,1)S(1)}, u32[]{:S(2)}, u32[]{:S(2)}) %collective-permute-start) | collective-permute-done | bytes 196640 | tf_op jit(solution)/shard_map/ppermute | solution.py:289
  4.2 1.7 %copy-done.1 = bf16[1,48,96,256]{3,2,1,0:T(8,128)(2,1)S(1)} copy-done((bf16[1,48,96,256]{3,2,1,0:T(8,128)(2,1)S(1)}, bf16[1,48,96,256]{3,2,1,0:T(8,128)(2,1)}, u32[]{:S(2)}) %copy-start.1) | copy-done | bytes 2359320
  5.9 6.5 %forward.1 = (bf16[50,96,256]{2,1,0:T(8,128)(2,1)S(1)}, bf16[14,32,256]{2,1,0:T(8,128)(2,1)S(1)}, f32[4,256]{1,0:T(4,128)S(1)}) custom-call(bf16[48,96,256]{2,1,0:T(8,128)(2,1)S(1)} %bitcast.58, bf16[12,24,256]{2,1,0:T(8,128)(2,1)S(1)} %bitcast.65, bf16[384,256]{1,0:T(8,128)(2,1)S(1)} %collective-permute-done.above_ref.below_ref, ...), custom_call_target="tpu_custom_call" | custom-call | flops 5775556608 | bytes 4718592 | tf_op jit(solution)/shard_map/forward/pallas_call | solution.py:452
  12.4 0.5 collective-permute-start.1
  12.8 0.8 collective-permute-done.1
  13.7 2.8 %collective-permute-start.3 = (f32[4,256]{1,0:T(4,128)S(1)}, f32[4,256]{1,0:T(4,128)S(1)}, u32[]{:S(2)}, u32[]{:S(2)}) collective-permute-start(f32[4,256]{1,0:T(4,128)S(1)} %add.78), channel_id=1, source_target_pairs={{0,4},{2,6},{4,0},{6,2},{8,12},{10,14},{12,8},{14,10},{16,20},{18,... | collective-permute-start | bytes 12296 | tf_op jit(solution)/shard_map/ppermute | solution.py:289
  16.5 1.4 %collective-permute-start.4 = (f32[4,256]{1,0:T(4,128)S(1)}, f32[4,256]{1,0:T(4,128)S(1)}, u32[]{:S(2)}, u32[]{:S(2)}) collective-permute-start(f32[4,256]{1,0:T(4,128)S(1)} %add.78), channel_id=1, source_target_pairs={{0,6},{2,4},{4,2},{6,0},{8,14},{10,12},{12,10},{14,8},{16,22},{18,... | collective-permute-start | bytes 12296 | tf_op jit(solution)/shard_map/ppermute | solution.py:289
  18.0 0.0 collective-permute-start.2
  18.0 0.1 collective-permute-done.3
  18.1 2.9 %collective-permute-done.4 = f32[4,256]{1,0:T(4,128)S(1)} collective-permute-done((f32[4,256]{1,0:T(4,128)S(1)}, f32[4,256]{1,0:T(4,128)S(1)}, u32[]{:S(2)}, u32[]{:S(2)}) %collective-permute-start.4) | collective-permute-done | bytes 4128 | tf_op jit(solution)/shard_map/ppermute | solution.py:289
  21.0 0.5 collective-permute-done.2
  21.6 2.6 %collective-permute-start.6 = (f32[4,256]{1,0:T(4,128)S(1)}, f32[4,256]{1,0:T(4,128)S(1)}, u32[]{:S(2)}, u32[]{:S(2)}) collective-permute-start(f32[4,256]{1,0:T(4,128)S(1)} %add_add_fusion.3), channel_id=1, source_target_pairs={{0,16},{2,18},{4,20},{6,22},{8,24},{10,26},{12,28},{14,30},{16,0},... | collective-permute-start | bytes 12296 | tf_op jit(solution)/shard_map/ppermute | solution.py:289
  24.1 1.4 %collective-permute-start.7 = (f32[4,256]{1,0:T(4,128)S(1)}, f32[4,256]{1,0:T(4,128)S(1)}, u32[]{:S(2)}, u32[]{:S(2)}) collective-permute-start(f32[4,256]{1,0:T(4,128)S(1)} %add_add_fusion.3), channel_id=1, source_target_pairs={{0,24},{2,26},{4,28},{6,30},{8,16},{10,18},{12,20},{14,22},{16,8},... | collective-permute-start | bytes 12296 | tf_op jit(solution)/shard_map/ppermute | solution.py:289
  25.5 0.2 collective-permute-start.5
  25.7 0.4 collective-permute-done.6
  26.1 3.5 %collective-permute-done.7 = f32[4,256]{1,0:T(4,128)S(1)} collective-permute-done((f32[4,256]{1,0:T(4,128)S(1)}, f32[4,256]{1,0:T(4,128)S(1)}, u32[]{:S(2)}, u32[]{:S(2)}) %collective-permute-start.7) | collective-permute-done | bytes 4128 | tf_op jit(solution)/shard_map/ppermute | solution.py:289
  29.5 0.0 collective-permute-done.5
  29.6 2.9 %slopes.1 = (f32[50,96,256]{2,1,0:T(8,128)S(1)}, f32[14,32,256]{2,1,0:T(8,128)S(1)}, f32[4,256]{1,0:T(4,128)S(1)}) custom-call(bf16[50,96,256]{2,1,0:T(8,128)(2,1)S(1)} %get-tuple-element.39.conv_four_ref, bf16[14,32,256]{2,1,0:T(8,128)(2,1)S(1)} %get-tuple-element.40.conv_six_ref, bf16[48,96,256]{2,1,0:T(8,128)(2,1)S(1)} %bitcast.56, ...), custom_call_target="tpu_custom_call" | custom-call | flops 57755568 | bytes 4718592 | tf_op jit(solution)/shard_map/slopes/pallas_call | solution.py:467
  32.5 0.1 collective-permute-start.8
  32.6 1.2 %collective-permute-done.8 = f32[4,256]{1,0:T(4,128)S(1)} collective-permute-done((f32[4,256]{1,0:T(4,128)S(1)}, f32[4,256]{1,0:T(4,128)S(1)}, u32[]{:S(2)}, u32[]{:S(2)}) %collective-permute-start.8) | collective-permute-done | bytes 4128 | tf_op jit(solution)/shard_map/ppermute | solution.py:289
  33.7 1.5 %collective-permute-start.10 = (f32[4,256]{1,0:T(4,128)S(1)}, f32[4,256]{1,0:T(4,128)S(1)}, u32[]{:S(2)}, u32[]{:S(2)}) collective-permute-start(f32[4,256]{1,0:T(4,128)S(1)} %add.85), channel_id=1, source_target_pairs={{0,4},{2,6},{4,0},{6,2},{8,12},{10,14},{12,8},{14,10},{16,20},{18,... | collective-permute-start | bytes 12296 | tf_op jit(solution)/shard_map/ppermute | solution.py:289
  35.3 1.0 %collective-permute-start.11 = (f32[4,256]{1,0:T(4,128)S(1)}, f32[4,256]{1,0:T(4,128)S(1)}, u32[]{:S(2)}, u32[]{:S(2)}) collective-permute-start(f32[4,256]{1,0:T(4,128)S(1)} %add.85), channel_id=1, source_target_pairs={{0,6},{2,4},{4,2},{6,0},{8,14},{10,12},{12,10},{14,8},{16,22},{18,... | collective-permute-start | bytes 12296 | tf_op jit(solution)/shard_map/ppermute | solution.py:289
  36.2 1.0 %collective-permute-start.9 = (f32[4,256]{1,0:T(4,128)S(1)}, f32[4,256]{1,0:T(4,128)S(1)}, u32[]{:S(2)}, u32[]{:S(2)}) collective-permute-start(f32[4,256]{1,0:T(4,128)S(1)} %add.85), channel_id=1, source_target_pairs={{0,2},{2,0},{4,6},{6,4},{8,10},{10,8},{12,14},{14,12},{16,18},{18,... | collective-permute-start | bytes 12296 | tf_op jit(solution)/shard_map/ppermute | solution.py:289
  37.2 0.1 collective-permute-done.10
  37.4 2.4 %collective-permute-done.11 = f32[4,256]{1,0:T(4,128)S(1)} collective-permute-done((f32[4,256]{1,0:T(4,128)S(1)}, f32[4,256]{1,0:T(4,128)S(1)}, u32[]{:S(2)}, u32[]{:S(2)}) %collective-permute-start.11) | collective-permute-done | bytes 4128 | tf_op jit(solution)/shard_map/ppermute | solution.py:289
  39.8 0.1 collective-permute-done.9
  39.9 1.2 %collective-permute-start.13 = (f32[4,256]{1,0:T(4,128)S(1)}, f32[4,256]{1,0:T(4,128)S(1)}, u32[]{:S(2)}, u32[]{:S(2)}) collective-permute-start(f32[4,256]{1,0:T(4,128)S(1)} %add_add_fusion.1), channel_id=1, source_target_pairs={{0,16},{2,18},{4,20},{6,22},{8,24},{10,26},{12,28},{14,30},{16,0},... | collective-permute-start | bytes 12296 | tf_op jit(solution)/shard_map/ppermute | solution.py:289
  41.1 0.9 %collective-permute-start.14 = (f32[4,256]{1,0:T(4,128)S(1)}, f32[4,256]{1,0:T(4,128)S(1)}, u32[]{:S(2)}, u32[]{:S(2)}) collective-permute-start(f32[4,256]{1,0:T(4,128)S(1)} %add_add_fusion.1), channel_id=1, source_target_pairs={{0,24},{2,26},{4,28},{6,30},{8,16},{10,18},{12,20},{14,22},{16,8},... | collective-permute-start | bytes 12296 | tf_op jit(solution)/shard_map/ppermute | solution.py:289
  42.0 1.4 %collective-permute-start.12 = (f32[4,256]{1,0:T(4,128)S(1)}, f32[4,256]{1,0:T(4,128)S(1)}, u32[]{:S(2)}, u32[]{:S(2)}) collective-permute-start(f32[4,256]{1,0:T(4,128)S(1)} %add_add_fusion.1), channel_id=1, source_target_pairs={{0,8},{2,10},{4,12},{6,14},{8,0},{10,2},{12,4},{14,6},{16,24},{18,... | collective-permute-start | bytes 12296 | tf_op jit(solution)/shard_map/ppermute | solution.py:289
  43.3 1.0 %collective-permute-done.13 = f32[4,256]{1,0:T(4,128)S(1)} collective-permute-done((f32[4,256]{1,0:T(4,128)S(1)}, f32[4,256]{1,0:T(4,128)S(1)}, u32[]{:S(2)}, u32[]{:S(2)}) %collective-permute-start.13) | collective-permute-done | bytes 4128 | tf_op jit(solution)/shard_map/ppermute | solution.py:289
  44.4 2.1 %collective-permute-done.14 = f32[4,256]{1,0:T(4,128)S(1)} collective-permute-done((f32[4,256]{1,0:T(4,128)S(1)}, f32[4,256]{1,0:T(4,128)S(1)}, u32[]{:S(2)}, u32[]{:S(2)}) %collective-permute-start.14) | collective-permute-done | bytes 4128 | tf_op jit(solution)/shard_map/ppermute | solution.py:289
  46.5 0.0 collective-permute-done.12
  46.5 7.5 %backward.1 = (bf16[50,96,768]{2,1,0:T(8,128)(2,1)S(1)}, bf16[14,32,768]{2,1,0:T(8,128)(2,1)S(1)}, f32[9,128,256]{2,1,0:T(8,128)S(1)}, bf16[1,9,128,256]{3,2,1,0:T(8,128)(2,1)S(1)}) custom-call(bf16[48,96,256]{2,1,0:T(8,128)(2,1)S(1)} %bitcast.59, bf16[12,24,256]{2,1,0:T(8,128)(2,1)S(1)} %bitcast.66, ...), custom_call_target="tpu_custom_call" | custom-call | flops 6930668032 | bytes 9437184 | tf_op jit(solution)/shard_map/backward/pallas_call | solution.py:486
  54.0 0.1 collective-permute-start.15
  54.1 2.0 %collective-permute-done.15 = bf16[9,128,256]{2,1,0:T(8,128)(2,1)S(1)} collective-permute-done((bf16[9,128,256]{2,1,0:T(8,128)(2,1)S(1)}, bf16[9,128,256]{2,1,0:T(8,128)(2,1)S(1)}, u32[]{:S(2)}, u32[]{:S(2)}) %collective-permute-start.15) | collective-permute-done | bytes 589856 | tf_op jit(solution)/shard_map/ppermute | solution.py:289
  56.1 0.1 fusion.3
  56.2 1.1 %collective-permute-start.16 = (bf16[288,256]{1,0:T(8,128)(2,1)S(1)}, bf16[288,256]{1,0:T(8,128)(2,1)S(1)}, u32[]{:S(2)}, u32[]{:S(2)}) collective-permute-start(bf16[288,256]{1,0:T(8,128)(2,1)S(1)} %get-tuple-element.54), channel_id=1, source_target_pairs={{0,2},{2,0},{4,6},{6,4},{8,10},{10,8},{12,14},{14,12},{16,18},{18,... | collective-permute-start | bytes 442376 | tf_op jit(solution)/shard_map/ppermute | solution.py:289
  57.3 1.5 %collective-permute-start.17 = (bf16[288,256]{1,0:T(8,128)(2,1)S(1)}, bf16[288,256]{1,0:T(8,128)(2,1)S(1)}, u32[]{:S(2)}, u32[]{:S(2)}) collective-permute-start(bf16[288,256]{1,0:T(8,128)(2,1)S(1)} %get-tuple-element.55), channel_id=1, source_target_pairs={{0,4},{2,6},{4,0},{6,2},{8,12},{10,14},{12,8},{14,10},{16,20},{18,... | collective-permute-start | bytes 442376 | tf_op jit(solution)/shard_map/ppermute | solution.py:289
  58.8 1.0 %collective-permute-start.18 = (bf16[288,256]{1,0:T(8,128)(2,1)S(1)}, bf16[288,256]{1,0:T(8,128)(2,1)S(1)}, u32[]{:S(2)}, u32[]{:S(2)}) collective-permute-start(bf16[288,256]{1,0:T(8,128)(2,1)S(1)} %get-tuple-element.56), channel_id=1, source_target_pairs={{0,6},{2,4},{4,2},{6,0},{8,14},{10,12},{12,10},{14,8},{16,22},{18,... | collective-permute-start | bytes 442376 | tf_op jit(solution)/shard_map/ppermute | solution.py:289
  59.8 8.0 %inputs.1 = (bf16[48,96,256]{2,1,0:T(8,128)(2,1)}, bf16[12,24,256]{2,1,0:T(8,128)(2,1)}) custom-call(bf16[50,96,768]{2,1,0:T(8,128)(2,1)S(1)} %get-tuple-element.51.three_four, bf16[14,32,768]{2,1,0:T(8,128)(2,1)S(1)} %get-tuple-element.52.three_six, bf16[9,256,256]{2,1,0:T(8,128)(2,1)S(1)} %copy-done.6), custom_call_target="tpu_custom_call" | custom-call | flops 5775556608 | bytes 4718592 | tf_op jit(solution)/shard_map/inputs/pallas_call | solution.py:505
  67.8 0.0 collective-permute-done.16
  67.8 0.1 fusion
  67.9 2.1 %collective-permute-start.21 = (bf16[72,256]{1,0:T(8,128)(2,1)S(1)}, bf16[72,256]{1,0:T(8,128)(2,1)S(1)}, u32[]{:S(2)}, u32[]{:S(2)}) collective-permute-start(bf16[72,256]{1,0:T(8,128)(2,1)S(1)} %get-tuple-element.79), channel_id=1, source_target_pairs={{0,24},{2,26},{4,28},{6,30},{8,16},{10,18},{12,20},{14,22},{16,8},... | collective-permute-start | bytes 110600 | tf_op jit(solution)/shard_map/ppermute | solution.py:289
  70.0 2.4 %collective-permute-start.19 = (bf16[72,256]{1,0:T(8,128)(2,1)S(1)}, bf16[72,256]{1,0:T(8,128)(2,1)S(1)}, u32[]{:S(2)}, u32[]{:S(2)}) collective-permute-start(bf16[72,256]{1,0:T(8,128)(2,1)S(1)} %get-tuple-element.78), channel_id=1, source_target_pairs={{0,8},{2,10},{4,12},{6,14},{8,0},{10,2},{12,4},{14,6},{16,24},{18,... | collective-permute-start | bytes 110600 | tf_op jit(solution)/shard_map/ppermute | solution.py:289
  72.4 1.5 %collective-permute-done.21 = bf16[72,256]{1,0:T(8,128)(2,1)S(1)} collective-permute-done((bf16[72,256]{1,0:T(8,128)(2,1)S(1)}, bf16[72,256]{1,0:T(8,128)(2,1)S(1)}, u32[]{:S(2)}, u32[]{:S(2)}) %collective-permute-start.21) | collective-permute-done | bytes 36896 | tf_op jit(solution)/shard_map/ppermute | solution.py:289
  73.9 1.0 %collective-permute-done.20 = bf16[72,256]{1,0:T(8,128)(2,1)S(1)} collective-permute-done((bf16[72,256]{1,0:T(8,128)(2,1)S(1)}, bf16[72,256]{1,0:T(8,128)(2,1)S(1)}, u32[]{:S(2)}, u32[]{:S(2)}) %collective-permute-start.20) | collective-permute-done | bytes 36896 | tf_op jit(solution)/shard_map/ppermute | solution.py:289
  75.0 2.1 %collective-permute-start.22 = (bf16[72,256]{1,0:T(8,128)(2,1)S(1)}, bf16[72,256]{1,0:T(8,128)(2,1)S(1)}, u32[]{:S(2)}, u32[]{:S(2)}) collective-permute-start(bf16[72,256]{1,0:T(8,128)(2,1)S(1)} %fusion.5), channel_id=1, source_target_pairs={{0,24},{2,26},{4,28},{6,30},{8,16},{10,18},{12,20},{14,22},{16,8},... | collective-permute-start | bytes 110600 | tf_op jit(solution)/shard_map/ppermute | solution.py:289
  77.0 0.9 collective-permute-start.23
  77.9 1.5 %collective-permute-start.24 = (bf16[72,256]{1,0:T(8,128)(2,1)S(1)}, bf16[72,256]{1,0:T(8,128)(2,1)S(1)}, u32[]{:S(2)}, u32[]{:S(2)}) collective-permute-start(bf16[72,256]{1,0:T(8,128)(2,1)S(1)} %fusion.5), channel_id=1, source_target_pairs={{0,8},{2,10},{4,12},{6,14},{8,0},{10,2},{12,4},{14,6},{16,24},{18,... | collective-permute-start | bytes 110600 | tf_op jit(solution)/shard_map/ppermute | solution.py:289
  79.4 1.4 %collective-permute-done.22 = bf16[72,256]{1,0:T(8,128)(2,1)S(1)} collective-permute-done((bf16[72,256]{1,0:T(8,128)(2,1)S(1)}, bf16[72,256]{1,0:T(8,128)(2,1)S(1)}, u32[]{:S(2)}, u32[]{:S(2)}) %collective-permute-start.22) | collective-permute-done | bytes 36896 | tf_op jit(solution)/shard_map/ppermute | solution.py:289
  80.8 1.5 %collective-permute-done.23 = bf16[72,256]{1,0:T(8,128)(2,1)S(1)} collective-permute-done((bf16[72,256]{1,0:T(8,128)(2,1)S(1)}, bf16[72,256]{1,0:T(8,128)(2,1)S(1)}, u32[]{:S(2)}, u32[]{:S(2)}) %collective-permute-start.23) | collective-permute-done | bytes 36896 | tf_op jit(solution)/shard_map/ppermute | solution.py:289
  82.2 0.0 collective-permute-done.24
  82.3 2.0 %collective-permute-start.25 = (bf16[288,256]{1,0:T(8,128)(2,1)S(1)}, bf16[288,256]{1,0:T(8,128)(2,1)S(1)}, u32[]{:S(2)}, u32[]{:S(2)}) collective-permute-start(bf16[288,256]{1,0:T(8,128)(2,1)S(1)} %bitcast.73), channel_id=1, source_target_pairs={{0,6},{2,4},{4,2},{6,0},{8,14},{10,12},{12,10},{14,8},{16,22},{18,... | collective-permute-start | bytes 442376 | tf_op jit(solution)/shard_map/ppermute | solution.py:289
  84.3 0.5 collective-permute-start.26
  84.8 1.0 %collective-permute-start.27 = (bf16[288,256]{1,0:T(8,128)(2,1)S(1)}, bf16[288,256]{1,0:T(8,128)(2,1)S(1)}, u32[]{:S(2)}, u32[]{:S(2)}) collective-permute-start(bf16[288,256]{1,0:T(8,128)(2,1)S(1)} %bitcast.75), channel_id=1, source_target_pairs={{0,2},{2,0},{4,6},{6,4},{8,10},{10,8},{12,14},{14,12},{16,18},{18,... | collective-permute-start | bytes 442376 | tf_op jit(solution)/shard_map/ppermute | solution.py:289
  85.9 0.6 pad_maximum_fusion.2
  86.4 2.0 %collective-permute-done.25 = bf16[288,256]{1,0:T(8,128)(2,1)S(1)} collective-permute-done((bf16[288,256]{1,0:T(8,128)(2,1)S(1)}, bf16[288,256]{1,0:T(8,128)(2,1)S(1)}, u32[]{:S(2)}, u32[]{:S(2)}) %collective-permute-start.25) | collective-permute-done | bytes 147488 | tf_op jit(solution)/shard_map/ppermute | solution.py:289
  88.5 1.5 %collective-permute-done.26 = bf16[288,256]{1,0:T(8,128)(2,1)S(1)} collective-permute-done((bf16[288,256]{1,0:T(8,128)(2,1)S(1)}, bf16[288,256]{1,0:T(8,128)(2,1)S(1)}, u32[]{:S(2)}, u32[]{:S(2)}) %collective-permute-start.26) | collective-permute-done | bytes 147488 | tf_op jit(solution)/shard_map/ppermute | solution.py:289
  90.0 0.1 select_bitcast_fusion.3
  90.1 0.1 pad_maximum_fusion
  90.1 1.1 %convert.1 = f32[9,128,256]{2,1,0:T(8,128)} convert(bf16[9,128,256]{2,1,0:T(8,128)(2,1)S(1)} %bitcast.68) | non-fusion elementwise | flops 294912 | bytes 1769472 | tf_op jit(solution)/shard_map/convert_element_type | solution.py:426
  (28 shorter events, 0.2 us)
Async XLA Ops:
  0.6 3.6 %copy-start.3 = (bf16[1,12,24,256]{3,2,1,0:T(8,128)(2,1)S(1)}, bf16[1,12,24,256]{3,2,1,0:T(8,128)(2,1)}, u32[]{:S(2)}) copy-start(bf16[1,12,24,256]{3,2,1,0:T(8,128)(2,1)} %param.8) | copy-start | bytes 442372
  0.7 3.6 %copy-start.6 = (bf16[9,256,256]{2,1,0:T(8,128)(2,1)S(1)}, bf16[9,256,256]{2,1,0:T(8,128)(2,1)}, u32[]{:S(2)}) copy-start(bf16[9,256,256]{2,1,0:T(8,128)(2,1)} %w_ref.3) | copy-start | bytes 3538948
  0.7 28.9 %copy-start.2 = (bf16[1,12,24,256]{3,2,1,0:T(8,128)(2,1)S(1)}, bf16[1,12,24,256]{3,2,1,0:T(8,128)(2,1)}, u32[]{:S(2)}) copy-start(bf16[1,12,24,256]{3,2,1,0:T(8,128)(2,1)} %param.13) | copy-start | bytes 442372
  0.7 28.9 %copy-start.4 = (f32[2,256]{1,0:T(2,128)S(1)}, f32[2,256]{1,0:T(2,128)}, u32[]{:S(2)}) copy-start(f32[2,256]{1,0:T(2,128)} %gain_ref.3) | copy-start | bytes 6148
  0.7 28.9 %copy-start.5 = (f32[2,256]{1,0:T(2,128)S(1)}, f32[2,256]{1,0:T(2,128)}, u32[]{:S(2)}) copy-start(f32[2,256]{1,0:T(2,128)} %shift_ref.3) | copy-start | bytes 6148
  2.4 27.2 %copy-start = (bf16[1,48,96,256]{3,2,1,0:T(8,128)(2,1)S(1)}, bf16[1,48,96,256]{3,2,1,0:T(8,128)(2,1)}, u32[]{:S(2)}) copy-start(bf16[1,48,96,256]{3,2,1,0:T(8,128)(2,1)} %param.12) | copy-start | bytes 7077892
  2.4 1.8 %collective-permute-start = (bf16[384,256]{1,0:T(8,128)(2,1)}, bf16[384,256]{1,0:T(8,128)(2,1)S(1)}, u32[]{:S(2)}, u32[]{:S(2)}) collective-permute-start(bf16[384,256]{1,0:T(8,128)(2,1)} %edges.1), channel_id=1, source_target_pairs={{0,1},{1,0},{2,3},{3,2},{4,5},{5,4},{6,7},{7,6},{8,9},{9,8},{10,11... | collective-permute-start | bytes 589832 | tf_op jit(solution)/shard_map/ppermute | solution.py:289
  4.2 1.7 %copy-start.1 = (bf16[1,48,96,256]{3,2,1,0:T(8,128)(2,1)S(1)}, bf16[1,48,96,256]{3,2,1,0:T(8,128)(2,1)}, u32[]{:S(2)}) copy-start(bf16[1,48,96,256]{3,2,1,0:T(8,128)(2,1)} %param.7) | copy-start | bytes 7077892
  12.4 1.3 %collective-permute-start.1 = (f32[4,256]{1,0:T(4,128)S(1)}, f32[4,256]{1,0:T(4,128)S(1)}, u32[]{:S(2)}, u32[]{:S(2)}) collective-permute-start(f32[4,256]{1,0:T(4,128)S(1)} %get-tuple-element.41), channel_id=1, source_target_pairs={{0,1},{1,0},{2,3},{3,2},{4,5},{5,4},{6,7},{7,6},{8,9},{9,8},{10,11... | collective-permute-start | bytes 12296 | tf_op jit(solution)/shard_map/ppermute | solution.py:289
  13.7 4.4 %collective-permute-start.3 = (f32[4,256]{1,0:T(4,128)S(1)}, f32[4,256]{1,0:T(4,128)S(1)}, u32[]{:S(2)}, u32[]{:S(2)}) collective-permute-start(f32[4,256]{1,0:T(4,128)S(1)} %add.78), channel_id=1, source_target_pairs={{0,4},{2,6},{4,0},{6,2},{8,12},{10,14},{12,8},{14,10},{16,20},{18,... | collective-permute-start | bytes 12296 | tf_op jit(solution)/shard_map/ppermute | solution.py:289
  16.5 4.5 %collective-permute-start.4 = (f32[4,256]{1,0:T(4,128)S(1)}, f32[4,256]{1,0:T(4,128)S(1)}, u32[]{:S(2)}, u32[]{:S(2)}) collective-permute-start(f32[4,256]{1,0:T(4,128)S(1)} %add.78), channel_id=1, source_target_pairs={{0,6},{2,4},{4,2},{6,0},{8,14},{10,12},{12,10},{14,8},{16,22},{18,... | collective-permute-start | bytes 12296 | tf_op jit(solution)/shard_map/ppermute | solution.py:289
  18.0 3.6 %collective-permute-start.2 = (f32[4,256]{1,0:T(4,128)S(1)}, f32[4,256]{1,0:T(4,128)S(1)}, u32[]{:S(2)}, u32[]{:S(2)}) collective-permute-start(f32[4,256]{1,0:T(4,128)S(1)} %add.78), channel_id=1, source_target_pairs={{0,2},{2,0},{4,6},{6,4},{8,10},{10,8},{12,14},{14,12},{16,18},{18,... | collective-permute-start | bytes 12296 | tf_op jit(solution)/shard_map/ppermute | solution.py:289
  21.6 4.5 %collective-permute-start.6 = (f32[4,256]{1,0:T(4,128)S(1)}, f32[4,256]{1,0:T(4,128)S(1)}, u32[]{:S(2)}, u32[]{:S(2)}) collective-permute-start(f32[4,256]{1,0:T(4,128)S(1)} %add_add_fusion.3), channel_id=1, source_target_pairs={{0,16},{2,18},{4,20},{6,22},{8,24},{10,26},{12,28},{14,30},{16,0},... | collective-permute-start | bytes 12296 | tf_op jit(solution)/shard_map/ppermute | solution.py:289
  24.1 5.4 %collective-permute-start.7 = (f32[4,256]{1,0:T(4,128)S(1)}, f32[4,256]{1,0:T(4,128)S(1)}, u32[]{:S(2)}, u32[]{:S(2)}) collective-permute-start(f32[4,256]{1,0:T(4,128)S(1)} %add_add_fusion.3), channel_id=1, source_target_pairs={{0,24},{2,26},{4,28},{6,30},{8,16},{10,18},{12,20},{14,22},{16,8},... | collective-permute-start | bytes 12296 | tf_op jit(solution)/shard_map/ppermute | solution.py:289
  25.5 4.1 %collective-permute-start.5 = (f32[4,256]{1,0:T(4,128)S(1)}, f32[4,256]{1,0:T(4,128)S(1)}, u32[]{:S(2)}, u32[]{:S(2)}) collective-permute-start(f32[4,256]{1,0:T(4,128)S(1)} %add_add_fusion.3), channel_id=1, source_target_pairs={{0,8},{2,10},{4,12},{6,14},{8,0},{10,2},{12,4},{14,6},{16,24},{18,... | collective-permute-start | bytes 12296 | tf_op jit(solution)/shard_map/ppermute | solution.py:289
  32.5 1.2 %collective-permute-start.8 = (f32[4,256]{1,0:T(4,128)S(1)}, f32[4,256]{1,0:T(4,128)S(1)}, u32[]{:S(2)}, u32[]{:S(2)}) collective-permute-start(f32[4,256]{1,0:T(4,128)S(1)} %get-tuple-element.44), channel_id=1, source_target_pairs={{0,1},{1,0},{2,3},{3,2},{4,5},{5,4},{6,7},{7,6},{8,9},{9,8},{10,11... | collective-permute-start | bytes 12296 | tf_op jit(solution)/shard_map/ppermute | solution.py:289
  33.7 3.6 %collective-permute-start.10 = (f32[4,256]{1,0:T(4,128)S(1)}, f32[4,256]{1,0:T(4,128)S(1)}, u32[]{:S(2)}, u32[]{:S(2)}) collective-permute-start(f32[4,256]{1,0:T(4,128)S(1)} %add.85), channel_id=1, source_target_pairs={{0,4},{2,6},{4,0},{6,2},{8,12},{10,14},{12,8},{14,10},{16,20},{18,... | collective-permute-start | bytes 12296 | tf_op jit(solution)/shard_map/ppermute | solution.py:289
  35.3 4.5 %collective-permute-start.11 = (f32[4,256]{1,0:T(4,128)S(1)}, f32[4,256]{1,0:T(4,128)S(1)}, u32[]{:S(2)}, u32[]{:S(2)}) collective-permute-start(f32[4,256]{1,0:T(4,128)S(1)} %add.85), channel_id=1, source_target_pairs={{0,6},{2,4},{4,2},{6,0},{8,14},{10,12},{12,10},{14,8},{16,22},{18,... | collective-permute-start | bytes 12296 | tf_op jit(solution)/shard_map/ppermute | solution.py:289
  36.2 3.6 %collective-permute-start.9 = (f32[4,256]{1,0:T(4,128)S(1)}, f32[4,256]{1,0:T(4,128)S(1)}, u32[]{:S(2)}, u32[]{:S(2)}) collective-permute-start(f32[4,256]{1,0:T(4,128)S(1)} %add.85), channel_id=1, source_target_pairs={{0,2},{2,0},{4,6},{6,4},{8,10},{10,8},{12,14},{14,12},{16,18},{18,... | collective-permute-start | bytes 12296 | tf_op jit(solution)/shard_map/ppermute | solution.py:289
  39.9 4.5 %collective-permute-start.13 = (f32[4,256]{1,0:T(4,128)S(1)}, f32[4,256]{1,0:T(4,128)S(1)}, u32[]{:S(2)}, u32[]{:S(2)}) collective-permute-start(f32[4,256]{1,0:T(4,128)S(1)} %add_add_fusion.1), channel_id=1, source_target_pairs={{0,16},{2,18},{4,20},{6,22},{8,24},{10,26},{12,28},{14,30},{16,0},... | collective-permute-start | bytes 12296 | tf_op jit(solution)/shard_map/ppermute | solution.py:289
  41.1 5.4 %collective-permute-start.14 = (f32[4,256]{1,0:T(4,128)S(1)}, f32[4,256]{1,0:T(4,128)S(1)}, u32[]{:S(2)}, u32[]{:S(2)}) collective-permute-start(f32[4,256]{1,0:T(4,128)S(1)} %add_add_fusion.1), channel_id=1, source_target_pairs={{0,24},{2,26},{4,28},{6,30},{8,16},{10,18},{12,20},{14,22},{16,8},... | collective-permute-start | bytes 12296 | tf_op jit(solution)/shard_map/ppermute | solution.py:289
  42.0 4.5 %collective-permute-start.12 = (f32[4,256]{1,0:T(4,128)S(1)}, f32[4,256]{1,0:T(4,128)S(1)}, u32[]{:S(2)}, u32[]{:S(2)}) collective-permute-start(f32[4,256]{1,0:T(4,128)S(1)} %add_add_fusion.1), channel_id=1, source_target_pairs={{0,8},{2,10},{4,12},{6,14},{8,0},{10,2},{12,4},{14,6},{16,24},{18,... | collective-permute-start | bytes 12296 | tf_op jit(solution)/shard_map/ppermute | solution.py:289
  54.0 2.1 %collective-permute-start.15 = (bf16[9,128,256]{2,1,0:T(8,128)(2,1)S(1)}, bf16[9,128,256]{2,1,0:T(8,128)(2,1)S(1)}, u32[]{:S(2)}, u32[]{:S(2)}) collective-permute-start(bf16[9,128,256]{2,1,0:T(8,128)(2,1)S(1)} %bitcast.67), channel_id=1, source_target_pairs={{0,1},{1,0},{2,3},{3,2},{4,5},{5,4},{6,7},{7,6},{8,9},{9,8},{10,11... | collective-permute-start | bytes 1769480 | tf_op jit(solution)/shard_map/ppermute | solution.py:289
  56.2 11.6 %collective-permute-start.16 = (bf16[288,256]{1,0:T(8,128)(2,1)S(1)}, bf16[288,256]{1,0:T(8,128)(2,1)S(1)}, u32[]{:S(2)}, u32[]{:S(2)}) collective-permute-start(bf16[288,256]{1,0:T(8,128)(2,1)S(1)} %get-tuple-element.54), channel_id=1, source_target_pairs={{0,2},{2,0},{4,6},{6,4},{8,10},{10,8},{12,14},{14,12},{16,18},{18,... | collective-permute-start | bytes 442376 | tf_op jit(solution)/shard_map/ppermute | solution.py:289
  57.3 10.5 %collective-permute-start.17 = (bf16[288,256]{1,0:T(8,128)(2,1)S(1)}, bf16[288,256]{1,0:T(8,128)(2,1)S(1)}, u32[]{:S(2)}, u32[]{:S(2)}) collective-permute-start(bf16[288,256]{1,0:T(8,128)(2,1)S(1)} %get-tuple-element.55), channel_id=1, source_target_pairs={{0,4},{2,6},{4,0},{6,2},{8,12},{10,14},{12,8},{14,10},{16,20},{18,... | collective-permute-start | bytes 442376 | tf_op jit(solution)/shard_map/ppermute | solution.py:289
  58.8 9.0 %collective-permute-start.18 = (bf16[288,256]{1,0:T(8,128)(2,1)S(1)}, bf16[288,256]{1,0:T(8,128)(2,1)S(1)}, u32[]{:S(2)}, u32[]{:S(2)}) collective-permute-start(bf16[288,256]{1,0:T(8,128)(2,1)S(1)} %get-tuple-element.56), channel_id=1, source_target_pairs={{0,6},{2,4},{4,2},{6,0},{8,14},{10,12},{12,10},{14,8},{16,22},{18,... | collective-permute-start | bytes 442376 | tf_op jit(solution)/shard_map/ppermute | solution.py:289
  67.9 6.0 %collective-permute-start.21 = (bf16[72,256]{1,0:T(8,128)(2,1)S(1)}, bf16[72,256]{1,0:T(8,128)(2,1)S(1)}, u32[]{:S(2)}, u32[]{:S(2)}) collective-permute-start(bf16[72,256]{1,0:T(8,128)(2,1)S(1)} %get-tuple-element.79), channel_id=1, source_target_pairs={{0,24},{2,26},{4,28},{6,30},{8,16},{10,18},{12,20},{14,22},{16,8},... | collective-permute-start | bytes 110600 | tf_op jit(solution)/shard_map/ppermute | solution.py:289
  70.0 4.9 %collective-permute-start.20 = (bf16[72,256]{1,0:T(8,128)(2,1)S(1)}, bf16[72,256]{1,0:T(8,128)(2,1)S(1)}, u32[]{:S(2)}, u32[]{:S(2)}) collective-permute-start(bf16[72,256]{1,0:T(8,128)(2,1)S(1)} %get-tuple-element.80), channel_id=1, source_target_pairs={{0,16},{2,18},{4,20},{6,22},{8,24},{10,26},{12,28},{14,30},{16,0},... | collective-permute-start | bytes 110600 | tf_op jit(solution)/shard_map/ppermute | solution.py:289
  70.0 4.9 %collective-permute-start.19 = (bf16[72,256]{1,0:T(8,128)(2,1)S(1)}, bf16[72,256]{1,0:T(8,128)(2,1)S(1)}, u32[]{:S(2)}, u32[]{:S(2)}) collective-permute-start(bf16[72,256]{1,0:T(8,128)(2,1)S(1)} %get-tuple-element.78), channel_id=1, source_target_pairs={{0,8},{2,10},{4,12},{6,14},{8,0},{10,2},{12,4},{14,6},{16,24},{18,... | collective-permute-start | bytes 110600 | tf_op jit(solution)/shard_map/ppermute | solution.py:289
  75.0 5.8 %collective-permute-start.22 = (bf16[72,256]{1,0:T(8,128)(2,1)S(1)}, bf16[72,256]{1,0:T(8,128)(2,1)S(1)}, u32[]{:S(2)}, u32[]{:S(2)}) collective-permute-start(bf16[72,256]{1,0:T(8,128)(2,1)S(1)} %fusion.5), channel_id=1, source_target_pairs={{0,24},{2,26},{4,28},{6,30},{8,16},{10,18},{12,20},{14,22},{16,8},... | collective-permute-start | bytes 110600 | tf_op jit(solution)/shard_map/ppermute | solution.py:289
  77.0 5.2 %collective-permute-start.23 = (bf16[72,256]{1,0:T(8,128)(2,1)S(1)}, bf16[72,256]{1,0:T(8,128)(2,1)S(1)}, u32[]{:S(2)}, u32[]{:S(2)}) collective-permute-start(bf16[72,256]{1,0:T(8,128)(2,1)S(1)} %fusion.5), channel_id=1, source_target_pairs={{0,16},{2,18},{4,20},{6,22},{8,24},{10,26},{12,28},{14,30},{16,0},... | collective-permute-start | bytes 110600 | tf_op jit(solution)/shard_map/ppermute | solution.py:289
  77.9 4.4 %collective-permute-start.24 = (bf16[72,256]{1,0:T(8,128)(2,1)S(1)}, bf16[72,256]{1,0:T(8,128)(2,1)S(1)}, u32[]{:S(2)}, u32[]{:S(2)}) collective-permute-start(bf16[72,256]{1,0:T(8,128)(2,1)S(1)} %fusion.5), channel_id=1, source_target_pairs={{0,8},{2,10},{4,12},{6,14},{8,0},{10,2},{12,4},{14,6},{16,24},{18,... | collective-permute-start | bytes 110600 | tf_op jit(solution)/shard_map/ppermute | solution.py:289
  82.3 6.2 %collective-permute-start.25 = (bf16[288,256]{1,0:T(8,128)(2,1)S(1)}, bf16[288,256]{1,0:T(8,128)(2,1)S(1)}, u32[]{:S(2)}, u32[]{:S(2)}) collective-permute-start(bf16[288,256]{1,0:T(8,128)(2,1)S(1)} %bitcast.73), channel_id=1, source_target_pairs={{0,6},{2,4},{4,2},{6,0},{8,14},{10,12},{12,10},{14,8},{16,22},{18,... | collective-permute-start | bytes 442376 | tf_op jit(solution)/shard_map/ppermute | solution.py:289
  84.3 5.7 %collective-permute-start.26 = (bf16[288,256]{1,0:T(8,128)(2,1)S(1)}, bf16[288,256]{1,0:T(8,128)(2,1)S(1)}, u32[]{:S(2)}, u32[]{:S(2)}) collective-permute-start(bf16[288,256]{1,0:T(8,128)(2,1)S(1)} %bitcast.74), channel_id=1, source_target_pairs={{0,4},{2,6},{4,0},{6,2},{8,12},{10,14},{12,8},{14,10},{16,20},{18,... | collective-permute-start | bytes 442376 | tf_op jit(solution)/shard_map/ppermute | solution.py:289
  84.8 5.2 %collective-permute-start.27 = (bf16[288,256]{1,0:T(8,128)(2,1)S(1)}, bf16[288,256]{1,0:T(8,128)(2,1)S(1)}, u32[]{:S(2)}, u32[]{:S(2)}) collective-permute-start(bf16[288,256]{1,0:T(8,128)(2,1)S(1)} %bitcast.75), channel_id=1, source_target_pairs={{0,2},{2,0},{4,6},{6,4},{8,10},{10,8},{12,14},{14,12},{16,18},{18,... | collective-permute-start | bytes 442376 | tf_op jit(solution)/shard_map/ppermute | solution.py:289

commit v2 on v1

--- a/solution.py
+++ b/solution.py
@@ -13,7 +13,7 @@
 F32 = jnp.float32
 BF16 = jnp.bfloat16
 VMEM_LIMIT = 20 * 1024 * 1024
-EDGE_LIMIT = 62 * 1024 * 1024
+EDGE_LIMIT = 60 * 1024 * 1024
 
 
 def chunk_of(rows, most):
@@ -268,20 +268,30 @@
                 sent_ref[step - 1, tap] = part.astype(BF16)
 
 
-def input_level(three, w_ref, grad_ref, most):
-    rows, cols, chan = grad_ref.shape
+def input_level(three, turned, grad, grad_ref, sems, most):
+    rows, cols, chan = grad.shape
     pitch = three.shape[1]
-    rhs = jnp.concatenate([w_ref[tap] for tap in range(9)], 1)
-    for start, end in chunks_of(rows, most):
+    copies = []
+    for index, (start, end) in enumerate(chunks_of(rows, most)):
         size = end - start
         lhs = beside(three, (start + 2, start + 1, start), size)
-        grad = lax.dot_general(lhs, rhs, (((1,), (1,)), ((), ())), preferred_element_type=F32)
-        grad_ref[start:end] = grad.reshape(size, pitch, chan)[:, :cols].astype(BF16)
-
-
-def input_kernel(three_four, three_six, w_ref, grad_four_ref, grad_six_ref):
-    input_level(three_six, w_ref, grad_six_ref, 12)
-    input_level(three_four, w_ref, grad_four_ref, 16)
+        term = jnp.dot(lhs, turned[...], preferred_element_type=F32)
+        grad[start:end] = term.reshape(size, pitch, chan)[:, :cols].astype(BF16)
+        copies.append(pltpu.make_async_copy(grad.at[start:end], grad_ref.at[start:end], sems.at[index]))
+        copies[-1].start()
+    return copies
+
+
+def input_kernel(
+    three_four, three_six, w_ref, grad_four_ref, grad_six_ref, turned, grad_four, grad_six, sems_four, sems_six
+):
+    chan = w_ref.shape[1]
+    for tap in range(9):
+        turned[tap * chan : (tap + 1) * chan] = w_ref[tap].T
+    copies = input_level(three_six, turned, grad_six, grad_six_ref, sems_six, 12)
+    copies += input_level(three_four, turned, grad_four, grad_four_ref, sems_four, 8)
+    for copy in copies:
+        copy.wait()
 
 
 def swap(array, axis, stride):
@@ -348,17 +358,28 @@
     return above, below
 
 
-def group_sum(sums):
-    stride = 1
+def swap_odd(array, axis, stride):
+    count, sp_count = lax.axis_size("rep"), lax.axis_size("sp")
+    pairs = []
+    for rep in range(count):
+        for sp in range(1, sp_count, 2):
+            other = (rep ^ stride) * sp_count + sp if axis == "rep" else rep * sp_count + (sp ^ stride)
+            pairs.append((rep * sp_count + sp, other))
+    return lax.ppermute(array, ("rep", "sp"), pairs)
+
+
+def group_sum(sums, odd):
+    sums = sums + swap(sums, "sp", 1)
+    stride = 2
     while stride < lax.axis_size("sp"):
-        sums = sums + swap(sums, "sp", stride)
+        sums = sums + swap_odd(sums, "sp", stride)
         stride = 2 * stride
     stride = 1
     while stride < GROUP:
-        met = [swap(sums, "rep", k * stride) for k in range(1, RADIX)]
+        met = [swap_odd(sums, "rep", k * stride) for k in range(1, RADIX)]
         sums = (sums + met[0]) + (met[1] + met[2])
         stride = RADIX * stride
-    return sums
+    return jnp.where(odd, sums, swap(sums, "sp", 1))
 
 
 def every_group(sums):
@@ -374,7 +395,7 @@
     for shift in (0, 2):
         digit = (lax.axis_index("rep") >> shift) & (RADIX - 1)
         found.append(([digit ^ k for k in range(RADIX)], (digit & 1) == 1, digit >= 2))
-    return found
+    return found + [(lax.axis_index("sp") & 1) == 1]
 
 
 def digit_order(parts, place):
@@ -420,10 +441,14 @@
         met = [swap(total, "rep", k * stride) for k in range(1, RADIX)]
         total = added(total.astype(F32), met).astype(BF16)
         stride = RADIX * stride
-    for stride, place in ((RADIX, found[1]), (1, found[0])):
-        met = [total] + [swap(total, "rep", k * stride) for k in range(1, RADIX)]
-        total = digit_order(met, place).reshape(-1, chan)
-    return total.astype(F32)
+    met = [total] + [swap(total, "rep", k * RADIX) for k in range(1, RADIX)]
+    total = digit_order(met, found[1]).reshape(-1, chan)
+    met = [total] + [swap(total, "rep", k) for k in range(1, RADIX)]
+    whole = jnp.zeros((RADIX,) + total.shape, F32)
+    for k in range(RADIX):
+        start = (found[0][0][k], 0, 0)
+        whole = lax.dynamic_update_slice(whole, met[k][None].astype(F32), start, allow_negative_indices=False)
+    return whole
 
 
 def local(level_four, level_six, conv_weight, bn_gain, bn_shift, cotan_four, cotan_six):
@@ -440,6 +465,7 @@
     found, four = lax.optimization_barrier((places(), four))
     above, below = edges(four, six, cot_four, cot_six)
     vmem = pl.BlockSpec(memory_space=pltpu.VMEM)
+    hbm = pl.BlockSpec(memory_space=pltpu.HBM)
     params = pltpu.CompilerParams(vmem_limit_bytes=VMEM_LIMIT)
     framed_four = jax.ShapeDtypeStruct((rows_four + 2, pitch_four, chan), BF16)
     framed_six = jax.ShapeDtypeStruct((rows_six + 2, pitch_six, chan), BF16)
@@ -462,7 +488,7 @@
         cost_estimate=cost(1, 4 * four.size),
         name="forward",
     )(four, six, above, below, conv_weight)
-    moments = group_sum(moments)
+    moments = group_sum(moments, found[2])
 
     slope_four, slope_six, slopes = pl.pallas_call(
         functools.partial(slope_kernel, counts),
@@ -477,7 +503,7 @@
         cost_estimate=cost(0.01, 4 * four.size),
         name="slopes",
     )(conv_four, conv_six, cot_four, cot_six, above, below, moments, bn_gain, bn_shift)
-    slopes = group_sum(slopes)
+    slopes = group_sum(slopes, found[2])
 
     share = chan // sp_count
     wide_four, wide_six = (
@@ -509,7 +535,14 @@
             jax.ShapeDtypeStruct(six.shape, BF16),
         ),
         in_specs=[vmem] * 3,
-        out_specs=(vmem, vmem),
+        out_specs=(hbm, hbm),
+        scratch_shapes=[
+            pltpu.VMEM((9 * chan, chan), BF16),
+            pltpu.VMEM(four.shape, BF16),
+            pltpu.VMEM(six.shape, BF16),
+            pltpu.SemaphoreType.DMA((len(chunks_of(rows_four, 8)),)),
+            pltpu.SemaphoreType.DMA((len(chunks_of(rows_six, 12)),)),
+        ],
         compiler_params=params,
         cost_estimate=cost(1, 4 * four.size),
         name="inputs",

time: 91.5 us -> 107 us (1.17)
  starting transfers between devices: 32.6 us -> 61.7 us
  waiting for transfers between devices: 27.3 us -> 16.8 us
  Pallas kernels: 26.6 us -> 25.2 us
  other arithmetic: 2.17 us -> 0.97 us
    ppermute x28 -> x18, starting transfers between devices: 32.6 us -> 53.6 us  [swap(): return lax.ppermute(array, axis, [(i, i ^ stride) for i in range(count)])]
    ppermute x28 -> x18, waiting for transfers between devices: 27.3 us -> 16.8 us  [swap(): return lax.ppermute(array, axis, [(i, i ^ stride) for i in range(count)])]
    ppermute x0 -> x12, starting transfers between devices: none -> 8.1 us  [swap_odd(): return lax.ppermute(array, ('rep', 'sp'), pairs)]
    convert_element_type x1 -> x0, other arithmetic: 1.12 us -> none  [weight_finish(): return total.astype(F32)]
  transfers between devices with their start and end apart: 28 -> 30, of which waited for: 20 -> 13; matrix products, arithmetic and copies ran while one was open for 1% -> 1% of each run, Pallas kernels for 9% -> 7%
where the time goes in v2:
time: 107 us
  starting transfers between devices  61.7 us (58%)
  Pallas kernels  25.2 us (24%)
  waiting for transfers between devices  16.8 us (16%)
  local copies, waits for them, and re-layouts  1.16 us (1%)
  between operations  1.08 us (1%)
    ppermute x18, starting transfers between devices, swap(): return lax.ppermute(array, axis, [(i, i ^ stride) for i in range(count)])  53.6 us
    ppermute x18, waiting for transfers between devices, swap(): return lax.ppermute(array, axis, [(i, i ^ stride) for i in range(count)])  16.8 us
    ppermute x12, starting transfers between devices, swap_odd(): return lax.ppermute(array, ('rep', 'sp'), pairs)  8.1 us
    pallas_call x1, Pallas kernels, local(): pl.pallas_call(input_kernel, out_shape=(jax.ShapeDtypeStruct(four.shape,...  7.14 us
    pallas_call x1, Pallas kernels, local(): pl.pallas_call(functools.partial(backward_kernel, counts, sp_count), out_...  7.11 us
    pallas_call x1, Pallas kernels, local(): pl.pallas_call(functools.partial(forward_kernel, sp_count), out_shape=(fr...  6.43 us
    pallas_call x1, Pallas kernels, local(): pl.pallas_call(functools.partial(slope_kernel, counts), out_shape=(jax.Sh...  2.75 us
  transfers between devices with their start and end apart: 30, of which 13 were waited for; matrix products, arithmetic and copies ran while one was open for 1% of the time, Pallas kernels for 7%

profile of v2, /device:TPU:0, one launch (start us, length us, event | category | flops | bytes accessed | tf_op | source)
XLA Modules:
  0.0 106.9 jit_solution(13044008602512260634)
XLA Ops:
  0.7 1.7 %edges.1 = bf16[384,256]{1,0:T(8,128)(2,1)} custom-call(bf16[48,96,256]{2,1,0:T(8,128)(2,1)} %bitcast.57, bf16[12,24,256]{2,1,0:T(8,128)(2,1)} %bitcast.64, bf16[48,96,256]{2,1,0:T(8,128)(2,1)} %bitcast.55, bf16[12,24,256]{2,1,0:T(8,128)(2,1)} %bitcast.62), custom_call_target="tpu_custom_call" | custom-call | tf_op jit(solution)/shard_map/edges/pallas_call | solution.py:341
  2.4 0.0 copy-start.2
  2.4 0.0 copy-start.4
  2.4 0.0 copy-start.5
  2.5 0.5 collective-permute-start
  3.0 1.3 %collective-permute-done.above_ref.below_ref = bf16[384,256]{1,0:T(8,128)(2,1)S(1)} collective-permute-done((bf16[384,256]{1,0:T(8,128)(2,1)}, bf16[384,256]{1,0:T(8,128)(2,1)S(1)}, u32[]{:S(2)}, u32[]{:S(2)}) %collective-permute-start) | collective-permute-done | bytes 196640 | tf_op jit(solution)/shard_map/ppermute | solution.py:299
  4.3 6.4 %forward.1 = (bf16[50,96,256]{2,1,0:T(8,128)(2,1)S(1)}, bf16[14,32,256]{2,1,0:T(8,128)(2,1)S(1)}, f32[4,256]{1,0:T(4,128)S(1)}) custom-call(bf16[48,96,256]{2,1,0:T(8,128)(2,1)S(1)} %bitcast.58, bf16[12,24,256]{2,1,0:T(8,128)(2,1)S(1)} %bitcast.65, bf16[384,256]{1,0:T(8,128)(2,1)S(1)} %collective-permute-done.above_ref.below_ref, ...), custom_call_target="tpu_custom_call" | custom-call | flops 5775556608 | bytes 4718592 | tf_op jit(solution)/shard_map/forward/pallas_call | solution.py:478
  10.7 0.4 collective-permute-start.1
  11.2 0.8 collective-permute-done.1
  12.0 0.6 collective-permute-start.3
  12.6 0.7 collective-permute-start.4
  13.3 0.7 collective-permute-start.2
  14.0 0.0 collective-permute-done.3
  14.0 0.0 collective-permute-done.4
  14.0 0.7 collective-permute-start.6
  14.7 0.7 collective-permute-start.7
  15.4 0.7 collective-permute-start.5
  16.0 0.0 collective-permute-done.6
  16.1 0.0 collective-permute-done.5
  16.1 19.5 %collective-permute-start.8 = (f32[4,256]{1,0:T(4,128)S(1)}, f32[4,256]{1,0:T(4,128)S(1)}, u32[]{:S(2)}, u32[]{:S(2)}) collective-permute-start(f32[4,256]{1,0:T(4,128)S(1)} %add_add_fusion.2), channel_id=1, source_target_pairs={{0,1},{1,0},{2,3},{3,2},{4,5},{5,4},{6,7},{7,6},{8,9},{9,8},{10,11... | collective-permute-start | bytes 12296 | tf_op jit(solution)/shard_map/ppermute | solution.py:299
  35.6 0.8 collective-permute-done.8
  36.5 2.7 %slopes.1 = (f32[50,96,256]{2,1,0:T(8,128)S(1)}, f32[14,32,256]{2,1,0:T(8,128)S(1)}, f32[4,256]{1,0:T(4,128)S(1)}) custom-call(bf16[50,96,256]{2,1,0:T(8,128)(2,1)S(1)} %get-tuple-element.38.conv_four_ref, bf16[14,32,256]{2,1,0:T(8,128)(2,1)S(1)} %get-tuple-element.39.conv_six_ref, bf16[48,96,256]{2,1,0:T(8,128)(2,1)S(1)} %bitcast.56, ...), custom_call_target="tpu_custom_call" | custom-call | flops 57755568 | bytes 4718592 | tf_op jit(solution)/shard_map/slopes/pallas_call | solution.py:493
  39.2 0.4 collective-permute-start.9
  39.6 0.8 collective-permute-done.9
  40.5 0.6 collective-permute-start.11
  41.1 0.7 collective-permute-start.12
  41.8 0.7 collective-permute-start.10
  42.5 0.0 collective-permute-done.12
  42.5 0.0 collective-permute-done.10
  42.5 0.7 collective-permute-start.14
  43.2 0.7 collective-permute-start.15
  43.8 0.8 collective-permute-start.13
  44.7 0.0 collective-permute-done.14
  44.7 0.0 collective-permute-done.13
  44.7 16.2 %collective-permute-start.16 = (f32[4,256]{1,0:T(4,128)S(1)}, f32[4,256]{1,0:T(4,128)S(1)}, u32[]{:S(2)}, u32[]{:S(2)}) collective-permute-start(f32[4,256]{1,0:T(4,128)S(1)} %add_add_fusion), channel_id=1, source_target_pairs={{0,1},{1,0},{2,3},{3,2},{4,5},{5,4},{6,7},{7,6},{8,9},{9,8},{10,11... | collective-permute-start | bytes 12296 | tf_op jit(solution)/shard_map/ppermute | solution.py:299
  60.9 0.8 collective-permute-done.16
  61.7 7.1 %backward.1 = (bf16[50,96,768]{2,1,0:T(8,128)(2,1)S(1)}, bf16[14,32,768]{2,1,0:T(8,128)(2,1)S(1)}, f32[9,128,256]{2,1,0:T(8,128)S(1)}, bf16[1,9,128,256]{3,2,1,0:T(8,128)(2,1)S(1)}) custom-call(bf16[48,96,256]{2,1,0:T(8,128)(2,1)S(1)} %bitcast.59, bf16[12,24,256]{2,1,0:T(8,128)(2,1)S(1)} %bitcast.66, ...), custom_call_target="tpu_custom_call" | custom-call | flops 6930668032 | bytes 9437184 | tf_op jit(solution)/shard_map/backward/pallas_call | solution.py:512
  68.9 0.4 collective-permute-start.17
  69.3 1.6 %collective-permute-done.17 = bf16[9,128,256]{2,1,0:T(8,128)(2,1)S(1)} collective-permute-done((bf16[9,128,256]{2,1,0:T(8,128)(2,1)S(1)}, bf16[9,128,256]{2,1,0:T(8,128)(2,1)S(1)}, u32[]{:S(2)}, u32[]{:S(2)}) %collective-permute-start.17) | collective-permute-done | bytes 589856 | tf_op jit(solution)/shard_map/ppermute | solution.py:299
  70.9 0.1 fusion.3
  71.0 1.6 %collective-permute-start.18 = (bf16[288,256]{1,0:T(8,128)(2,1)S(1)}, bf16[288,256]{1,0:T(8,128)(2,1)S(1)}, u32[]{:S(2)}, u32[]{:S(2)}) collective-permute-start(bf16[288,256]{1,0:T(8,128)(2,1)S(1)} %get-tuple-element.54), channel_id=1, source_target_pairs={{0,2},{2,0},{4,6},{6,4},{8,10},{10,8},{12,14},{14,12},{16,18},{18,... | collective-permute-start | bytes 442376 | tf_op jit(solution)/shard_map/ppermute | solution.py:299
  72.6 1.5 %collective-permute-start.19 = (bf16[288,256]{1,0:T(8,128)(2,1)S(1)}, bf16[288,256]{1,0:T(8,128)(2,1)S(1)}, u32[]{:S(2)}, u32[]{:S(2)}) collective-permute-start(bf16[288,256]{1,0:T(8,128)(2,1)S(1)} %get-tuple-element.55), channel_id=1, source_target_pairs={{0,4},{2,6},{4,0},{6,2},{8,12},{10,14},{12,8},{14,10},{16,20},{18,... | collective-permute-start | bytes 442376 | tf_op jit(solution)/shard_map/ppermute | solution.py:299
  74.1 0.5 collective-permute-start.20
  74.6 7.1 %inputs.1 = (bf16[48,96,256]{2,1,0:T(8,128)(2,1)}, bf16[12,24,256]{2,1,0:T(8,128)(2,1)}) custom-call(bf16[50,96,768]{2,1,0:T(8,128)(2,1)S(1)} %get-tuple-element.51.three_four, bf16[14,32,768]{2,1,0:T(8,128)(2,1)S(1)} %get-tuple-element.52.three_six, bf16[9,256,256]{2,1,0:T(8,128)(2,1)S(1)} %copy-done.6), custom_call_target="tpu_custom_call" | custom-call | flops 5775556608 | bytes 4718592 | tf_op jit(solution)/shard_map/inputs/pallas_call | solution.py:531
  81.8 0.1 fusion
  81.9 2.7 %collective-permute-start.23 = (bf16[72,256]{1,0:T(8,128)(2,1)S(1)}, bf16[72,256]{1,0:T(8,128)(2,1)S(1)}, u32[]{:S(2)}, u32[]{:S(2)}) collective-permute-start(bf16[72,256]{1,0:T(8,128)(2,1)S(1)} %get-tuple-element.73), channel_id=1, source_target_pairs={{0,24},{2,26},{4,28},{6,30},{8,16},{10,18},{12,20},{14,22},{16,8},... | collective-permute-start | bytes 110600 | tf_op jit(solution)/shard_map/ppermute | solution.py:299
  84.6 1.7 %collective-permute-start.21 = (bf16[72,256]{1,0:T(8,128)(2,1)S(1)}, bf16[72,256]{1,0:T(8,128)(2,1)S(1)}, u32[]{:S(2)}, u32[]{:S(2)}) collective-permute-start(bf16[72,256]{1,0:T(8,128)(2,1)S(1)} %get-tuple-element.72), channel_id=1, source_target_pairs={{0,8},{2,10},{4,12},{6,14},{8,0},{10,2},{12,4},{14,6},{16,24},{18,... | collective-permute-start | bytes 110600 | tf_op jit(solution)/shard_map/ppermute | solution.py:299
  86.4 1.4 %collective-permute-done.23 = bf16[72,256]{1,0:T(8,128)(2,1)S(1)} collective-permute-done((bf16[72,256]{1,0:T(8,128)(2,1)S(1)}, bf16[72,256]{1,0:T(8,128)(2,1)S(1)}, u32[]{:S(2)}, u32[]{:S(2)}) %collective-permute-start.23) | collective-permute-done | bytes 36896 | tf_op jit(solution)/shard_map/ppermute | solution.py:299
  87.8 1.7 %collective-permute-done.22 = bf16[72,256]{1,0:T(8,128)(2,1)S(1)} collective-permute-done((bf16[72,256]{1,0:T(8,128)(2,1)S(1)}, bf16[72,256]{1,0:T(8,128)(2,1)S(1)}, u32[]{:S(2)}, u32[]{:S(2)}) %collective-permute-start.22) | collective-permute-done | bytes 36896 | tf_op jit(solution)/shard_map/ppermute | solution.py:299
  89.5 1.9 %collective-permute-start.24 = (bf16[72,256]{1,0:T(8,128)(2,1)S(1)}, bf16[72,256]{1,0:T(8,128)(2,1)S(1)}, u32[]{:S(2)}, u32[]{:S(2)}) collective-permute-start(bf16[72,256]{1,0:T(8,128)(2,1)S(1)} %fusion.5), channel_id=1, source_target_pairs={{0,24},{2,26},{4,28},{6,30},{8,16},{10,18},{12,20},{14,22},{16,8},... | collective-permute-start | bytes 110600 | tf_op jit(solution)/shard_map/ppermute | solution.py:299
  91.4 0.5 collective-permute-start.25
  91.9 2.1 %collective-permute-start.26 = (bf16[72,256]{1,0:T(8,128)(2,1)S(1)}, bf16[72,256]{1,0:T(8,128)(2,1)S(1)}, u32[]{:S(2)}, u32[]{:S(2)}) collective-permute-start(bf16[72,256]{1,0:T(8,128)(2,1)S(1)} %fusion.5), channel_id=1, source_target_pairs={{0,8},{2,10},{4,12},{6,14},{8,0},{10,2},{12,4},{14,6},{16,24},{18,... | collective-permute-start | bytes 110600 | tf_op jit(solution)/shard_map/ppermute | solution.py:299
  94.0 0.6 pad_maximum_fusion.1
  94.5 0.8 collective-permute-done.24
  95.3 1.3 %collective-permute-done.25 = bf16[72,256]{1,0:T(8,128)(2,1)S(1)} collective-permute-done((bf16[72,256]{1,0:T(8,128)(2,1)S(1)}, bf16[72,256]{1,0:T(8,128)(2,1)S(1)}, u32[]{:S(2)}, u32[]{:S(2)}) %collective-permute-start.25) | collective-permute-done | bytes 36896 | tf_op jit(solution)/shard_map/ppermute | solution.py:299
  96.7 1.6 %collective-permute-start.27 = (bf16[288,256]{1,0:T(8,128)(2,1)S(1)}, bf16[288,256]{1,0:T(8,128)(2,1)S(1)}, u32[]{:S(2)}, u32[]{:S(2)}) collective-permute-start(bf16[288,256]{1,0:T(8,128)(2,1)S(1)} %bitcast.73), channel_id=1, source_target_pairs={{0,2},{2,0},{4,6},{6,4},{8,10},{10,8},{12,14},{14,12},{16,18},{18,... | collective-permute-start | bytes 442376 | tf_op jit(solution)/shard_map/ppermute | solution.py:299
  98.3 1.5 %collective-permute-start.28 = (bf16[288,256]{1,0:T(8,128)(2,1)S(1)}, bf16[288,256]{1,0:T(8,128)(2,1)S(1)}, u32[]{:S(2)}, u32[]{:S(2)}) collective-permute-start(bf16[288,256]{1,0:T(8,128)(2,1)S(1)} %bitcast.74), channel_id=1, source_target_pairs={{0,4},{2,6},{4,0},{6,2},{8,12},{10,14},{12,8},{14,10},{16,20},{18,... | collective-permute-start | bytes 442376 | tf_op jit(solution)/shard_map/ppermute | solution.py:299
  99.8 0.5 collective-permute-start.29
  100.3 0.1 broadcast_in_dim.14
  100.4 1.9 %collective-permute-done.27 = bf16[288,256]{1,0:T(8,128)(2,1)S(1)} collective-permute-done((bf16[288,256]{1,0:T(8,128)(2,1)S(1)}, bf16[288,256]{1,0:T(8,128)(2,1)S(1)}, u32[]{:S(2)}, u32[]{:S(2)}) %collective-permute-start.27) | collective-permute-done | bytes 147488 | tf_op jit(solution)/shard_map/ppermute | solution.py:299
  102.4 1.1 %collective-permute-done.28 = bf16[288,256]{1,0:T(8,128)(2,1)S(1)} collective-permute-done((bf16[288,256]{1,0:T(8,128)(2,1)S(1)}, bf16[288,256]{1,0:T(8,128)(2,1)S(1)}, u32[]{:S(2)}, u32[]{:S(2)}) %collective-permute-start.28) | collective-permute-done | bytes 147488 | tf_op jit(solution)/shard_map/ppermute | solution.py:299
  103.5 2.3 %collective-permute-done.29 = bf16[288,256]{1,0:T(8,128)(2,1)S(1)} collective-permute-done((bf16[288,256]{1,0:T(8,128)(2,1)S(1)}, bf16[288,256]{1,0:T(8,128)(2,1)S(1)}, u32[]{:S(2)}, u32[]{:S(2)}) %collective-permute-start.29) | collective-permute-done | bytes 147488 | tf_op jit(solution)/shard_map/ppermute | solution.py:299
  105.9 0.0 copy-start.7
  105.9 1.0 copy-done.7
  (38 shorter events, 0.3 us)
Async XLA Ops:
  0.6 3.6 %copy-start.1 = (bf16[1,48,96,256]{3,2,1,0:T(8,128)(2,1)S(1)}, bf16[1,48,96,256]{3,2,1,0:T(8,128)(2,1)}, u32[]{:S(2)}) copy-start(bf16[1,48,96,256]{3,2,1,0:T(8,128)(2,1)} %param.7) | copy-start | bytes 7077892
  0.7 3.6 %copy-start.3 = (bf16[1,12,24,256]{3,2,1,0:T(8,128)(2,1)S(1)}, bf16[1,12,24,256]{3,2,1,0:T(8,128)(2,1)}, u32[]{:S(2)}) copy-start(bf16[1,12,24,256]{3,2,1,0:T(8,128)(2,1)} %param.8) | copy-start | bytes 442372
  0.7 3.6 %copy-start.6 = (bf16[9,256,256]{2,1,0:T(8,128)(2,1)S(1)}, bf16[9,256,256]{2,1,0:T(8,128)(2,1)}, u32[]{:S(2)}) copy-start(bf16[9,256,256]{2,1,0:T(8,128)(2,1)} %w_ref.3) | copy-start | bytes 3538948
  2.4 34.0 %copy-start.2 = (bf16[1,12,24,256]{3,2,1,0:T(8,128)(2,1)S(1)}, bf16[1,12,24,256]{3,2,1,0:T(8,128)(2,1)}, u32[]{:S(2)}) copy-start(bf16[1,12,24,256]{3,2,1,0:T(8,128)(2,1)} %param.13) | copy-start | bytes 442372
  2.4 34.0 %copy-start.4 = (f32[2,256]{1,0:T(2,128)S(1)}, f32[2,256]{1,0:T(2,128)}, u32[]{:S(2)}) copy-start(f32[2,256]{1,0:T(2,128)} %gain_ref.3) | copy-start | bytes 6148
  2.4 34.0 %copy-start.5 = (f32[2,256]{1,0:T(2,128)S(1)}, f32[2,256]{1,0:T(2,128)}, u32[]{:S(2)}) copy-start(f32[2,256]{1,0:T(2,128)} %shift_ref.3) | copy-start | bytes 6148
  2.5 1.8 %collective-permute-start = (bf16[384,256]{1,0:T(8,128)(2,1)}, bf16[384,256]{1,0:T(8,128)(2,1)S(1)}, u32[]{:S(2)}, u32[]{:S(2)}) collective-permute-start(bf16[384,256]{1,0:T(8,128)(2,1)} %edges.1), channel_id=1, source_target_pairs={{0,1},{1,0},{2,3},{3,2},{4,5},{5,4},{6,7},{7,6},{8,9},{9,8},{10,11... | collective-permute-start | bytes 589832 | tf_op jit(solution)/shard_map/ppermute | solution.py:299
  4.3 32.2 %copy-start = (bf16[1,48,96,256]{3,2,1,0:T(8,128)(2,1)S(1)}, bf16[1,48,96,256]{3,2,1,0:T(8,128)(2,1)}, u32[]{:S(2)}) copy-start(bf16[1,48,96,256]{3,2,1,0:T(8,128)(2,1)} %param.12) | copy-start | bytes 7077892
  10.7 1.3 %collective-permute-start.1 = (f32[4,256]{1,0:T(4,128)S(1)}, f32[4,256]{1,0:T(4,128)S(1)}, u32[]{:S(2)}, u32[]{:S(2)}) collective-permute-start(f32[4,256]{1,0:T(4,128)S(1)} %get-tuple-element.41), channel_id=1, source_target_pairs={{0,1},{1,0},{2,3},{3,2},{4,5},{5,4},{6,7},{7,6},{8,9},{9,8},{10,11... | collective-permute-start | bytes 12296 | tf_op jit(solution)/shard_map/ppermute | solution.py:299
  12.0 2.0 %collective-permute-start.3 = (f32[4,256]{1,0:T(4,128)S(1)}, f32[4,256]{1,0:T(4,128)S(1)}, u32[]{:S(2)}, u32[]{:S(2)}) collective-permute-start(f32[4,256]{1,0:T(4,128)S(1)} %add.78), channel_id=1, source_target_pairs={{1,5},{3,7},{5,1},{7,3},{9,13},{11,15},{13,9},{15,11},{17,21},{19,... | collective-permute-start | bytes 12296 | tf_op jit(solution)/shard_map/ppermute | solution.py:368
  12.6 1.4 %collective-permute-start.4 = (f32[4,256]{1,0:T(4,128)S(1)}, f32[4,256]{1,0:T(4,128)S(1)}, u32[]{:S(2)}, u32[]{:S(2)}) collective-permute-start(f32[4,256]{1,0:T(4,128)S(1)} %add.78), channel_id=1, source_target_pairs={{1,7},{3,5},{5,3},{7,1},{9,15},{11,13},{13,11},{15,9},{17,23},{19,... | collective-permute-start | bytes 12296 | tf_op jit(solution)/shard_map/ppermute | solution.py:368
  13.3 0.7 collective-permute-start.2
  14.0 2.0 %collective-permute-start.6 = (f32[4,256]{1,0:T(4,128)S(1)}, f32[4,256]{1,0:T(4,128)S(1)}, u32[]{:S(2)}, u32[]{:S(2)}) collective-permute-start(f32[4,256]{1,0:T(4,128)S(1)} %add_add_fusion.3), channel_id=1, source_target_pairs={{1,17},{3,19},{5,21},{7,23},{9,25},{11,27},{13,29},{15,31},{17,1},... | collective-permute-start | bytes 12296 | tf_op jit(solution)/shard_map/ppermute | solution.py:368
  14.7 1.4 %collective-permute-start.7 = (f32[4,256]{1,0:T(4,128)S(1)}, f32[4,256]{1,0:T(4,128)S(1)}, u32[]{:S(2)}, u32[]{:S(2)}) collective-permute-start(f32[4,256]{1,0:T(4,128)S(1)} %add_add_fusion.3), channel_id=1, source_target_pairs={{1,25},{3,27},{5,29},{7,31},{9,17},{11,19},{13,21},{15,23},{17,9},... | collective-permute-start | bytes 12296 | tf_op jit(solution)/shard_map/ppermute | solution.py:368
  15.4 0.7 collective-permute-start.5
  16.1 20.4 %collective-permute-start.8 = (f32[4,256]{1,0:T(4,128)S(1)}, f32[4,256]{1,0:T(4,128)S(1)}, u32[]{:S(2)}, u32[]{:S(2)}) collective-permute-start(f32[4,256]{1,0:T(4,128)S(1)} %add_add_fusion.2), channel_id=1, source_target_pairs={{0,1},{1,0},{2,3},{3,2},{4,5},{5,4},{6,7},{7,6},{8,9},{9,8},{10,11... | collective-permute-start | bytes 12296 | tf_op jit(solution)/shard_map/ppermute | solution.py:299
  39.2 1.2 %collective-permute-start.9 = (f32[4,256]{1,0:T(4,128)S(1)}, f32[4,256]{1,0:T(4,128)S(1)}, u32[]{:S(2)}, u32[]{:S(2)}) collective-permute-start(f32[4,256]{1,0:T(4,128)S(1)} %get-tuple-element.44), channel_id=1, source_target_pairs={{0,1},{1,0},{2,3},{3,2},{4,5},{5,4},{6,7},{7,6},{8,9},{9,8},{10,11... | collective-permute-start | bytes 12296 | tf_op jit(solution)/shard_map/ppermute | solution.py:299
  40.5 2.0 %collective-permute-start.11 = (f32[4,256]{1,0:T(4,128)S(1)}, f32[4,256]{1,0:T(4,128)S(1)}, u32[]{:S(2)}, u32[]{:S(2)}) collective-permute-start(f32[4,256]{1,0:T(4,128)S(1)} %add.85), channel_id=1, source_target_pairs={{1,5},{3,7},{5,1},{7,3},{9,13},{11,15},{13,9},{15,11},{17,21},{19,... | collective-permute-start | bytes 12296 | tf_op jit(solution)/shard_map/ppermute | solution.py:368
  41.1 1.4 %collective-permute-start.12 = (f32[4,256]{1,0:T(4,128)S(1)}, f32[4,256]{1,0:T(4,128)S(1)}, u32[]{:S(2)}, u32[]{:S(2)}) collective-permute-start(f32[4,256]{1,0:T(4,128)S(1)} %add.85), channel_id=1, source_target_pairs={{1,7},{3,5},{5,3},{7,1},{9,15},{11,13},{13,11},{15,9},{17,23},{19,... | collective-permute-start | bytes 12296 | tf_op jit(solution)/shard_map/ppermute | solution.py:368
  41.8 0.7 collective-permute-start.10
  42.5 2.2 %collective-permute-start.14 = (f32[4,256]{1,0:T(4,128)S(1)}, f32[4,256]{1,0:T(4,128)S(1)}, u32[]{:S(2)}, u32[]{:S(2)}) collective-permute-start(f32[4,256]{1,0:T(4,128)S(1)} %add_add_fusion.1), channel_id=1, source_target_pairs={{1,17},{3,19},{5,21},{7,23},{9,25},{11,27},{13,29},{15,31},{17,1},... | collective-permute-start | bytes 12296 | tf_op jit(solution)/shard_map/ppermute | solution.py:368
  43.2 1.5 %collective-permute-start.15 = (f32[4,256]{1,0:T(4,128)S(1)}, f32[4,256]{1,0:T(4,128)S(1)}, u32[]{:S(2)}, u32[]{:S(2)}) collective-permute-start(f32[4,256]{1,0:T(4,128)S(1)} %add_add_fusion.1), channel_id=1, source_target_pairs={{1,25},{3,27},{5,29},{7,31},{9,17},{11,19},{13,21},{15,23},{17,9},... | collective-permute-start | bytes 12296 | tf_op jit(solution)/shard_map/ppermute | solution.py:368
  43.8 0.9 collective-permute-start.13
  44.7 17.0 %collective-permute-start.16 = (f32[4,256]{1,0:T(4,128)S(1)}, f32[4,256]{1,0:T(4,128)S(1)}, u32[]{:S(2)}, u32[]{:S(2)}) collective-permute-start(f32[4,256]{1,0:T(4,128)S(1)} %add_add_fusion), channel_id=1, source_target_pairs={{0,1},{1,0},{2,3},{3,2},{4,5},{5,4},{6,7},{7,6},{8,9},{9,8},{10,11... | collective-permute-start | bytes 12296 | tf_op jit(solution)/shard_map/ppermute | solution.py:299
  68.9 2.1 %collective-permute-start.17 = (bf16[9,128,256]{2,1,0:T(8,128)(2,1)S(1)}, bf16[9,128,256]{2,1,0:T(8,128)(2,1)S(1)}, u32[]{:S(2)}, u32[]{:S(2)}) collective-permute-start(bf16[9,128,256]{2,1,0:T(8,128)(2,1)S(1)} %bitcast.67), channel_id=1, source_target_pairs={{0,1},{1,0},{2,3},{3,2},{4,5},{5,4},{6,7},{7,6},{8,9},{9,8},{10,11... | collective-permute-start | bytes 1769480 | tf_op jit(solution)/shard_map/ppermute | solution.py:299
  71.0 10.7 %collective-permute-start.18 = (bf16[288,256]{1,0:T(8,128)(2,1)S(1)}, bf16[288,256]{1,0:T(8,128)(2,1)S(1)}, u32[]{:S(2)}, u32[]{:S(2)}) collective-permute-start(bf16[288,256]{1,0:T(8,128)(2,1)S(1)} %get-tuple-element.54), channel_id=1, source_target_pairs={{0,2},{2,0},{4,6},{6,4},{8,10},{10,8},{12,14},{14,12},{16,18},{18,... | collective-permute-start | bytes 442376 | tf_op jit(solution)/shard_map/ppermute | solution.py:299
  72.6 9.2 %collective-permute-start.19 = (bf16[288,256]{1,0:T(8,128)(2,1)S(1)}, bf16[288,256]{1,0:T(8,128)(2,1)S(1)}, u32[]{:S(2)}, u32[]{:S(2)}) collective-permute-start(bf16[288,256]{1,0:T(8,128)(2,1)S(1)} %get-tuple-element.55), channel_id=1, source_target_pairs={{0,4},{2,6},{4,0},{6,2},{8,12},{10,14},{12,8},{14,10},{16,20},{18,... | collective-permute-start | bytes 442376 | tf_op jit(solution)/shard_map/ppermute | solution.py:299
  74.1 7.7 %collective-permute-start.20 = (bf16[288,256]{1,0:T(8,128)(2,1)S(1)}, bf16[288,256]{1,0:T(8,128)(2,1)S(1)}, u32[]{:S(2)}, u32[]{:S(2)}) collective-permute-start(bf16[288,256]{1,0:T(8,128)(2,1)S(1)} %get-tuple-element.56), channel_id=1, source_target_pairs={{0,6},{2,4},{4,2},{6,0},{8,14},{10,12},{12,10},{14,8},{16,22},{18,... | collective-permute-start | bytes 442376 | tf_op jit(solution)/shard_map/ppermute | solution.py:299
  81.9 5.9 %collective-permute-start.23 = (bf16[72,256]{1,0:T(8,128)(2,1)S(1)}, bf16[72,256]{1,0:T(8,128)(2,1)S(1)}, u32[]{:S(2)}, u32[]{:S(2)}) collective-permute-start(bf16[72,256]{1,0:T(8,128)(2,1)S(1)} %get-tuple-element.73), channel_id=1, source_target_pairs={{0,24},{2,26},{4,28},{6,30},{8,16},{10,18},{12,20},{14,22},{16,8},... | collective-permute-start | bytes 110600 | tf_op jit(solution)/shard_map/ppermute | solution.py:299
  84.6 4.9 %collective-permute-start.22 = (bf16[72,256]{1,0:T(8,128)(2,1)S(1)}, bf16[72,256]{1,0:T(8,128)(2,1)S(1)}, u32[]{:S(2)}, u32[]{:S(2)}) collective-permute-start(bf16[72,256]{1,0:T(8,128)(2,1)S(1)} %get-tuple-element.74), channel_id=1, source_target_pairs={{0,16},{2,18},{4,20},{6,22},{8,24},{10,26},{12,28},{14,30},{16,0},... | collective-permute-start | bytes 110600 | tf_op jit(solution)/shard_map/ppermute | solution.py:299
  84.6 4.9 %collective-permute-start.21 = (bf16[72,256]{1,0:T(8,128)(2,1)S(1)}, bf16[72,256]{1,0:T(8,128)(2,1)S(1)}, u32[]{:S(2)}, u32[]{:S(2)}) collective-permute-start(bf16[72,256]{1,0:T(8,128)(2,1)S(1)} %get-tuple-element.72), channel_id=1, source_target_pairs={{0,8},{2,10},{4,12},{6,14},{8,0},{10,2},{12,4},{14,6},{16,24},{18,... | collective-permute-start | bytes 110600 | tf_op jit(solution)/shard_map/ppermute | solution.py:299
  89.5 5.8 %collective-permute-start.24 = (bf16[72,256]{1,0:T(8,128)(2,1)S(1)}, bf16[72,256]{1,0:T(8,128)(2,1)S(1)}, u32[]{:S(2)}, u32[]{:S(2)}) collective-permute-start(bf16[72,256]{1,0:T(8,128)(2,1)S(1)} %fusion.5), channel_id=1, source_target_pairs={{0,24},{2,26},{4,28},{6,30},{8,16},{10,18},{12,20},{14,22},{16,8},... | collective-permute-start | bytes 110600 | tf_op jit(solution)/shard_map/ppermute | solution.py:299
  91.4 5.3 %collective-permute-start.25 = (bf16[72,256]{1,0:T(8,128)(2,1)S(1)}, bf16[72,256]{1,0:T(8,128)(2,1)S(1)}, u32[]{:S(2)}, u32[]{:S(2)}) collective-permute-start(bf16[72,256]{1,0:T(8,128)(2,1)S(1)} %fusion.5), channel_id=1, source_target_pairs={{0,16},{2,18},{4,20},{6,22},{8,24},{10,26},{12,28},{14,30},{16,0},... | collective-permute-start | bytes 110600 | tf_op jit(solution)/shard_map/ppermute | solution.py:299
  91.9 4.8 %collective-permute-start.26 = (bf16[72,256]{1,0:T(8,128)(2,1)S(1)}, bf16[72,256]{1,0:T(8,128)(2,1)S(1)}, u32[]{:S(2)}, u32[]{:S(2)}) collective-permute-start(bf16[72,256]{1,0:T(8,128)(2,1)S(1)} %fusion.5), channel_id=1, source_target_pairs={{0,8},{2,10},{4,12},{6,14},{8,0},{10,2},{12,4},{14,6},{16,24},{18,... | collective-permute-start | bytes 110600 | tf_op jit(solution)/shard_map/ppermute | solution.py:299
  96.7 5.6 %collective-permute-start.27 = (bf16[288,256]{1,0:T(8,128)(2,1)S(1)}, bf16[288,256]{1,0:T(8,128)(2,1)S(1)}, u32[]{:S(2)}, u32[]{:S(2)}) collective-permute-start(bf16[288,256]{1,0:T(8,128)(2,1)S(1)} %bitcast.73), channel_id=1, source_target_pairs={{0,2},{2,0},{4,6},{6,4},{8,10},{10,8},{12,14},{14,12},{16,18},{18,... | collective-permute-start | bytes 442376 | tf_op jit(solution)/shard_map/ppermute | solution.py:299
  98.3 5.2 %collective-permute-start.28 = (bf16[288,256]{1,0:T(8,128)(2,1)S(1)}, bf16[288,256]{1,0:T(8,128)(2,1)S(1)}, u32[]{:S(2)}, u32[]{:S(2)}) collective-permute-start(bf16[288,256]{1,0:T(8,128)(2,1)S(1)} %bitcast.74), channel_id=1, source_target_pairs={{0,4},{2,6},{4,0},{6,2},{8,12},{10,14},{12,8},{14,10},{16,20},{18,... | collective-permute-start | bytes 442376 | tf_op jit(solution)/shard_map/ppermute | solution.py:299
  99.8 6.0 %collective-permute-start.29 = (bf16[288,256]{1,0:T(8,128)(2,1)S(1)}, bf16[288,256]{1,0:T(8,128)(2,1)S(1)}, u32[]{:S(2)}, u32[]{:S(2)}) collective-permute-start(bf16[288,256]{1,0:T(8,128)(2,1)S(1)} %bitcast.75), channel_id=1, source_target_pairs={{0,6},{2,4},{4,2},{6,0},{8,14},{10,12},{12,10},{14,8},{16,22},{18,... | collective-permute-start | bytes 442376 | tf_op jit(solution)/shard_map/ppermute | solution.py:299
  105.9 1.0 copy-start.7

commit v3 on v2

--- a/solution.py
+++ b/solution.py
@@ -362,8 +362,10 @@
     count, sp_count = lax.axis_size("rep"), lax.axis_size("sp")
     pairs = []
     for rep in range(count):
-        for sp in range(1, sp_count, 2):
-            other = (rep ^ stride) * sp_count + sp if axis == "rep" else rep * sp_count + (sp ^ stride)
+        for sp in range(sp_count):
+            other = rep * sp_count + sp
+            if sp % 2 == 1:
+                other = (rep ^ stride) * sp_count + sp if axis == "rep" else rep * sp_count + (sp ^ stride)
             pairs.append((rep * sp_count + sp, other))
     return lax.ppermute(array, ("rep", "sp"), pairs)
 

time: 107 us -> 107 us (level)
  no operation moved by 1% of the time
where the time goes in v3:
time: 107 us
  starting transfers between devices  61.7 us (58%)
  Pallas kernels  25.2 us (24%)
  waiting for transfers between devices  16.8 us (16%)
  local copies, waits for them, and re-layouts  1.16 us (1%)
  between operations  1.08 us (1%)
    ppermute x18, starting transfers between devices, swap(): return lax.ppermute(array, axis, [(i, i ^ stride) for i in range(count)])  53.6 us
    ppermute x18, waiting for transfers between devices, swap(): return lax.ppermute(array, axis, [(i, i ^ stride) for i in range(count)])  16.8 us
    ppermute x12, starting transfers between devices, swap_odd(): return lax.ppermute(array, ('rep', 'sp'), pairs)  8.1 us
    pallas_call x1, Pallas kernels, local(): pl.pallas_call(input_kernel, out_shape=(jax.ShapeDtypeStruct(four.shape,...  7.14 us
    pallas_call x1, Pallas kernels, local(): pl.pallas_call(functools.partial(backward_kernel, counts, sp_count), out_...  7.11 us
    pallas_call x1, Pallas kernels, local(): pl.pallas_call(functools.partial(forward_kernel, sp_count), out_shape=(fr...  6.43 us
    pallas_call x1, Pallas kernels, local(): pl.pallas_call(functools.partial(slope_kernel, counts), out_shape=(jax.Sh...  2.75 us
  transfers between devices with their start and end apart: 30, of which 13 were waited for; matrix products, arithmetic and copies ran while one was open for 1% of the time, Pallas kernels for 7%

profile of v3, /device:TPU:0, one launch (start us, length us, event | category | flops | bytes accessed | tf_op | source)
XLA Modules:
  0.0 106.9 jit_solution(11219047509575404882)
XLA Ops:
  0.7 1.7 %edges.1 = bf16[384,256]{1,0:T(8,128)(2,1)} custom-call(bf16[48,96,256]{2,1,0:T(8,128)(2,1)} %bitcast.57, bf16[12,24,256]{2,1,0:T(8,128)(2,1)} %bitcast.64, bf16[48,96,256]{2,1,0:T(8,128)(2,1)} %bitcast.55, bf16[12,24,256]{2,1,0:T(8,128)(2,1)} %bitcast.62), custom_call_target="tpu_custom_call" | custom-call | tf_op jit(solution)/shard_map/edges/pallas_call | solution.py:341
  2.4 0.0 copy-start.2
  2.4 0.0 copy-start.4
  2.4 0.0 copy-start.5
  2.5 0.5 collective-permute-start
  3.0 1.3 %collective-permute-done.above_ref.below_ref = bf16[384,256]{1,0:T(8,128)(2,1)S(1)} collective-permute-done((bf16[384,256]{1,0:T(8,128)(2,1)}, bf16[384,256]{1,0:T(8,128)(2,1)S(1)}, u32[]{:S(2)}, u32[]{:S(2)}) %collective-permute-start) | collective-permute-done | bytes 196640 | tf_op jit(solution)/shard_map/ppermute | solution.py:299
  4.3 6.4 %forward.1 = (bf16[50,96,256]{2,1,0:T(8,128)(2,1)S(1)}, bf16[14,32,256]{2,1,0:T(8,128)(2,1)S(1)}, f32[4,256]{1,0:T(4,128)S(1)}) custom-call(bf16[48,96,256]{2,1,0:T(8,128)(2,1)S(1)} %bitcast.58, bf16[12,24,256]{2,1,0:T(8,128)(2,1)S(1)} %bitcast.65, bf16[384,256]{1,0:T(8,128)(2,1)S(1)} %collective-permute-done.above_ref.below_ref, ...), custom_call_target="tpu_custom_call" | custom-call | flops 5775556608 | bytes 4718592 | tf_op jit(solution)/shard_map/forward/pallas_call | solution.py:480
  10.7 0.4 collective-permute-start.1
  11.2 0.8 collective-permute-done.1
  12.0 0.6 collective-permute-start.3
  12.6 0.7 collective-permute-start.4
  13.3 0.7 collective-permute-start.2
  14.0 0.0 collective-permute-done.3
  14.0 0.0 collective-permute-done.4
  14.0 0.7 collective-permute-start.6
  14.7 0.7 collective-permute-start.7
  15.4 0.7 collective-permute-start.5
  16.0 0.0 collective-permute-done.6
  16.1 0.0 collective-permute-done.5
  16.1 19.5 %collective-permute-start.8 = (f32[4,256]{1,0:T(4,128)S(1)}, f32[4,256]{1,0:T(4,128)S(1)}, u32[]{:S(2)}, u32[]{:S(2)}) collective-permute-start(f32[4,256]{1,0:T(4,128)S(1)} %add_add_fusion.2), channel_id=1, source_target_pairs={{0,1},{1,0},{2,3},{3,2},{4,5},{5,4},{6,7},{7,6},{8,9},{9,8},{10,11... | collective-permute-start | bytes 12296 | tf_op jit(solution)/shard_map/ppermute | solution.py:299
  35.6 0.8 collective-permute-done.8
  36.5 2.7 %slopes.1 = (f32[50,96,256]{2,1,0:T(8,128)S(1)}, f32[14,32,256]{2,1,0:T(8,128)S(1)}, f32[4,256]{1,0:T(4,128)S(1)}) custom-call(bf16[50,96,256]{2,1,0:T(8,128)(2,1)S(1)} %get-tuple-element.38.conv_four_ref, bf16[14,32,256]{2,1,0:T(8,128)(2,1)S(1)} %get-tuple-element.39.conv_six_ref, bf16[48,96,256]{2,1,0:T(8,128)(2,1)S(1)} %bitcast.56, ...), custom_call_target="tpu_custom_call" | custom-call | flops 57755568 | bytes 4718592 | tf_op jit(solution)/shard_map/slopes/pallas_call | solution.py:495
  39.2 0.4 collective-permute-start.9
  39.6 0.8 collective-permute-done.9
  40.5 0.6 collective-permute-start.11
  41.1 0.7 collective-permute-start.12
  41.8 0.7 collective-permute-start.10
  42.5 0.0 collective-permute-done.12
  42.5 0.0 collective-permute-done.10
  42.5 0.7 collective-permute-start.14
  43.2 0.7 collective-permute-start.15
  43.8 0.8 collective-permute-start.13
  44.7 0.0 collective-permute-done.14
  44.7 0.0 collective-permute-done.13
  44.7 16.2 %collective-permute-start.16 = (f32[4,256]{1,0:T(4,128)S(1)}, f32[4,256]{1,0:T(4,128)S(1)}, u32[]{:S(2)}, u32[]{:S(2)}) collective-permute-start(f32[4,256]{1,0:T(4,128)S(1)} %add_add_fusion), channel_id=1, source_target_pairs={{0,1},{1,0},{2,3},{3,2},{4,5},{5,4},{6,7},{7,6},{8,9},{9,8},{10,11... | collective-permute-start | bytes 12296 | tf_op jit(solution)/shard_map/ppermute | solution.py:299
  60.9 0.8 collective-permute-done.16
  61.7 7.1 %backward.1 = (bf16[50,96,768]{2,1,0:T(8,128)(2,1)S(1)}, bf16[14,32,768]{2,1,0:T(8,128)(2,1)S(1)}, f32[9,128,256]{2,1,0:T(8,128)S(1)}, bf16[1,9,128,256]{3,2,1,0:T(8,128)(2,1)S(1)}) custom-call(bf16[48,96,256]{2,1,0:T(8,128)(2,1)S(1)} %bitcast.59, bf16[12,24,256]{2,1,0:T(8,128)(2,1)S(1)} %bitcast.66, ...), custom_call_target="tpu_custom_call" | custom-call | flops 6930668032 | bytes 9437184 | tf_op jit(solution)/shard_map/backward/pallas_call | solution.py:514
  68.9 0.4 collective-permute-start.17
  69.3 1.6 %collective-permute-done.17 = bf16[9,128,256]{2,1,0:T(8,128)(2,1)S(1)} collective-permute-done((bf16[9,128,256]{2,1,0:T(8,128)(2,1)S(1)}, bf16[9,128,256]{2,1,0:T(8,128)(2,1)S(1)}, u32[]{:S(2)}, u32[]{:S(2)}) %collective-permute-start.17) | collective-permute-done | bytes 589856 | tf_op jit(solution)/shard_map/ppermute | solution.py:299
  70.9 0.1 fusion.3
  71.0 1.6 %collective-permute-start.18 = (bf16[288,256]{1,0:T(8,128)(2,1)S(1)}, bf16[288,256]{1,0:T(8,128)(2,1)S(1)}, u32[]{:S(2)}, u32[]{:S(2)}) collective-permute-start(bf16[288,256]{1,0:T(8,128)(2,1)S(1)} %get-tuple-element.54), channel_id=1, source_target_pairs={{0,2},{2,0},{4,6},{6,4},{8,10},{10,8},{12,14},{14,12},{16,18},{18,... | collective-permute-start | bytes 442376 | tf_op jit(solution)/shard_map/ppermute | solution.py:299
  72.6 1.5 %collective-permute-start.19 = (bf16[288,256]{1,0:T(8,128)(2,1)S(1)}, bf16[288,256]{1,0:T(8,128)(2,1)S(1)}, u32[]{:S(2)}, u32[]{:S(2)}) collective-permute-start(bf16[288,256]{1,0:T(8,128)(2,1)S(1)} %get-tuple-element.55), channel_id=1, source_target_pairs={{0,4},{2,6},{4,0},{6,2},{8,12},{10,14},{12,8},{14,10},{16,20},{18,... | collective-permute-start | bytes 442376 | tf_op jit(solution)/shard_map/ppermute | solution.py:299
  74.1 0.5 collective-permute-start.20
  74.6 7.1 %inputs.1 = (bf16[48,96,256]{2,1,0:T(8,128)(2,1)}, bf16[12,24,256]{2,1,0:T(8,128)(2,1)}) custom-call(bf16[50,96,768]{2,1,0:T(8,128)(2,1)S(1)} %get-tuple-element.51.three_four, bf16[14,32,768]{2,1,0:T(8,128)(2,1)S(1)} %get-tuple-element.52.three_six, bf16[9,256,256]{2,1,0:T(8,128)(2,1)S(1)} %copy-done.6), custom_call_target="tpu_custom_call" | custom-call | flops 5775556608 | bytes 4718592 | tf_op jit(solution)/shard_map/inputs/pallas_call | solution.py:533
  81.8 0.1 fusion
  81.9 2.7 %collective-permute-start.23 = (bf16[72,256]{1,0:T(8,128)(2,1)S(1)}, bf16[72,256]{1,0:T(8,128)(2,1)S(1)}, u32[]{:S(2)}, u32[]{:S(2)}) collective-permute-start(bf16[72,256]{1,0:T(8,128)(2,1)S(1)} %get-tuple-element.73), channel_id=1, source_target_pairs={{0,24},{2,26},{4,28},{6,30},{8,16},{10,18},{12,20},{14,22},{16,8},... | collective-permute-start | bytes 110600 | tf_op jit(solution)/shard_map/ppermute | solution.py:299
  84.6 1.7 %collective-permute-start.21 = (bf16[72,256]{1,0:T(8,128)(2,1)S(1)}, bf16[72,256]{1,0:T(8,128)(2,1)S(1)}, u32[]{:S(2)}, u32[]{:S(2)}) collective-permute-start(bf16[72,256]{1,0:T(8,128)(2,1)S(1)} %get-tuple-element.72), channel_id=1, source_target_pairs={{0,8},{2,10},{4,12},{6,14},{8,0},{10,2},{12,4},{14,6},{16,24},{18,... | collective-permute-start | bytes 110600 | tf_op jit(solution)/shard_map/ppermute | solution.py:299
  86.4 1.4 %collective-permute-done.23 = bf16[72,256]{1,0:T(8,128)(2,1)S(1)} collective-permute-done((bf16[72,256]{1,0:T(8,128)(2,1)S(1)}, bf16[72,256]{1,0:T(8,128)(2,1)S(1)}, u32[]{:S(2)}, u32[]{:S(2)}) %collective-permute-start.23) | collective-permute-done | bytes 36896 | tf_op jit(solution)/shard_map/ppermute | solution.py:299
  87.8 1.7 %collective-permute-done.22 = bf16[72,256]{1,0:T(8,128)(2,1)S(1)} collective-permute-done((bf16[72,256]{1,0:T(8,128)(2,1)S(1)}, bf16[72,256]{1,0:T(8,128)(2,1)S(1)}, u32[]{:S(2)}, u32[]{:S(2)}) %collective-permute-start.22) | collective-permute-done | bytes 36896 | tf_op jit(solution)/shard_map/ppermute | solution.py:299
  89.5 1.9 %collective-permute-start.24 = (bf16[72,256]{1,0:T(8,128)(2,1)S(1)}, bf16[72,256]{1,0:T(8,128)(2,1)S(1)}, u32[]{:S(2)}, u32[]{:S(2)}) collective-permute-start(bf16[72,256]{1,0:T(8,128)(2,1)S(1)} %fusion.5), channel_id=1, source_target_pairs={{0,24},{2,26},{4,28},{6,30},{8,16},{10,18},{12,20},{14,22},{16,8},... | collective-permute-start | bytes 110600 | tf_op jit(solution)/shard_map/ppermute | solution.py:299
  91.4 0.5 collective-permute-start.25
  91.9 2.1 %collective-permute-start.26 = (bf16[72,256]{1,0:T(8,128)(2,1)S(1)}, bf16[72,256]{1,0:T(8,128)(2,1)S(1)}, u32[]{:S(2)}, u32[]{:S(2)}) collective-permute-start(bf16[72,256]{1,0:T(8,128)(2,1)S(1)} %fusion.5), channel_id=1, source_target_pairs={{0,8},{2,10},{4,12},{6,14},{8,0},{10,2},{12,4},{14,6},{16,24},{18,... | collective-permute-start | bytes 110600 | tf_op jit(solution)/shard_map/ppermute | solution.py:299
  94.0 0.6 pad_maximum_fusion.1
  94.5 0.8 collective-permute-done.24
  95.3 1.3 %collective-permute-done.25 = bf16[72,256]{1,0:T(8,128)(2,1)S(1)} collective-permute-done((bf16[72,256]{1,0:T(8,128)(2,1)S(1)}, bf16[72,256]{1,0:T(8,128)(2,1)S(1)}, u32[]{:S(2)}, u32[]{:S(2)}) %collective-permute-start.25) | collective-permute-done | bytes 36896 | tf_op jit(solution)/shard_map/ppermute | solution.py:299
  96.7 1.6 %collective-permute-start.27 = (bf16[288,256]{1,0:T(8,128)(2,1)S(1)}, bf16[288,256]{1,0:T(8,128)(2,1)S(1)}, u32[]{:S(2)}, u32[]{:S(2)}) collective-permute-start(bf16[288,256]{1,0:T(8,128)(2,1)S(1)} %bitcast.73), channel_id=1, source_target_pairs={{0,2},{2,0},{4,6},{6,4},{8,10},{10,8},{12,14},{14,12},{16,18},{18,... | collective-permute-start | bytes 442376 | tf_op jit(solution)/shard_map/ppermute | solution.py:299
  98.3 1.5 %collective-permute-start.28 = (bf16[288,256]{1,0:T(8,128)(2,1)S(1)}, bf16[288,256]{1,0:T(8,128)(2,1)S(1)}, u32[]{:S(2)}, u32[]{:S(2)}) collective-permute-start(bf16[288,256]{1,0:T(8,128)(2,1)S(1)} %bitcast.74), channel_id=1, source_target_pairs={{0,4},{2,6},{4,0},{6,2},{8,12},{10,14},{12,8},{14,10},{16,20},{18,... | collective-permute-start | bytes 442376 | tf_op jit(solution)/shard_map/ppermute | solution.py:299
  99.8 0.5 collective-permute-start.29
  100.3 0.1 broadcast_in_dim.14
  100.4 1.9 %collective-permute-done.27 = bf16[288,256]{1,0:T(8,128)(2,1)S(1)} collective-permute-done((bf16[288,256]{1,0:T(8,128)(2,1)S(1)}, bf16[288,256]{1,0:T(8,128)(2,1)S(1)}, u32[]{:S(2)}, u32[]{:S(2)}) %collective-permute-start.27) | collective-permute-done | bytes 147488 | tf_op jit(solution)/shard_map/ppermute | solution.py:299
  102.4 1.1 %collective-permute-done.28 = bf16[288,256]{1,0:T(8,128)(2,1)S(1)} collective-permute-done((bf16[288,256]{1,0:T(8,128)(2,1)S(1)}, bf16[288,256]{1,0:T(8,128)(2,1)S(1)}, u32[]{:S(2)}, u32[]{:S(2)}) %collective-permute-start.28) | collective-permute-done | bytes 147488 | tf_op jit(solution)/shard_map/ppermute | solution.py:299
  103.5 2.3 %collective-permute-done.29 = bf16[288,256]{1,0:T(8,128)(2,1)S(1)} collective-permute-done((bf16[288,256]{1,0:T(8,128)(2,1)S(1)}, bf16[288,256]{1,0:T(8,128)(2,1)S(1)}, u32[]{:S(2)}, u32[]{:S(2)}) %collective-permute-start.29) | collective-permute-done | bytes 147488 | tf_op jit(solution)/shard_map/ppermute | solution.py:299
  105.9 0.0 copy-start.7
  105.9 1.0 copy-done.7
  (38 shorter events, 0.3 us)
Async XLA Ops:
  0.6 3.6 %copy-start.1 = (bf16[1,48,96,256]{3,2,1,0:T(8,128)(2,1)S(1)}, bf16[1,48,96,256]{3,2,1,0:T(8,128)(2,1)}, u32[]{:S(2)}) copy-start(bf16[1,48,96,256]{3,2,1,0:T(8,128)(2,1)} %param.7) | copy-start | bytes 7077892
  0.7 3.6 %copy-start.3 = (bf16[1,12,24,256]{3,2,1,0:T(8,128)(2,1)S(1)}, bf16[1,12,24,256]{3,2,1,0:T(8,128)(2,1)}, u32[]{:S(2)}) copy-start(bf16[1,12,24,256]{3,2,1,0:T(8,128)(2,1)} %param.8) | copy-start | bytes 442372
  0.7 3.6 %copy-start.6 = (bf16[9,256,256]{2,1,0:T(8,128)(2,1)S(1)}, bf16[9,256,256]{2,1,0:T(8,128)(2,1)}, u32[]{:S(2)}) copy-start(bf16[9,256,256]{2,1,0:T(8,128)(2,1)} %w_ref.3) | copy-start | bytes 3538948
  2.4 34.0 %copy-start.2 = (bf16[1,12,24,256]{3,2,1,0:T(8,128)(2,1)S(1)}, bf16[1,12,24,256]{3,2,1,0:T(8,128)(2,1)}, u32[]{:S(2)}) copy-start(bf16[1,12,24,256]{3,2,1,0:T(8,128)(2,1)} %param.13) | copy-start | bytes 442372
  2.4 34.0 %copy-start.4 = (f32[2,256]{1,0:T(2,128)S(1)}, f32[2,256]{1,0:T(2,128)}, u32[]{:S(2)}) copy-start(f32[2,256]{1,0:T(2,128)} %gain_ref.3) | copy-start | bytes 6148
  2.4 34.0 %copy-start.5 = (f32[2,256]{1,0:T(2,128)S(1)}, f32[2,256]{1,0:T(2,128)}, u32[]{:S(2)}) copy-start(f32[2,256]{1,0:T(2,128)} %shift_ref.3) | copy-start | bytes 6148
  2.5 1.8 %collective-permute-start = (bf16[384,256]{1,0:T(8,128)(2,1)}, bf16[384,256]{1,0:T(8,128)(2,1)S(1)}, u32[]{:S(2)}, u32[]{:S(2)}) collective-permute-start(bf16[384,256]{1,0:T(8,128)(2,1)} %edges.1), channel_id=1, source_target_pairs={{0,1},{1,0},{2,3},{3,2},{4,5},{5,4},{6,7},{7,6},{8,9},{9,8},{10,11... | collective-permute-start | bytes 589832 | tf_op jit(solution)/shard_map/ppermute | solution.py:299
  4.3 32.2 %copy-start = (bf16[1,48,96,256]{3,2,1,0:T(8,128)(2,1)S(1)}, bf16[1,48,96,256]{3,2,1,0:T(8,128)(2,1)}, u32[]{:S(2)}) copy-start(bf16[1,48,96,256]{3,2,1,0:T(8,128)(2,1)} %param.12) | copy-start | bytes 7077892
  10.7 1.3 %collective-permute-start.1 = (f32[4,256]{1,0:T(4,128)S(1)}, f32[4,256]{1,0:T(4,128)S(1)}, u32[]{:S(2)}, u32[]{:S(2)}) collective-permute-start(f32[4,256]{1,0:T(4,128)S(1)} %get-tuple-element.41), channel_id=1, source_target_pairs={{0,1},{1,0},{2,3},{3,2},{4,5},{5,4},{6,7},{7,6},{8,9},{9,8},{10,11... | collective-permute-start | bytes 12296 | tf_op jit(solution)/shard_map/ppermute | solution.py:299
  12.0 2.0 %collective-permute-start.3 = (f32[4,256]{1,0:T(4,128)S(1)}, f32[4,256]{1,0:T(4,128)S(1)}, u32[]{:S(2)}, u32[]{:S(2)}) collective-permute-start(f32[4,256]{1,0:T(4,128)S(1)} %add.78), channel_id=1, source_target_pairs={{0,0},{1,5},{2,2},{3,7},{4,4},{5,1},{6,6},{7,3},{8,8},{9,13},{10,1... | collective-permute-start | bytes 12296 | tf_op jit(solution)/shard_map/ppermute | solution.py:370
  12.6 1.4 %collective-permute-start.4 = (f32[4,256]{1,0:T(4,128)S(1)}, f32[4,256]{1,0:T(4,128)S(1)}, u32[]{:S(2)}, u32[]{:S(2)}) collective-permute-start(f32[4,256]{1,0:T(4,128)S(1)} %add.78), channel_id=1, source_target_pairs={{0,0},{1,7},{2,2},{3,5},{4,4},{5,3},{6,6},{7,1},{8,8},{9,15},{10,1... | collective-permute-start | bytes 12296 | tf_op jit(solution)/shard_map/ppermute | solution.py:370
  13.3 0.7 collective-permute-start.2
  14.0 2.0 %collective-permute-start.6 = (f32[4,256]{1,0:T(4,128)S(1)}, f32[4,256]{1,0:T(4,128)S(1)}, u32[]{:S(2)}, u32[]{:S(2)}) collective-permute-start(f32[4,256]{1,0:T(4,128)S(1)} %add_add_fusion.3), channel_id=1, source_target_pairs={{0,0},{1,17},{2,2},{3,19},{4,4},{5,21},{6,6},{7,23},{8,8},{9,25},{... | collective-permute-start | bytes 12296 | tf_op jit(solution)/shard_map/ppermute | solution.py:370
  14.7 1.4 %collective-permute-start.7 = (f32[4,256]{1,0:T(4,128)S(1)}, f32[4,256]{1,0:T(4,128)S(1)}, u32[]{:S(2)}, u32[]{:S(2)}) collective-permute-start(f32[4,256]{1,0:T(4,128)S(1)} %add_add_fusion.3), channel_id=1, source_target_pairs={{0,0},{1,25},{2,2},{3,27},{4,4},{5,29},{6,6},{7,31},{8,8},{9,17},{... | collective-permute-start | bytes 12296 | tf_op jit(solution)/shard_map/ppermute | solution.py:370
  15.4 0.7 collective-permute-start.5
  16.1 20.4 %collective-permute-start.8 = (f32[4,256]{1,0:T(4,128)S(1)}, f32[4,256]{1,0:T(4,128)S(1)}, u32[]{:S(2)}, u32[]{:S(2)}) collective-permute-start(f32[4,256]{1,0:T(4,128)S(1)} %add_add_fusion.2), channel_id=1, source_target_pairs={{0,1},{1,0},{2,3},{3,2},{4,5},{5,4},{6,7},{7,6},{8,9},{9,8},{10,11... | collective-permute-start | bytes 12296 | tf_op jit(solution)/shard_map/ppermute | solution.py:299
  39.2 1.2 %collective-permute-start.9 = (f32[4,256]{1,0:T(4,128)S(1)}, f32[4,256]{1,0:T(4,128)S(1)}, u32[]{:S(2)}, u32[]{:S(2)}) collective-permute-start(f32[4,256]{1,0:T(4,128)S(1)} %get-tuple-element.44), channel_id=1, source_target_pairs={{0,1},{1,0},{2,3},{3,2},{4,5},{5,4},{6,7},{7,6},{8,9},{9,8},{10,11... | collective-permute-start | bytes 12296 | tf_op jit(solution)/shard_map/ppermute | solution.py:299
  40.5 2.0 %collective-permute-start.11 = (f32[4,256]{1,0:T(4,128)S(1)}, f32[4,256]{1,0:T(4,128)S(1)}, u32[]{:S(2)}, u32[]{:S(2)}) collective-permute-start(f32[4,256]{1,0:T(4,128)S(1)} %add.85), channel_id=1, source_target_pairs={{0,0},{1,5},{2,2},{3,7},{4,4},{5,1},{6,6},{7,3},{8,8},{9,13},{10,1... | collective-permute-start | bytes 12296 | tf_op jit(solution)/shard_map/ppermute | solution.py:370
  41.1 1.4 %collective-permute-start.12 = (f32[4,256]{1,0:T(4,128)S(1)}, f32[4,256]{1,0:T(4,128)S(1)}, u32[]{:S(2)}, u32[]{:S(2)}) collective-permute-start(f32[4,256]{1,0:T(4,128)S(1)} %add.85), channel_id=1, source_target_pairs={{0,0},{1,7},{2,2},{3,5},{4,4},{5,3},{6,6},{7,1},{8,8},{9,15},{10,1... | collective-permute-start | bytes 12296 | tf_op jit(solution)/shard_map/ppermute | solution.py:370
  41.8 0.7 collective-permute-start.10
  42.5 2.2 %collective-permute-start.14 = (f32[4,256]{1,0:T(4,128)S(1)}, f32[4,256]{1,0:T(4,128)S(1)}, u32[]{:S(2)}, u32[]{:S(2)}) collective-permute-start(f32[4,256]{1,0:T(4,128)S(1)} %add_add_fusion.1), channel_id=1, source_target_pairs={{0,0},{1,17},{2,2},{3,19},{4,4},{5,21},{6,6},{7,23},{8,8},{9,25},{... | collective-permute-start | bytes 12296 | tf_op jit(solution)/shard_map/ppermute | solution.py:370
  43.2 1.5 %collective-permute-start.15 = (f32[4,256]{1,0:T(4,128)S(1)}, f32[4,256]{1,0:T(4,128)S(1)}, u32[]{:S(2)}, u32[]{:S(2)}) collective-permute-start(f32[4,256]{1,0:T(4,128)S(1)} %add_add_fusion.1), channel_id=1, source_target_pairs={{0,0},{1,25},{2,2},{3,27},{4,4},{5,29},{6,6},{7,31},{8,8},{9,17},{... | collective-permute-start | bytes 12296 | tf_op jit(solution)/shard_map/ppermute | solution.py:370
  43.8 0.9 collective-permute-start.13
  44.7 17.0 %collective-permute-start.16 = (f32[4,256]{1,0:T(4,128)S(1)}, f32[4,256]{1,0:T(4,128)S(1)}, u32[]{:S(2)}, u32[]{:S(2)}) collective-permute-start(f32[4,256]{1,0:T(4,128)S(1)} %add_add_fusion), channel_id=1, source_target_pairs={{0,1},{1,0},{2,3},{3,2},{4,5},{5,4},{6,7},{7,6},{8,9},{9,8},{10,11... | collective-permute-start | bytes 12296 | tf_op jit(solution)/shard_map/ppermute | solution.py:299
  68.9 2.1 %collective-permute-start.17 = (bf16[9,128,256]{2,1,0:T(8,128)(2,1)S(1)}, bf16[9,128,256]{2,1,0:T(8,128)(2,1)S(1)}, u32[]{:S(2)}, u32[]{:S(2)}) collective-permute-start(bf16[9,128,256]{2,1,0:T(8,128)(2,1)S(1)} %bitcast.67), channel_id=1, source_target_pairs={{0,1},{1,0},{2,3},{3,2},{4,5},{5,4},{6,7},{7,6},{8,9},{9,8},{10,11... | collective-permute-start | bytes 1769480 | tf_op jit(solution)/shard_map/ppermute | solution.py:299
  71.0 10.7 %collective-permute-start.18 = (bf16[288,256]{1,0:T(8,128)(2,1)S(1)}, bf16[288,256]{1,0:T(8,128)(2,1)S(1)}, u32[]{:S(2)}, u32[]{:S(2)}) collective-permute-start(bf16[288,256]{1,0:T(8,128)(2,1)S(1)} %get-tuple-element.54), channel_id=1, source_target_pairs={{0,2},{2,0},{4,6},{6,4},{8,10},{10,8},{12,14},{14,12},{16,18},{18,... | collective-permute-start | bytes 442376 | tf_op jit(solution)/shard_map/ppermute | solution.py:299
  72.6 9.2 %collective-permute-start.19 = (bf16[288,256]{1,0:T(8,128)(2,1)S(1)}, bf16[288,256]{1,0:T(8,128)(2,1)S(1)}, u32[]{:S(2)}, u32[]{:S(2)}) collective-permute-start(bf16[288,256]{1,0:T(8,128)(2,1)S(1)} %get-tuple-element.55), channel_id=1, source_target_pairs={{0,4},{2,6},{4,0},{6,2},{8,12},{10,14},{12,8},{14,10},{16,20},{18,... | collective-permute-start | bytes 442376 | tf_op jit(solution)/shard_map/ppermute | solution.py:299
  74.1 7.7 %collective-permute-start.20 = (bf16[288,256]{1,0:T(8,128)(2,1)S(1)}, bf16[288,256]{1,0:T(8,128)(2,1)S(1)}, u32[]{:S(2)}, u32[]{:S(2)}) collective-permute-start(bf16[288,256]{1,0:T(8,128)(2,1)S(1)} %get-tuple-element.56), channel_id=1, source_target_pairs={{0,6},{2,4},{4,2},{6,0},{8,14},{10,12},{12,10},{14,8},{16,22},{18,... | collective-permute-start | bytes 442376 | tf_op jit(solution)/shard_map/ppermute | solution.py:299
  81.9 5.9 %collective-permute-start.23 = (bf16[72,256]{1,0:T(8,128)(2,1)S(1)}, bf16[72,256]{1,0:T(8,128)(2,1)S(1)}, u32[]{:S(2)}, u32[]{:S(2)}) collective-permute-start(bf16[72,256]{1,0:T(8,128)(2,1)S(1)} %get-tuple-element.73), channel_id=1, source_target_pairs={{0,24},{2,26},{4,28},{6,30},{8,16},{10,18},{12,20},{14,22},{16,8},... | collective-permute-start | bytes 110600 | tf_op jit(solution)/shard_map/ppermute | solution.py:299
  84.6 4.9 %collective-permute-start.22 = (bf16[72,256]{1,0:T(8,128)(2,1)S(1)}, bf16[72,256]{1,0:T(8,128)(2,1)S(1)}, u32[]{:S(2)}, u32[]{:S(2)}) collective-permute-start(bf16[72,256]{1,0:T(8,128)(2,1)S(1)} %get-tuple-element.74), channel_id=1, source_target_pairs={{0,16},{2,18},{4,20},{6,22},{8,24},{10,26},{12,28},{14,30},{16,0},... | collective-permute-start | bytes 110600 | tf_op jit(solution)/shard_map/ppermute | solution.py:299
  84.6 4.9 %collective-permute-start.21 = (bf16[72,256]{1,0:T(8,128)(2,1)S(1)}, bf16[72,256]{1,0:T(8,128)(2,1)S(1)}, u32[]{:S(2)}, u32[]{:S(2)}) collective-permute-start(bf16[72,256]{1,0:T(8,128)(2,1)S(1)} %get-tuple-element.72), channel_id=1, source_target_pairs={{0,8},{2,10},{4,12},{6,14},{8,0},{10,2},{12,4},{14,6},{16,24},{18,... | collective-permute-start | bytes 110600 | tf_op jit(solution)/shard_map/ppermute | solution.py:299
  89.5 5.8 %collective-permute-start.24 = (bf16[72,256]{1,0:T(8,128)(2,1)S(1)}, bf16[72,256]{1,0:T(8,128)(2,1)S(1)}, u32[]{:S(2)}, u32[]{:S(2)}) collective-permute-start(bf16[72,256]{1,0:T(8,128)(2,1)S(1)} %fusion.5), channel_id=1, source_target_pairs={{0,24},{2,26},{4,28},{6,30},{8,16},{10,18},{12,20},{14,22},{16,8},... | collective-permute-start | bytes 110600 | tf_op jit(solution)/shard_map/ppermute | solution.py:299
  91.4 5.3 %collective-permute-start.25 = (bf16[72,256]{1,0:T(8,128)(2,1)S(1)}, bf16[72,256]{1,0:T(8,128)(2,1)S(1)}, u32[]{:S(2)}, u32[]{:S(2)}) collective-permute-start(bf16[72,256]{1,0:T(8,128)(2,1)S(1)} %fusion.5), channel_id=1, source_target_pairs={{0,16},{2,18},{4,20},{6,22},{8,24},{10,26},{12,28},{14,30},{16,0},... | collective-permute-start | bytes 110600 | tf_op jit(solution)/shard_map/ppermute | solution.py:299
  91.9 4.8 %collective-permute-start.26 = (bf16[72,256]{1,0:T(8,128)(2,1)S(1)}, bf16[72,256]{1,0:T(8,128)(2,1)S(1)}, u32[]{:S(2)}, u32[]{:S(2)}) collective-permute-start(bf16[72,256]{1,0:T(8,128)(2,1)S(1)} %fusion.5), channel_id=1, source_target_pairs={{0,8},{2,10},{4,12},{6,14},{8,0},{10,2},{12,4},{14,6},{16,24},{18,... | collective-permute-start | bytes 110600 | tf_op jit(solution)/shard_map/ppermute | solution.py:299
  96.7 5.6 %collective-permute-start.27 = (bf16[288,256]{1,0:T(8,128)(2,1)S(1)}, bf16[288,256]{1,0:T(8,128)(2,1)S(1)}, u32[]{:S(2)}, u32[]{:S(2)}) collective-permute-start(bf16[288,256]{1,0:T(8,128)(2,1)S(1)} %bitcast.73), channel_id=1, source_target_pairs={{0,2},{2,0},{4,6},{6,4},{8,10},{10,8},{12,14},{14,12},{16,18},{18,... | collective-permute-start | bytes 442376 | tf_op jit(solution)/shard_map/ppermute | solution.py:299
  98.3 5.2 %collective-permute-start.28 = (bf16[288,256]{1,0:T(8,128)(2,1)S(1)}, bf16[288,256]{1,0:T(8,128)(2,1)S(1)}, u32[]{:S(2)}, u32[]{:S(2)}) collective-permute-start(bf16[288,256]{1,0:T(8,128)(2,1)S(1)} %bitcast.74), channel_id=1, source_target_pairs={{0,4},{2,6},{4,0},{6,2},{8,12},{10,14},{12,8},{14,10},{16,20},{18,... | collective-permute-start | bytes 442376 | tf_op jit(solution)/shard_map/ppermute | solution.py:299
  99.8 6.0 %collective-permute-start.29 = (bf16[288,256]{1,0:T(8,128)(2,1)S(1)}, bf16[288,256]{1,0:T(8,128)(2,1)S(1)}, u32[]{:S(2)}, u32[]{:S(2)}) collective-permute-start(bf16[288,256]{1,0:T(8,128)(2,1)S(1)} %bitcast.75), channel_id=1, source_target_pairs={{0,6},{2,4},{4,2},{6,0},{8,14},{10,12},{12,10},{14,8},{16,22},{18,... | collective-permute-start | bytes 442376 | tf_op jit(solution)/shard_map/ppermute | solution.py:299
  105.9 1.0 copy-start.7

commit v4 on v2

--- a/solution.py
+++ b/solution.py
@@ -9,6 +9,7 @@
 
 GROUP = 16
 RADIX = 4
+FAR_FIRST = (3, 2, 1)
 EPSILON = 1e-05
 F32 = jnp.float32
 BF16 = jnp.bfloat16
@@ -268,28 +269,43 @@
                 sent_ref[step - 1, tap] = part.astype(BF16)
 
 
-def input_level(three, turned, grad, grad_ref, sems, most):
-    rows, cols, chan = grad.shape
+def input_chunks(three, turned, grad, chunks, offset, sent=None):
+    cols, chan = grad.shape[1:]
     pitch = three.shape[1]
-    copies = []
-    for index, (start, end) in enumerate(chunks_of(rows, most)):
+    for index, (start, end) in enumerate(chunks):
         size = end - start
         lhs = beside(three, (start + 2, start + 1, start), size)
         term = jnp.dot(lhs, turned[...], preferred_element_type=F32)
-        grad[start:end] = term.reshape(size, pitch, chan)[:, :cols].astype(BF16)
-        copies.append(pltpu.make_async_copy(grad.at[start:end], grad_ref.at[start:end], sems.at[index]))
-        copies[-1].start()
-    return copies
-
-
-def input_kernel(
-    three_four, three_six, w_ref, grad_four_ref, grad_six_ref, turned, grad_four, grad_six, sems_four, sems_six
-):
+        grad[start - offset : end - offset] = term.reshape(size, pitch, chan)[:, :cols].astype(BF16)
+        if sent is not None:
+            sent(index, start, end)
+
+
+def input_first_kernel(chunks, three_four, w_ref, grad_ref, turned):
     chan = w_ref.shape[1]
     for tap in range(9):
         turned[tap * chan : (tap + 1) * chan] = w_ref[tap].T
-    copies = input_level(three_six, turned, grad_six, grad_six_ref, sems_six, 12)
-    copies += input_level(three_four, turned, grad_four, grad_four_ref, sems_four, 8)
+    input_chunks(three_four, turned, grad_ref, chunks, 0)
+
+
+def input_second_kernel(
+    chunks, done, three_four, three_six, turned, first_ref, grad_four_ref, grad_six_ref,
+    grad_four, grad_six, sem_first, sems_four, sems_six,
+):
+    copies = [pltpu.make_async_copy(first_ref, grad_four_ref.at[:done], sem_first)]
+    copies[0].start()
+
+    def sender(grad, grad_ref, offset, sems):
+        def sent(index, start, end):
+            copy = pltpu.make_async_copy(grad.at[start - offset : end - offset], grad_ref.at[start:end], sems.at[index])
+            copy.start()
+            copies.append(copy)
+
+        return sent
+
+    six_chunks = chunks_of(grad_six.shape[0], 12)
+    input_chunks(three_six, turned, grad_six, six_chunks, 0, sender(grad_six, grad_six_ref, 0, sems_six))
+    input_chunks(three_four, turned, grad_four, chunks, done, sender(grad_four, grad_four_ref, done, sems_four))
     for copy in copies:
         copy.wait()
 
@@ -358,28 +374,29 @@
     return above, below
 
 
-def swap_odd(array, axis, stride):
+def swap_across(array, axis, stride):
     count, sp_count = lax.axis_size("rep"), lax.axis_size("sp")
-    pairs = []
-    for rep in range(count):
-        for sp in range(1, sp_count, 2):
-            other = (rep ^ stride) * sp_count + sp if axis == "rep" else rep * sp_count + (sp ^ stride)
-            pairs.append((rep * sp_count + sp, other))
+    rep_stride, sp_stride = (stride, 1) if axis == "rep" else (0, stride ^ 1)
+    pairs = [
+        (rep * sp_count + sp, (rep ^ rep_stride) * sp_count + (sp ^ sp_stride))
+        for rep in range(count)
+        for sp in range(sp_count)
+    ]
     return lax.ppermute(array, ("rep", "sp"), pairs)
 
 
-def group_sum(sums, odd):
+def group_sum(sums):
     sums = sums + swap(sums, "sp", 1)
     stride = 2
     while stride < lax.axis_size("sp"):
-        sums = sums + swap_odd(sums, "sp", stride)
+        sums = sums + swap_across(sums, "sp", stride)
         stride = 2 * stride
     stride = 1
     while stride < GROUP:
-        met = [swap_odd(sums, "rep", k * stride) for k in range(1, RADIX)]
-        sums = (sums + met[0]) + (met[1] + met[2])
+        met = [swap_across(sums, "rep", k * stride) for k in FAR_FIRST]
+        sums = (sums + met[2]) + (met[1] + met[0])
         stride = RADIX * stride
-    return jnp.where(odd, sums, swap(sums, "sp", 1))
+    return sums
 
 
 def every_group(sums):
@@ -395,7 +412,7 @@
     for shift in (0, 2):
         digit = (lax.axis_index("rep") >> shift) & (RADIX - 1)
         found.append(([digit ^ k for k in range(RADIX)], (digit & 1) == 1, digit >= 2))
-    return found + [(lax.axis_index("sp") & 1) == 1]
+    return found
 
 
 def digit_order(parts, place):
@@ -420,32 +437,34 @@
             total = total + piece_of(part, place[0][k]).astype(F32)
         return total
 
-    return piece(0), [piece(k).astype(BF16) for k in range(1, RADIX)]
+    return piece(0), [piece(k).astype(BF16) for k in FAR_FIRST]
 
 
 def added(own, met):
-    return (own + met[0].astype(F32)) + (met[1].astype(F32) + met[2].astype(F32))
-
-
-def weight_finish(total, found):
+    return (own + met[2].astype(F32)) + (met[1].astype(F32) + met[0].astype(F32))
+
+
+def fours(pieces, stride):
+    return [swap(piece, "rep", k * stride) for k, piece in zip(FAR_FIRST, pieces)]
+
+
+def scatter_next(total, place):
+    pieces = total.reshape(RADIX, -1, total.shape[1])
+    return piece_of(pieces, place[0][0]), [piece_of(pieces, place[0][k]).astype(BF16) for k in FAR_FIRST]
+
+
+def weight_gather(total, found):
     chan = total.shape[1]
-    indices = found[1][0]
-    pieces = total.reshape(RADIX, -1, chan)
-    met = [
-        swap(piece_of(pieces, indices[k]).astype(BF16), "rep", k * RADIX)
-        for k in range(1, RADIX)
-    ]
-    total = added(piece_of(pieces, indices[0]), met).astype(BF16)
+    total = total.astype(BF16)
     stride = GROUP
     while stride < lax.axis_size("rep"):
-        met = [swap(total, "rep", k * stride) for k in range(1, RADIX)]
-        total = added(total.astype(F32), met).astype(BF16)
+        total = added(total.astype(F32), fours([total] * 3, stride)).astype(BF16)
         stride = RADIX * stride
-    met = [total] + [swap(total, "rep", k * RADIX) for k in range(1, RADIX)]
+    met = [total] + fours([total] * 3, RADIX)[::-1]
     total = digit_order(met, found[1]).reshape(-1, chan)
-    met = [total] + [swap(total, "rep", k) for k in range(1, RADIX)]
+    met = [total] + fours([total] * 3, 1)[::-1]
     whole = jnp.zeros((RADIX,) + total.shape, F32)
-    for k in range(RADIX):
+    for k in (0,) + FAR_FIRST:
         start = (found[0][0][k], 0, 0)
         whole = lax.dynamic_update_slice(whole, met[k][None].astype(F32), start, allow_negative_indices=False)
     return whole
@@ -488,7 +507,7 @@
         cost_estimate=cost(1, 4 * four.size),
         name="forward",
     )(four, six, above, below, conv_weight)
-    moments = group_sum(moments, found[2])
+    moments = group_sum(moments)
 
     slope_four, slope_six, slopes = pl.pallas_call(
         functools.partial(slope_kernel, counts),
@@ -503,7 +522,7 @@
         cost_estimate=cost(0.01, 4 * four.size),
         name="slopes",
     )(conv_four, conv_six, cot_four, cot_six, above, below, moments, bn_gain, bn_shift)
-    slopes = group_sum(slopes, found[2])
+    slopes = group_sum(slopes)
 
     share = chan // sp_count
     wide_four, wide_six = (
@@ -527,28 +546,48 @@
 
     piece, pieces = scatter_start(own, sent, found[0])
     pieces, three_four = lax.optimization_barrier((pieces, three_four))
-    met = [swap(pieces[k - 1], "rep", k) for k in range(1, RADIX)]
+    met = fours(pieces, 1)
+    chunks = chunks_of(rows_four, 8)
+    split = -(-2 * len(chunks) // 3)
+    done = chunks[split - 1][1]
+    grad_first, turned = pl.pallas_call(
+        functools.partial(input_first_kernel, chunks[:split]),
+        out_shape=(
+            jax.ShapeDtypeStruct((done, cols_four, chan), BF16),
+            jax.ShapeDtypeStruct((9 * chan, chan), BF16),
+        ),
+        in_specs=[vmem] * 2,
+        out_specs=(vmem, vmem),
+        compiler_params=params,
+        cost_estimate=cost(0.6, 3 * four.size),
+        name="inputs_first",
+    )(three_four, conv_weight)
+    met, grad_first = lax.optimization_barrier((met, grad_first))
+
+    piece, pieces = scatter_next(added(piece, met), found[1])
+    pieces, three_six = lax.optimization_barrier((pieces, three_six))
+    met = fours(pieces, RADIX)
     grad_four, grad_six = pl.pallas_call(
-        input_kernel,
+        functools.partial(input_second_kernel, chunks[split:], done),
         out_shape=(
             jax.ShapeDtypeStruct(four.shape, BF16),
             jax.ShapeDtypeStruct(six.shape, BF16),
         ),
-        in_specs=[vmem] * 3,
+        in_specs=[vmem] * 4,
         out_specs=(hbm, hbm),
         scratch_shapes=[
-            pltpu.VMEM((9 * chan, chan), BF16),
-            pltpu.VMEM(four.shape, BF16),
+            pltpu.VMEM((max(rows_four - done, 1), cols_four, chan), BF16),
             pltpu.VMEM(six.shape, BF16),
-            pltpu.SemaphoreType.DMA((len(chunks_of(rows_four, 8)),)),
+            pltpu.SemaphoreType.DMA,
+            pltpu.SemaphoreType.DMA((len(chunks),)),
             pltpu.SemaphoreType.DMA((len(chunks_of(rows_six, 12)),)),
         ],
         compiler_params=params,
-        cost_estimate=cost(1, 4 * four.size),
-        name="inputs",
-    )(three_four, three_six, conv_weight)
+        cost_estimate=cost(0.4, 2 * four.size),
+        name="inputs_second",
+    )(three_four, three_six, turned, grad_first)
     met, grad_six = lax.optimization_barrier((met, grad_six))
-    grad_weight = weight_finish(added(piece, met), found).reshape(own.shape)
+    grad_weight = weight_gather(added(piece, met), found).reshape(own.shape)
     totals = every_group(slopes)
     grad_gain = jnp.stack([totals[1], totals[3]])
     grad_shift = jnp.stack([totals[0], totals[2]])

time: 107 us -> 85.7 us (0.80)
  starting transfers between devices: 61.7 us -> 31.7 us
  waiting for transfers between devices: 16.8 us -> 25 us
    ppermute x18 -> x16, starting transfers between devices: 53.6 us -> 17.6 us  [swap(): return lax.ppermute(array, axis, [(i, i ^ stride) for i in range(count)])]
    ppermute x12, waiting for transfers between devices: 0.03 us -> 11.4 us  [swap_across(): return lax.ppermute(array, ('rep', 'sp'), pairs)]
    ppermute x12, starting transfers between devices: 8.1 us -> 14.1 us  [swap_across(): return lax.ppermute(array, ('rep', 'sp'), pairs)]
    ppermute x18 -> x16, waiting for transfers between devices: 16.8 us -> 13.6 us  [swap(): return lax.ppermute(array, axis, [(i, i ^ stride) for i in range(count)])]
    pallas_call x1 -> x2, Pallas kernels: 7.14 us -> 7.15 us  [the longest x1 3.86 us: local(): pl.pallas_call(functools.partial(input_first_kernel, chunks[:split]), out...]
  transfers between devices with their start and end apart: 30 -> 28, of which waited for: 13 -> 17; matrix products, arithmetic and copies ran while one was open for 1% -> 1% of each run, Pallas kernels for 7% -> 8%
where the time goes in v4:
time: 85.7 us; the launch traced here: 85.5 us
  starting transfers between devices  31.7 us (37%)
  Pallas kernels  25.7 us (30%)
  waiting for transfers between devices  25 us (29%)
  local copies, waits for them, and re-layouts  1.16 us (1%)
  other arithmetic  0.99 us (1%)
  between operations  0.91 us (1%)
    ppermute x16, starting transfers between devices, swap(): return lax.ppermute(array, axis, [(i, i ^ stride) for i in range(count)])  17.6 us
    ppermute x12, starting transfers between devices, swap_across(): return lax.ppermute(array, ('rep', 'sp'), pairs)  14.1 us
    ppermute x16, waiting for transfers between devices, swap(): return lax.ppermute(array, axis, [(i, i ^ stride) for i in range(count)])  13.6 us
    ppermute x12, waiting for transfers between devices, swap_across(): return lax.ppermute(array, ('rep', 'sp'), pairs)  11.4 us
    pallas_call x1, Pallas kernels, local(): pl.pallas_call(functools.partial(backward_kernel, counts, sp_count), out_...  7.53 us
    pallas_call x1, Pallas kernels, local(): pl.pallas_call(functools.partial(forward_kernel, sp_count), out_shape=(fr...  6.44 us
    pallas_call x1, Pallas kernels, local(): pl.pallas_call(functools.partial(input_first_kernel, chunks[:split]), out...  3.86 us
    pallas_call x1, Pallas kernels, local(): pl.pallas_call(functools.partial(input_second_kernel, chunks[split:], don...  3.28 us
  transfers between devices with their start and end apart: 28, of which 17 were waited for; matrix products, arithmetic and copies ran while one was open for 1% of the time, Pallas kernels for 8%

profile of v4, /device:TPU:0, one launch (start us, length us, event | category | flops | bytes accessed | tf_op | source)
XLA Modules:
  0.0 85.5 jit_solution(791414217260519832)
XLA Ops:
  0.7 1.7 %edges.1 = bf16[384,256]{1,0:T(8,128)(2,1)} custom-call(bf16[48,96,256]{2,1,0:T(8,128)(2,1)} %bitcast.57, bf16[12,24,256]{2,1,0:T(8,128)(2,1)} %bitcast.64, bf16[48,96,256]{2,1,0:T(8,128)(2,1)} %bitcast.55, bf16[12,24,256]{2,1,0:T(8,128)(2,1)} %bitcast.62), custom_call_target="tpu_custom_call" | custom-call | tf_op jit(solution)/shard_map/edges/pallas_call | solution.py:357
  2.4 0.0 copy-start.2
  2.4 0.0 copy-start.4
  2.4 0.0 copy-start.5
  2.5 0.5 collective-permute-start
  3.0 1.3 %collective-permute-done.above_ref.below_ref = bf16[384,256]{1,0:T(8,128)(2,1)S(1)} collective-permute-done((bf16[384,256]{1,0:T(8,128)(2,1)}, bf16[384,256]{1,0:T(8,128)(2,1)S(1)}, u32[]{:S(2)}, u32[]{:S(2)}) %collective-permute-start) | collective-permute-done | bytes 196640 | tf_op jit(solution)/shard_map/ppermute | solution.py:315
  4.3 6.4 %forward.1 = (bf16[50,96,256]{2,1,0:T(8,128)(2,1)S(1)}, bf16[14,32,256]{2,1,0:T(8,128)(2,1)S(1)}, f32[4,256]{1,0:T(4,128)S(1)}) custom-call(bf16[48,96,256]{2,1,0:T(8,128)(2,1)S(1)} %bitcast.58, bf16[12,24,256]{2,1,0:T(8,128)(2,1)S(1)} %bitcast.65, bf16[384,256]{1,0:T(8,128)(2,1)S(1)} %collective-permute-done.above_ref.below_ref, ...), custom_call_target="tpu_custom_call" | custom-call | flops 5775556608 | bytes 4718592 | tf_op jit(solution)/shard_map/forward/pallas_call | solution.py:497
  10.7 0.4 collective-permute-start.1
  11.2 0.8 collective-permute-done.1
  12.0 2.6 %collective-permute-start.3 = (f32[4,256]{1,0:T(4,128)S(1)}, f32[4,256]{1,0:T(4,128)S(1)}, u32[]{:S(2)}, u32[]{:S(2)}) collective-permute-start(f32[4,256]{1,0:T(4,128)S(1)} %add.78), channel_id=1, source_target_pairs={{0,5},{1,4},{2,7},{3,6},{4,1},{5,0},{6,3},{7,2},{8,13},{9,12},{10,... | collective-permute-start | bytes 12296 | tf_op jit(solution)/shard_map/ppermute | solution.py:385
  14.6 1.4 %collective-permute-start.4 = (f32[4,256]{1,0:T(4,128)S(1)}, f32[4,256]{1,0:T(4,128)S(1)}, u32[]{:S(2)}, u32[]{:S(2)}) collective-permute-start(f32[4,256]{1,0:T(4,128)S(1)} %add.78), channel_id=1, source_target_pairs={{0,7},{1,6},{2,5},{3,4},{4,3},{5,2},{6,1},{7,0},{8,15},{9,14},{10,... | collective-permute-start | bytes 12296 | tf_op jit(solution)/shard_map/ppermute | solution.py:385
  16.0 0.1 collective-permute-start.2
  16.1 0.0 collective-permute-done.3
  16.1 2.5 %collective-permute-done.4 = f32[4,256]{1,0:T(4,128)S(1)} collective-permute-done((f32[4,256]{1,0:T(4,128)S(1)}, f32[4,256]{1,0:T(4,128)S(1)}, u32[]{:S(2)}, u32[]{:S(2)}) %collective-permute-start.4) | collective-permute-done | bytes 4128 | tf_op jit(solution)/shard_map/ppermute | solution.py:385
  18.6 0.5 collective-permute-done.2
  19.0 2.4 %collective-permute-start.6 = (f32[4,256]{1,0:T(4,128)S(1)}, f32[4,256]{1,0:T(4,128)S(1)}, u32[]{:S(2)}, u32[]{:S(2)}) collective-permute-start(f32[4,256]{1,0:T(4,128)S(1)} %add_add_fusion.3), channel_id=1, source_target_pairs={{0,17},{1,16},{2,19},{3,18},{4,21},{5,20},{6,23},{7,22},{8,25},{9,... | collective-permute-start | bytes 12296 | tf_op jit(solution)/shard_map/ppermute | solution.py:385
  21.4 1.3 %collective-permute-start.7 = (f32[4,256]{1,0:T(4,128)S(1)}, f32[4,256]{1,0:T(4,128)S(1)}, u32[]{:S(2)}, u32[]{:S(2)}) collective-permute-start(f32[4,256]{1,0:T(4,128)S(1)} %add_add_fusion.3), channel_id=1, source_target_pairs={{0,25},{1,24},{2,27},{3,26},{4,29},{5,28},{6,31},{7,30},{8,17},{9,... | collective-permute-start | bytes 12296 | tf_op jit(solution)/shard_map/ppermute | solution.py:385
  22.7 0.2 collective-permute-start.5
  22.9 0.0 collective-permute-done.6
  23.0 3.3 %collective-permute-done.7 = f32[4,256]{1,0:T(4,128)S(1)} collective-permute-done((f32[4,256]{1,0:T(4,128)S(1)}, f32[4,256]{1,0:T(4,128)S(1)}, u32[]{:S(2)}, u32[]{:S(2)}) %collective-permute-start.7) | collective-permute-done | bytes 4128 | tf_op jit(solution)/shard_map/ppermute | solution.py:385
  26.3 2.9 %slopes.1 = (f32[50,96,256]{2,1,0:T(8,128)S(1)}, f32[14,32,256]{2,1,0:T(8,128)S(1)}, f32[4,256]{1,0:T(4,128)S(1)}) custom-call(bf16[50,96,256]{2,1,0:T(8,128)(2,1)S(1)} %get-tuple-element.47.conv_four_ref, bf16[14,32,256]{2,1,0:T(8,128)(2,1)S(1)} %get-tuple-element.48.conv_six_ref, bf16[48,96,256]{2,1,0:T(8,128)(2,1)S(1)} %bitcast.56, ...), custom_call_target="tpu_custom_call" | custom-call | flops 57755568 | bytes 4718592 | tf_op jit(solution)/shard_map/slopes/pallas_call | solution.py:512
  29.2 0.4 collective-permute-start.8
  29.6 0.8 collective-permute-done.8
  30.4 1.5 %collective-permute-start.10 = (f32[4,256]{1,0:T(4,128)S(1)}, f32[4,256]{1,0:T(4,128)S(1)}, u32[]{:S(2)}, u32[]{:S(2)}) collective-permute-start(f32[4,256]{1,0:T(4,128)S(1)} %add.85), channel_id=1, source_target_pairs={{0,5},{1,4},{2,7},{3,6},{4,1},{5,0},{6,3},{7,2},{8,13},{9,12},{10,... | collective-permute-start | bytes 12296 | tf_op jit(solution)/shard_map/ppermute | solution.py:385
  31.9 1.0 %collective-permute-start.11 = (f32[4,256]{1,0:T(4,128)S(1)}, f32[4,256]{1,0:T(4,128)S(1)}, u32[]{:S(2)}, u32[]{:S(2)}) collective-permute-start(f32[4,256]{1,0:T(4,128)S(1)} %add.85), channel_id=1, source_target_pairs={{0,7},{1,6},{2,5},{3,4},{4,3},{5,2},{6,1},{7,0},{8,15},{9,14},{10,... | collective-permute-start | bytes 12296 | tf_op jit(solution)/shard_map/ppermute | solution.py:385
  32.9 0.7 collective-permute-start.9
  33.6 0.0 collective-permute-done.10
  33.6 2.2 %collective-permute-done.11 = f32[4,256]{1,0:T(4,128)S(1)} collective-permute-done((f32[4,256]{1,0:T(4,128)S(1)}, f32[4,256]{1,0:T(4,128)S(1)}, u32[]{:S(2)}, u32[]{:S(2)}) %collective-permute-start.11) | collective-permute-done | bytes 4128 | tf_op jit(solution)/shard_map/ppermute | solution.py:385
  35.8 0.1 collective-permute-done.9
  35.9 1.0 %collective-permute-start.13 = (f32[4,256]{1,0:T(4,128)S(1)}, f32[4,256]{1,0:T(4,128)S(1)}, u32[]{:S(2)}, u32[]{:S(2)}) collective-permute-start(f32[4,256]{1,0:T(4,128)S(1)} %add_add_fusion.1), channel_id=1, source_target_pairs={{0,17},{1,16},{2,19},{3,18},{4,21},{5,20},{6,23},{7,22},{8,25},{9,... | collective-permute-start | bytes 12296 | tf_op jit(solution)/shard_map/ppermute | solution.py:385
  36.9 0.9 %collective-permute-start.14 = (f32[4,256]{1,0:T(4,128)S(1)}, f32[4,256]{1,0:T(4,128)S(1)}, u32[]{:S(2)}, u32[]{:S(2)}) collective-permute-start(f32[4,256]{1,0:T(4,128)S(1)} %add_add_fusion.1), channel_id=1, source_target_pairs={{0,25},{1,24},{2,27},{3,26},{4,29},{5,28},{6,31},{7,30},{8,17},{9,... | collective-permute-start | bytes 12296 | tf_op jit(solution)/shard_map/ppermute | solution.py:385
  37.8 1.1 %collective-permute-start.12 = (f32[4,256]{1,0:T(4,128)S(1)}, f32[4,256]{1,0:T(4,128)S(1)}, u32[]{:S(2)}, u32[]{:S(2)}) collective-permute-start(f32[4,256]{1,0:T(4,128)S(1)} %add_add_fusion.1), channel_id=1, source_target_pairs={{0,9},{1,8},{2,11},{3,10},{4,13},{5,12},{6,15},{7,14},{8,1},{9,0},... | collective-permute-start | bytes 12296 | tf_op jit(solution)/shard_map/ppermute | solution.py:385
  38.9 0.9 %collective-permute-done.13 = f32[4,256]{1,0:T(4,128)S(1)} collective-permute-done((f32[4,256]{1,0:T(4,128)S(1)}, f32[4,256]{1,0:T(4,128)S(1)}, u32[]{:S(2)}, u32[]{:S(2)}) %collective-permute-start.13) | collective-permute-done | bytes 4128 | tf_op jit(solution)/shard_map/ppermute | solution.py:385
  39.8 1.9 %collective-permute-done.14 = f32[4,256]{1,0:T(4,128)S(1)} collective-permute-done((f32[4,256]{1,0:T(4,128)S(1)}, f32[4,256]{1,0:T(4,128)S(1)}, u32[]{:S(2)}, u32[]{:S(2)}) %collective-permute-start.14) | collective-permute-done | bytes 4128 | tf_op jit(solution)/shard_map/ppermute | solution.py:385
  41.7 0.0 collective-permute-done.12
  41.7 7.5 %backward.1 = (bf16[50,96,768]{2,1,0:T(8,128)(2,1)S(1)}, bf16[14,32,768]{2,1,0:T(8,128)(2,1)S(1)}, f32[9,128,256]{2,1,0:T(8,128)S(1)}, bf16[1,9,128,256]{3,2,1,0:T(8,128)(2,1)S(1)}) custom-call(bf16[48,96,256]{2,1,0:T(8,128)(2,1)S(1)} %bitcast.59, bf16[12,24,256]{2,1,0:T(8,128)(2,1)S(1)} %bitcast.66, ...), custom_call_target="tpu_custom_call" | custom-call | flops 6930668032 | bytes 9437184 | tf_op jit(solution)/shard_map/backward/pallas_call | solution.py:531
  49.2 0.3 collective-permute-start.15
  49.5 1.8 %collective-permute-done.15 = bf16[9,128,256]{2,1,0:T(8,128)(2,1)S(1)} collective-permute-done((bf16[9,128,256]{2,1,0:T(8,128)(2,1)S(1)}, bf16[9,128,256]{2,1,0:T(8,128)(2,1)S(1)}, u32[]{:S(2)}, u32[]{:S(2)}) %collective-permute-start.15) | collective-permute-done | bytes 589856 | tf_op jit(solution)/shard_map/ppermute | solution.py:315
  51.3 0.1 fusion.3
  51.4 1.8 %collective-permute-start.16 = (bf16[288,256]{1,0:T(8,128)(2,1)S(1)}, bf16[288,256]{1,0:T(8,128)(2,1)S(1)}, u32[]{:S(2)}, u32[]{:S(2)}) collective-permute-start(bf16[288,256]{1,0:T(8,128)(2,1)S(1)} %get-tuple-element.61), channel_id=1, source_target_pairs={{0,6},{2,4},{4,2},{6,0},{8,14},{10,12},{12,10},{14,8},{16,22},{18,... | collective-permute-start | bytes 442376 | tf_op jit(solution)/shard_map/ppermute | solution.py:315
  53.2 0.5 collective-permute-start.17
  53.7 1.3 %collective-permute-start.18 = (bf16[288,256]{1,0:T(8,128)(2,1)S(1)}, bf16[288,256]{1,0:T(8,128)(2,1)S(1)}, u32[]{:S(2)}, u32[]{:S(2)}) collective-permute-start(bf16[288,256]{1,0:T(8,128)(2,1)S(1)} %get-tuple-element.63), channel_id=1, source_target_pairs={{0,2},{2,0},{4,6},{6,4},{8,10},{10,8},{12,14},{14,12},{16,18},{18,... | collective-permute-start | bytes 442376 | tf_op jit(solution)/shard_map/ppermute | solution.py:315
  55.0 3.9 %inputs_first.1 = (bf16[32,96,256]{2,1,0:T(8,128)(2,1)S(1)}, bf16[2304,256]{1,0:T(8,128)(2,1)S(1)}) custom-call(bf16[50,96,768]{2,1,0:T(8,128)(2,1)S(1)} %get-tuple-element.59.three_four, bf16[9,256,256]{2,1,0:T(8,128)(2,1)S(1)} %copy-done.6), custom_call_target="tpu_custom_call" | custom-call | flops 3465334016 | bytes 3538944 | tf_op jit(solution)/shard_map/inputs_first/pallas_call | solution.py:553
  58.9 0.3 collective-permute-done.16
  59.1 2.4 %collective-permute-done.17 = bf16[288,256]{1,0:T(8,128)(2,1)S(1)} collective-permute-done((bf16[288,256]{1,0:T(8,128)(2,1)S(1)}, bf16[288,256]{1,0:T(8,128)(2,1)S(1)}, u32[]{:S(2)}, u32[]{:S(2)}) %collective-permute-start.17) | collective-permute-done | bytes 147488 | tf_op jit(solution)/shard_map/ppermute | solution.py:315
  61.5 0.1 fusion
  61.6 2.0 %collective-permute-start.19 = (bf16[72,256]{1,0:T(8,128)(2,1)S(1)}, bf16[72,256]{1,0:T(8,128)(2,1)S(1)}, u32[]{:S(2)}, u32[]{:S(2)}) collective-permute-start(bf16[72,256]{1,0:T(8,128)(2,1)S(1)} %get-tuple-element.76), channel_id=1, source_target_pairs={{0,24},{2,26},{4,28},{6,30},{8,16},{10,18},{12,20},{14,22},{16,8},... | collective-permute-start | bytes 110600 | tf_op jit(solution)/shard_map/ppermute | solution.py:315
  63.7 0.0 collective-permute-start.20
  63.7 2.4 %collective-permute-start.21 = (bf16[72,256]{1,0:T(8,128)(2,1)S(1)}, bf16[72,256]{1,0:T(8,128)(2,1)S(1)}, u32[]{:S(2)}, u32[]{:S(2)}) collective-permute-start(bf16[72,256]{1,0:T(8,128)(2,1)S(1)} %get-tuple-element.78), channel_id=1, source_target_pairs={{0,8},{2,10},{4,12},{6,14},{8,0},{10,2},{12,4},{14,6},{16,24},{18,... | collective-permute-start | bytes 110600 | tf_op jit(solution)/shard_map/ppermute | solution.py:315
  66.1 3.3 %inputs_second.1 = (bf16[48,96,256]{2,1,0:T(8,128)(2,1)}, bf16[12,24,256]{2,1,0:T(8,128)(2,1)}) custom-call(bf16[50,96,768]{2,1,0:T(8,128)(2,1)S(1)} %get-tuple-element.59.three_four, bf16[14,32,768]{2,1,0:T(8,128)(2,1)S(1)} %get-tuple-element.72.three_six, bf16[2304,256]{1,0:T(8,128)(2,1)S(1)} %get-tuple-element.73.turned, ...), custom_call_target="tpu_custom_call" | custom-call | flops 2310222592 | bytes 2359296 | tf_op jit(solution)/shard_map/inputs_second/pallas_call | solution.py:570
  69.4 2.0 %collective-permute-start.22 = (bf16[72,256]{1,0:T(8,128)(2,1)S(1)}, bf16[72,256]{1,0:T(8,128)(2,1)S(1)}, u32[]{:S(2)}, u32[]{:S(2)}) collective-permute-start(bf16[72,256]{1,0:T(8,128)(2,1)S(1)} %fusion.5), channel_id=1, source_target_pairs={{0,24},{2,26},{4,28},{6,30},{8,16},{10,18},{12,20},{14,22},{16,8},... | collective-permute-start | bytes 110600 | tf_op jit(solution)/shard_map/ppermute | solution.py:315
  71.5 0.1 collective-permute-start.23
  71.6 2.3 %collective-permute-start.24 = (bf16[72,256]{1,0:T(8,128)(2,1)S(1)}, bf16[72,256]{1,0:T(8,128)(2,1)S(1)}, u32[]{:S(2)}, u32[]{:S(2)}) collective-permute-start(bf16[72,256]{1,0:T(8,128)(2,1)S(1)} %fusion.5), channel_id=1, source_target_pairs={{0,8},{2,10},{4,12},{6,14},{8,0},{10,2},{12,4},{14,6},{16,24},{18,... | collective-permute-start | bytes 110600 | tf_op jit(solution)/shard_map/ppermute | solution.py:315
  73.9 0.6 pad_maximum_fusion.1
  74.5 1.0 %collective-permute-done.22 = bf16[72,256]{1,0:T(8,128)(2,1)S(1)} collective-permute-done((bf16[72,256]{1,0:T(8,128)(2,1)S(1)}, bf16[72,256]{1,0:T(8,128)(2,1)S(1)}, u32[]{:S(2)}, u32[]{:S(2)}) %collective-permute-start.22) | collective-permute-done | bytes 36896 | tf_op jit(solution)/shard_map/ppermute | solution.py:315
  75.5 1.0 %collective-permute-done.23 = bf16[72,256]{1,0:T(8,128)(2,1)S(1)} collective-permute-done((bf16[72,256]{1,0:T(8,128)(2,1)S(1)}, bf16[72,256]{1,0:T(8,128)(2,1)S(1)}, u32[]{:S(2)}, u32[]{:S(2)}) %collective-permute-start.23) | collective-permute-done | bytes 36896 | tf_op jit(solution)/shard_map/ppermute | solution.py:315
  76.5 1.8 %collective-permute-start.25 = (bf16[288,256]{1,0:T(8,128)(2,1)S(1)}, bf16[288,256]{1,0:T(8,128)(2,1)S(1)}, u32[]{:S(2)}, u32[]{:S(2)}) collective-permute-start(bf16[288,256]{1,0:T(8,128)(2,1)S(1)} %bitcast.73), channel_id=1, source_target_pairs={{0,6},{2,4},{4,2},{6,0},{8,14},{10,12},{12,10},{14,8},{16,22},{18,... | collective-permute-start | bytes 442376 | tf_op jit(solution)/shard_map/ppermute | solution.py:315
  78.3 0.7 collective-permute-start.26
  79.0 1.1 %collective-permute-start.27 = (bf16[288,256]{1,0:T(8,128)(2,1)S(1)}, bf16[288,256]{1,0:T(8,128)(2,1)S(1)}, u32[]{:S(2)}, u32[]{:S(2)}) collective-permute-start(bf16[288,256]{1,0:T(8,128)(2,1)S(1)} %bitcast.75), channel_id=1, source_target_pairs={{0,2},{2,0},{4,6},{6,4},{8,10},{10,8},{12,14},{14,12},{16,18},{18,... | collective-permute-start | bytes 442376 | tf_op jit(solution)/shard_map/ppermute | solution.py:315
  80.1 0.1 broadcast_in_dim.14
  80.2 2.8 %collective-permute-done.25 = bf16[288,256]{1,0:T(8,128)(2,1)S(1)} collective-permute-done((bf16[288,256]{1,0:T(8,128)(2,1)S(1)}, bf16[288,256]{1,0:T(8,128)(2,1)S(1)}, u32[]{:S(2)}, u32[]{:S(2)}) %collective-permute-start.25) | collective-permute-done | bytes 147488 | tf_op jit(solution)/shard_map/ppermute | solution.py:315
  83.0 1.4 %collective-permute-done.26 = bf16[288,256]{1,0:T(8,128)(2,1)S(1)} collective-permute-done((bf16[288,256]{1,0:T(8,128)(2,1)S(1)}, bf16[288,256]{1,0:T(8,128)(2,1)S(1)}, u32[]{:S(2)}, u32[]{:S(2)}) %collective-permute-start.26) | collective-permute-done | bytes 147488 | tf_op jit(solution)/shard_map/ppermute | solution.py:315
  84.5 0.0 copy-start.7
  84.5 1.0 %copy-done.7 = f32[4,288,256]{2,1,0:T(8,128)} copy-done((f32[4,288,256]{2,1,0:T(8,128)}, f32[4,288,256]{2,1,0:T(8,128)S(1)}, u32[]{:S(2)}) %copy-start.7) | copy-done | bytes 1179672
  (33 shorter events, 0.3 us)
Async XLA Ops:
  0.6 3.6 %copy-start.1 = (bf16[1,48,96,256]{3,2,1,0:T(8,128)(2,1)S(1)}, bf16[1,48,96,256]{3,2,1,0:T(8,128)(2,1)}, u32[]{:S(2)}) copy-start(bf16[1,48,96,256]{3,2,1,0:T(8,128)(2,1)} %param.7) | copy-start | bytes 7077892
  0.7 3.6 %copy-start.3 = (bf16[1,12,24,256]{3,2,1,0:T(8,128)(2,1)S(1)}, bf16[1,12,24,256]{3,2,1,0:T(8,128)(2,1)}, u32[]{:S(2)}) copy-start(bf16[1,12,24,256]{3,2,1,0:T(8,128)(2,1)} %param.8) | copy-start | bytes 442372
  0.7 3.6 %copy-start.6 = (bf16[9,256,256]{2,1,0:T(8,128)(2,1)S(1)}, bf16[9,256,256]{2,1,0:T(8,128)(2,1)}, u32[]{:S(2)}) copy-start(bf16[9,256,256]{2,1,0:T(8,128)(2,1)} %w_ref.3) | copy-start | bytes 3538948
  2.4 23.8 %copy-start.2 = (bf16[1,12,24,256]{3,2,1,0:T(8,128)(2,1)S(1)}, bf16[1,12,24,256]{3,2,1,0:T(8,128)(2,1)}, u32[]{:S(2)}) copy-start(bf16[1,12,24,256]{3,2,1,0:T(8,128)(2,1)} %param.13) | copy-start | bytes 442372
  2.4 23.8 %copy-start.4 = (f32[2,256]{1,0:T(2,128)S(1)}, f32[2,256]{1,0:T(2,128)}, u32[]{:S(2)}) copy-start(f32[2,256]{1,0:T(2,128)} %gain_ref.3) | copy-start | bytes 6148
  2.4 23.8 %copy-start.5 = (f32[2,256]{1,0:T(2,128)S(1)}, f32[2,256]{1,0:T(2,128)}, u32[]{:S(2)}) copy-start(f32[2,256]{1,0:T(2,128)} %shift_ref.3) | copy-start | bytes 6148
  2.5 1.8 %collective-permute-start = (bf16[384,256]{1,0:T(8,128)(2,1)}, bf16[384,256]{1,0:T(8,128)(2,1)S(1)}, u32[]{:S(2)}, u32[]{:S(2)}) collective-permute-start(bf16[384,256]{1,0:T(8,128)(2,1)} %edges.1), channel_id=1, source_target_pairs={{0,1},{1,0},{2,3},{3,2},{4,5},{5,4},{6,7},{7,6},{8,9},{9,8},{10,11... | collective-permute-start | bytes 589832 | tf_op jit(solution)/shard_map/ppermute | solution.py:315
  4.3 22.0 %copy-start = (bf16[1,48,96,256]{3,2,1,0:T(8,128)(2,1)S(1)}, bf16[1,48,96,256]{3,2,1,0:T(8,128)(2,1)}, u32[]{:S(2)}) copy-start(bf16[1,48,96,256]{3,2,1,0:T(8,128)(2,1)} %param.12) | copy-start | bytes 7077892
  10.7 1.3 %collective-permute-start.1 = (f32[4,256]{1,0:T(4,128)S(1)}, f32[4,256]{1,0:T(4,128)S(1)}, u32[]{:S(2)}, u32[]{:S(2)}) collective-permute-start(f32[4,256]{1,0:T(4,128)S(1)} %get-tuple-element.49), channel_id=1, source_target_pairs={{0,1},{1,0},{2,3},{3,2},{4,5},{5,4},{6,7},{7,6},{8,9},{9,8},{10,11... | collective-permute-start | bytes 12296 | tf_op jit(solution)/shard_map/ppermute | solution.py:315
  12.0 4.1 %collective-permute-start.3 = (f32[4,256]{1,0:T(4,128)S(1)}, f32[4,256]{1,0:T(4,128)S(1)}, u32[]{:S(2)}, u32[]{:S(2)}) collective-permute-start(f32[4,256]{1,0:T(4,128)S(1)} %add.78), channel_id=1, source_target_pairs={{0,5},{1,4},{2,7},{3,6},{4,1},{5,0},{6,3},{7,2},{8,13},{9,12},{10,... | collective-permute-start | bytes 12296 | tf_op jit(solution)/shard_map/ppermute | solution.py:385
  14.6 3.9 %collective-permute-start.4 = (f32[4,256]{1,0:T(4,128)S(1)}, f32[4,256]{1,0:T(4,128)S(1)}, u32[]{:S(2)}, u32[]{:S(2)}) collective-permute-start(f32[4,256]{1,0:T(4,128)S(1)} %add.78), channel_id=1, source_target_pairs={{0,7},{1,6},{2,5},{3,4},{4,3},{5,2},{6,1},{7,0},{8,15},{9,14},{10,... | collective-permute-start | bytes 12296 | tf_op jit(solution)/shard_map/ppermute | solution.py:385
  16.0 3.0 %collective-permute-start.2 = (f32[4,256]{1,0:T(4,128)S(1)}, f32[4,256]{1,0:T(4,128)S(1)}, u32[]{:S(2)}, u32[]{:S(2)}) collective-permute-start(f32[4,256]{1,0:T(4,128)S(1)} %add.78), channel_id=1, source_target_pairs={{0,3},{1,2},{2,1},{3,0},{4,7},{5,6},{6,5},{7,4},{8,11},{9,10},{10,... | collective-permute-start | bytes 12296 | tf_op jit(solution)/shard_map/ppermute | solution.py:385
  19.0 3.9 %collective-permute-start.6 = (f32[4,256]{1,0:T(4,128)S(1)}, f32[4,256]{1,0:T(4,128)S(1)}, u32[]{:S(2)}, u32[]{:S(2)}) collective-permute-start(f32[4,256]{1,0:T(4,128)S(1)} %add_add_fusion.3), channel_id=1, source_target_pairs={{0,17},{1,16},{2,19},{3,18},{4,21},{5,20},{6,23},{7,22},{8,25},{9,... | collective-permute-start | bytes 12296 | tf_op jit(solution)/shard_map/ppermute | solution.py:385
  21.4 4.8 %collective-permute-start.7 = (f32[4,256]{1,0:T(4,128)S(1)}, f32[4,256]{1,0:T(4,128)S(1)}, u32[]{:S(2)}, u32[]{:S(2)}) collective-permute-start(f32[4,256]{1,0:T(4,128)S(1)} %add_add_fusion.3), channel_id=1, source_target_pairs={{0,25},{1,24},{2,27},{3,26},{4,29},{5,28},{6,31},{7,30},{8,17},{9,... | collective-permute-start | bytes 12296 | tf_op jit(solution)/shard_map/ppermute | solution.py:385
  22.7 3.5 %collective-permute-start.5 = (f32[4,256]{1,0:T(4,128)S(1)}, f32[4,256]{1,0:T(4,128)S(1)}, u32[]{:S(2)}, u32[]{:S(2)}) collective-permute-start(f32[4,256]{1,0:T(4,128)S(1)} %add_add_fusion.3), channel_id=1, source_target_pairs={{0,9},{1,8},{2,11},{3,10},{4,13},{5,12},{6,15},{7,14},{8,1},{9,0},... | collective-permute-start | bytes 12296 | tf_op jit(solution)/shard_map/ppermute | solution.py:385
  29.2 1.2 %collective-permute-start.8 = (f32[4,256]{1,0:T(4,128)S(1)}, f32[4,256]{1,0:T(4,128)S(1)}, u32[]{:S(2)}, u32[]{:S(2)}) collective-permute-start(f32[4,256]{1,0:T(4,128)S(1)} %get-tuple-element.52), channel_id=1, source_target_pairs={{0,1},{1,0},{2,3},{3,2},{4,5},{5,4},{6,7},{7,6},{8,9},{9,8},{10,11... | collective-permute-start | bytes 12296 | tf_op jit(solution)/shard_map/ppermute | solution.py:315
  30.4 3.2 %collective-permute-start.10 = (f32[4,256]{1,0:T(4,128)S(1)}, f32[4,256]{1,0:T(4,128)S(1)}, u32[]{:S(2)}, u32[]{:S(2)}) collective-permute-start(f32[4,256]{1,0:T(4,128)S(1)} %add.85), channel_id=1, source_target_pairs={{0,5},{1,4},{2,7},{3,6},{4,1},{5,0},{6,3},{7,2},{8,13},{9,12},{10,... | collective-permute-start | bytes 12296 | tf_op jit(solution)/shard_map/ppermute | solution.py:385
  31.9 3.9 %collective-permute-start.11 = (f32[4,256]{1,0:T(4,128)S(1)}, f32[4,256]{1,0:T(4,128)S(1)}, u32[]{:S(2)}, u32[]{:S(2)}) collective-permute-start(f32[4,256]{1,0:T(4,128)S(1)} %add.85), channel_id=1, source_target_pairs={{0,7},{1,6},{2,5},{3,4},{4,3},{5,2},{6,1},{7,0},{8,15},{9,14},{10,... | collective-permute-start | bytes 12296 | tf_op jit(solution)/shard_map/ppermute | solution.py:385
  32.9 3.0 %collective-permute-start.9 = (f32[4,256]{1,0:T(4,128)S(1)}, f32[4,256]{1,0:T(4,128)S(1)}, u32[]{:S(2)}, u32[]{:S(2)}) collective-permute-start(f32[4,256]{1,0:T(4,128)S(1)} %add.85), channel_id=1, source_target_pairs={{0,3},{1,2},{2,1},{3,0},{4,7},{5,6},{6,5},{7,4},{8,11},{9,10},{10,... | collective-permute-start | bytes 12296 | tf_op jit(solution)/shard_map/ppermute | solution.py:385
  35.9 3.9 %collective-permute-start.13 = (f32[4,256]{1,0:T(4,128)S(1)}, f32[4,256]{1,0:T(4,128)S(1)}, u32[]{:S(2)}, u32[]{:S(2)}) collective-permute-start(f32[4,256]{1,0:T(4,128)S(1)} %add_add_fusion.1), channel_id=1, source_target_pairs={{0,17},{1,16},{2,19},{3,18},{4,21},{5,20},{6,23},{7,22},{8,25},{9,... | collective-permute-start | bytes 12296 | tf_op jit(solution)/shard_map/ppermute | solution.py:385
  36.9 4.8 %collective-permute-start.14 = (f32[4,256]{1,0:T(4,128)S(1)}, f32[4,256]{1,0:T(4,128)S(1)}, u32[]{:S(2)}, u32[]{:S(2)}) collective-permute-start(f32[4,256]{1,0:T(4,128)S(1)} %add_add_fusion.1), channel_id=1, source_target_pairs={{0,25},{1,24},{2,27},{3,26},{4,29},{5,28},{6,31},{7,30},{8,17},{9,... | collective-permute-start | bytes 12296 | tf_op jit(solution)/shard_map/ppermute | solution.py:385
  37.8 3.9 %collective-permute-start.12 = (f32[4,256]{1,0:T(4,128)S(1)}, f32[4,256]{1,0:T(4,128)S(1)}, u32[]{:S(2)}, u32[]{:S(2)}) collective-permute-start(f32[4,256]{1,0:T(4,128)S(1)} %add_add_fusion.1), channel_id=1, source_target_pairs={{0,9},{1,8},{2,11},{3,10},{4,13},{5,12},{6,15},{7,14},{8,1},{9,0},... | collective-permute-start | bytes 12296 | tf_op jit(solution)/shard_map/ppermute | solution.py:385
  49.2 2.1 %collective-permute-start.15 = (bf16[9,128,256]{2,1,0:T(8,128)(2,1)S(1)}, bf16[9,128,256]{2,1,0:T(8,128)(2,1)S(1)}, u32[]{:S(2)}, u32[]{:S(2)}) collective-permute-start(bf16[9,128,256]{2,1,0:T(8,128)(2,1)S(1)} %bitcast.67), channel_id=1, source_target_pairs={{0,1},{1,0},{2,3},{3,2},{4,5},{5,4},{6,7},{7,6},{8,9},{9,8},{10,11... | collective-permute-start | bytes 1769480 | tf_op jit(solution)/shard_map/ppermute | solution.py:315
  51.4 7.7 %collective-permute-start.16 = (bf16[288,256]{1,0:T(8,128)(2,1)S(1)}, bf16[288,256]{1,0:T(8,128)(2,1)S(1)}, u32[]{:S(2)}, u32[]{:S(2)}) collective-permute-start(bf16[288,256]{1,0:T(8,128)(2,1)S(1)} %get-tuple-element.61), channel_id=1, source_target_pairs={{0,6},{2,4},{4,2},{6,0},{8,14},{10,12},{12,10},{14,8},{16,22},{18,... | collective-permute-start | bytes 442376 | tf_op jit(solution)/shard_map/ppermute | solution.py:315
  53.2 8.3 %collective-permute-start.17 = (bf16[288,256]{1,0:T(8,128)(2,1)S(1)}, bf16[288,256]{1,0:T(8,128)(2,1)S(1)}, u32[]{:S(2)}, u32[]{:S(2)}) collective-permute-start(bf16[288,256]{1,0:T(8,128)(2,1)S(1)} %get-tuple-element.62), channel_id=1, source_target_pairs={{0,4},{2,6},{4,0},{6,2},{8,12},{10,14},{12,8},{14,10},{16,20},{18,... | collective-permute-start | bytes 442376 | tf_op jit(solution)/shard_map/ppermute | solution.py:315
  53.7 7.8 %collective-permute-start.18 = (bf16[288,256]{1,0:T(8,128)(2,1)S(1)}, bf16[288,256]{1,0:T(8,128)(2,1)S(1)}, u32[]{:S(2)}, u32[]{:S(2)}) collective-permute-start(bf16[288,256]{1,0:T(8,128)(2,1)S(1)} %get-tuple-element.63), channel_id=1, source_target_pairs={{0,2},{2,0},{4,6},{6,4},{8,10},{10,8},{12,14},{14,12},{16,18},{18,... | collective-permute-start | bytes 442376 | tf_op jit(solution)/shard_map/ppermute | solution.py:315
  61.6 7.7 %collective-permute-start.19 = (bf16[72,256]{1,0:T(8,128)(2,1)S(1)}, bf16[72,256]{1,0:T(8,128)(2,1)S(1)}, u32[]{:S(2)}, u32[]{:S(2)}) collective-permute-start(bf16[72,256]{1,0:T(8,128)(2,1)S(1)} %get-tuple-element.76), channel_id=1, source_target_pairs={{0,24},{2,26},{4,28},{6,30},{8,16},{10,18},{12,20},{14,22},{16,8},... | collective-permute-start | bytes 110600 | tf_op jit(solution)/shard_map/ppermute | solution.py:315
  63.7 5.7 %collective-permute-start.20 = (bf16[72,256]{1,0:T(8,128)(2,1)S(1)}, bf16[72,256]{1,0:T(8,128)(2,1)S(1)}, u32[]{:S(2)}, u32[]{:S(2)}) collective-permute-start(bf16[72,256]{1,0:T(8,128)(2,1)S(1)} %get-tuple-element.77), channel_id=1, source_target_pairs={{0,16},{2,18},{4,20},{6,22},{8,24},{10,26},{12,28},{14,30},{16,0},... | collective-permute-start | bytes 110600 | tf_op jit(solution)/shard_map/ppermute | solution.py:315
  63.7 5.7 %collective-permute-start.21 = (bf16[72,256]{1,0:T(8,128)(2,1)S(1)}, bf16[72,256]{1,0:T(8,128)(2,1)S(1)}, u32[]{:S(2)}, u32[]{:S(2)}) collective-permute-start(bf16[72,256]{1,0:T(8,128)(2,1)S(1)} %get-tuple-element.78), channel_id=1, source_target_pairs={{0,8},{2,10},{4,12},{6,14},{8,0},{10,2},{12,4},{14,6},{16,24},{18,... | collective-permute-start | bytes 110600 | tf_op jit(solution)/shard_map/ppermute | solution.py:315
  69.4 6.0 %collective-permute-start.22 = (bf16[72,256]{1,0:T(8,128)(2,1)S(1)}, bf16[72,256]{1,0:T(8,128)(2,1)S(1)}, u32[]{:S(2)}, u32[]{:S(2)}) collective-permute-start(bf16[72,256]{1,0:T(8,128)(2,1)S(1)} %fusion.5), channel_id=1, source_target_pairs={{0,24},{2,26},{4,28},{6,30},{8,16},{10,18},{12,20},{14,22},{16,8},... | collective-permute-start | bytes 110600 | tf_op jit(solution)/shard_map/ppermute | solution.py:315
  71.5 5.0 %collective-permute-start.23 = (bf16[72,256]{1,0:T(8,128)(2,1)S(1)}, bf16[72,256]{1,0:T(8,128)(2,1)S(1)}, u32[]{:S(2)}, u32[]{:S(2)}) collective-permute-start(bf16[72,256]{1,0:T(8,128)(2,1)S(1)} %fusion.5), channel_id=1, source_target_pairs={{0,16},{2,18},{4,20},{6,22},{8,24},{10,26},{12,28},{14,30},{16,0},... | collective-permute-start | bytes 110600 | tf_op jit(solution)/shard_map/ppermute | solution.py:315
  71.6 4.9 %collective-permute-start.24 = (bf16[72,256]{1,0:T(8,128)(2,1)S(1)}, bf16[72,256]{1,0:T(8,128)(2,1)S(1)}, u32[]{:S(2)}, u32[]{:S(2)}) collective-permute-start(bf16[72,256]{1,0:T(8,128)(2,1)S(1)} %fusion.5), channel_id=1, source_target_pairs={{0,8},{2,10},{4,12},{6,14},{8,0},{10,2},{12,4},{14,6},{16,24},{18,... | collective-permute-start | bytes 110600 | tf_op jit(solution)/shard_map/ppermute | solution.py:315
  76.5 6.4 %collective-permute-start.25 = (bf16[288,256]{1,0:T(8,128)(2,1)S(1)}, bf16[288,256]{1,0:T(8,128)(2,1)S(1)}, u32[]{:S(2)}, u32[]{:S(2)}) collective-permute-start(bf16[288,256]{1,0:T(8,128)(2,1)S(1)} %bitcast.73), channel_id=1, source_target_pairs={{0,6},{2,4},{4,2},{6,0},{8,14},{10,12},{12,10},{14,8},{16,22},{18,... | collective-permute-start | bytes 442376 | tf_op jit(solution)/shard_map/ppermute | solution.py:315
  78.3 6.1 %collective-permute-start.26 = (bf16[288,256]{1,0:T(8,128)(2,1)S(1)}, bf16[288,256]{1,0:T(8,128)(2,1)S(1)}, u32[]{:S(2)}, u32[]{:S(2)}) collective-permute-start(bf16[288,256]{1,0:T(8,128)(2,1)S(1)} %bitcast.74), channel_id=1, source_target_pairs={{0,4},{2,6},{4,0},{6,2},{8,12},{10,14},{12,8},{14,10},{16,20},{18,... | collective-permute-start | bytes 442376 | tf_op jit(solution)/shard_map/ppermute | solution.py:315
  79.0 5.5 %collective-permute-start.27 = (bf16[288,256]{1,0:T(8,128)(2,1)S(1)}, bf16[288,256]{1,0:T(8,128)(2,1)S(1)}, u32[]{:S(2)}, u32[]{:S(2)}) collective-permute-start(bf16[288,256]{1,0:T(8,128)(2,1)S(1)} %bitcast.75), channel_id=1, source_target_pairs={{0,2},{2,0},{4,6},{6,4},{8,10},{10,8},{12,14},{14,12},{16,18},{18,... | collective-permute-start | bytes 442376 | tf_op jit(solution)/shard_map/ppermute | solution.py:315
  84.5 1.0 %copy-start.7 = (f32[4,288,256]{2,1,0:T(8,128)}, f32[4,288,256]{2,1,0:T(8,128)S(1)}, u32[]{:S(2)}) copy-start(f32[4,288,256]{2,1,0:T(8,128)S(1)} %convert_dynamic-update-slice_fusion) | copy-start | bytes 3538948
